TPU v7x, 32 devices: a whole 2x2x4 slice. The times are simulated.
32 devices in a mesh: island: 2 (over y), fsdp: 16 (over z, x, core).
Axes of the slice: x: 2, y: 2, z: 4, core: 2. Of those that a mesh axis runs over, the one named last changes fastest.
Arguments:
- momentum: float32 [2, 32768, 128], P('island', 'fsdp'), may hold values from -6 to 6
- gradient: bfloat16 [2, 32768, 128], P('island', 'fsdp'), may hold values from -6 to 6
- params: float32 [32768, 128], P('fsdp'), may hold values from -6 to 6
- indices: int32 [2, 32768, 32], P('island', 'fsdp'), may hold values from 0 to 127, all different within a row
Outputs:
- new_momentum: float32 [2, 32768, 128], P('island', 'fsdp')
- new_params: bfloat16 [32768, 128], P('fsdp')
Inputs may be any that keep to these rules, and one draw needn't show every extreme that they name: `indices`: the 32 numbers of one island and block are distinct.
All inputs are finite; a program needn't handle non-finite values.
Results may differ from a plain program's by a relative error of at most 0.001.
Values may be sent and summed in bfloat16 or wider, within the bound.
No kernel may reach another device: no remote copies, remote signals or barrier semaphores. Data moves between devices by JAX's collectives and lax.ppermute only.
A program may use at most 64 MiB of HBM per device.

v0:
```python
import math

import jax
import jax.numpy as jnp
from jax import lax
from jax.sharding import PartitionSpec as P


def dct_table(length):
    freq = jnp.arange(length, dtype=jnp.float32)[:, None]
    place = jnp.arange(length, dtype=jnp.float32)[None, :]
    scale = jnp.where(freq == 0, jnp.sqrt(1.0 / length), jnp.sqrt(2.0 / length))
    return scale * jnp.cos(jnp.pi * (place + 0.5) * freq / length)


def keep_mask(numbers, length):
    counter = jnp.arange(length, dtype=jnp.int32)
    hits = jnp.any(numbers[:, :, None] == counter, axis=1)
    return hits.astype(jnp.float32)


def one_hot_table(numbers, length):
    counter = jnp.arange(length, dtype=jnp.int32)
    return (numbers[:, :, None] == counter).astype(jnp.float32)


def row_blocks(count):
    return math.gcd(count, 256)


def select_values(coef, numbers):
    count, length = coef.shape
    keep = numbers.shape[1]
    rows = row_blocks(count)
    coef_blocks = coef.reshape(count // rows, rows, length)
    number_blocks = numbers.reshape(count // rows, rows, keep)

    def pick(pair):
        onehot = one_hot_table(pair[1], length)
        return jnp.einsum("ct,ckt->ck", pair[0], onehot, precision=lax.Precision.HIGHEST)

    return lax.map(pick, (coef_blocks, number_blocks)).reshape(count, keep)


def spread_total(all_values, all_numbers, length):
    islands, count, keep = all_values.shape
    rows = row_blocks(count)
    value_blocks = all_values.reshape(islands, count // rows, rows, keep).transpose(1, 0, 2, 3)
    number_blocks = all_numbers.reshape(islands, count // rows, rows, keep).transpose(1, 0, 2, 3)

    def place(pair):
        dense = jnp.zeros((rows, length), jnp.float32)
        for other in range(islands):
            onehot = one_hot_table(pair[1][other], length)
            dense = dense + jnp.einsum(
                "ck,ckt->ct", pair[0][other], onehot, precision=lax.Precision.HIGHEST
            )
        return dense

    return lax.map(place, (value_blocks, number_blocks)).reshape(count, length)


def local(momentum, gradient, params, indices):
    length = momentum.shape[2]
    table = dct_table(length)
    mom = 0.999 * momentum[0] + gradient[0].astype(jnp.float32)
    coef = jnp.dot(
        mom, table.T, precision=lax.Precision.HIGHEST, preferred_element_type=jnp.float32
    )
    kept = coef * keep_mask(indices[0], length)
    new_momentum = mom - jnp.dot(
        kept, table, precision=lax.Precision.HIGHEST, preferred_element_type=jnp.float32
    )
    islands = lax.axis_size("island")
    values = select_values(coef, indices[0])
    all_values, all_indices = (
        lax.all_gather(values[None], "island", axis=0, tiled=True),
        lax.all_gather(indices, "island", axis=0, tiled=True),
    )
    total = spread_total(all_values, all_indices, length)
    update = jnp.dot(
        total / islands, table, precision=lax.Precision.HIGHEST, preferred_element_type=jnp.float32
    )
    fresh = (params - update).astype(jnp.bfloat16)
    return (new_momentum[None], fresh)


def solution(mesh):
    in_specs = (
        P("island", "fsdp", None),
        P("island", "fsdp", None),
        P("fsdp", None),
        P("island", "fsdp", None),
    )
    out_specs = (P("island", "fsdp", None), P("fsdp", None))
    return jax.shard_map(local, mesh=mesh, in_specs=in_specs, out_specs=out_specs, check_vma=False)
```

profile of v0, /device:TPU:0, one launch (start us, length us, event | category | flops | bytes accessed | tf_op | source)
XLA Modules:
  0.0 130.6 jit_solution(11759483536014679392)
XLA Ops:
  0.7 2.6 %fusion.9 = f32[2048,128]{1,0:T(8,128)S(1)} fusion(bf16[1,2048,128]{2,1,0:T(8,128)(2,1)} %param.9, f32[1,2048,128]{2,1,0:T(8,128)} %param.8, f32[128]{0:T(128)S(1)} %get-tuple-element.81, f32[128]{0:T(128)S(1)} %get-tuple-element.80), kind=kOutput, calls=%fused_computation.23 | convolution fusion | flops 403488768 | bytes 2622464 | tf_op jit(solution)/shard_map/dot_general | solution.py:67
  3.3 0.3 copy.19
  3.7 32.9 %while.20 = (s32[]{:T(128)}, f32[8,256,32]{2,1,0:T(8,128)S(1)}, f32[8,256,128]{2,1,0:T(8,128)S(1)}, s32[8,256,32]{2,1,0:T(8,128)S(1)}, s32[]{:T(128)}) while((s32[]{:T(128)}, f32[8,256,32]{2,1,0:T(8,128)S(1)}, f32[8,256,128]{2,1,0:T(8,128)S(1)}, s32[8,256,32]{2,1,0:T(8,128)S(1)}, s32[]{:T(128)}) %tuple.52), condition=%wide.region_2.3_spmd, body=%wide.region_1.2_spmd.sunk | while | flops 13631490 | bytes 786505 | solution.py:42
  3.7 4.0 %fusion.39 = f32[256,1,32]{2,1,0:T(1,128)S(1)} fusion(f32[256,128,1]{1,2,0:T(1,128)S(1)} %bitcast.96, s32[256,32]{1,0:T(8,128)S(1)} %dynamic-slice_bitcast_fusion.2), kind=kOutput, calls=%fused_computation.1.clone.1 | convolution fusion | flops 13631488 | bytes 196608 | tf_op jit(solution)/shard_map/while/body/eval_jaxpr/ct,ckt->ck/dot_general | solution.py:40
  7.8 4.0 %fusion.39 = f32[256,1,32]{2,1,0:T(1,128)S(1)} fusion(f32[256,128,1]{1,2,0:T(1,128)S(1)} %bitcast.96, s32[256,32]{1,0:T(8,128)S(1)} %dynamic-slice_bitcast_fusion.2), kind=kOutput, calls=%fused_computation.1.clone.1 | convolution fusion | flops 13631488 | bytes 196608 | tf_op jit(solution)/shard_map/while/body/eval_jaxpr/ct,ckt->ck/dot_general | solution.py:40
  11.9 4.0 %fusion.39 = f32[256,1,32]{2,1,0:T(1,128)S(1)} fusion(f32[256,128,1]{1,2,0:T(1,128)S(1)} %bitcast.96, s32[256,32]{1,0:T(8,128)S(1)} %dynamic-slice_bitcast_fusion.2), kind=kOutput, calls=%fused_computation.1.clone.1 | convolution fusion | flops 13631488 | bytes 196608 | tf_op jit(solution)/shard_map/while/body/eval_jaxpr/ct,ckt->ck/dot_general | solution.py:40
  16.0 4.0 %fusion.39 = f32[256,1,32]{2,1,0:T(1,128)S(1)} fusion(f32[256,128,1]{1,2,0:T(1,128)S(1)} %bitcast.96, s32[256,32]{1,0:T(8,128)S(1)} %dynamic-slice_bitcast_fusion.2), kind=kOutput, calls=%fused_computation.1.clone.1 | convolution fusion | flops 13631488 | bytes 196608 | tf_op jit(solution)/shard_map/while/body/eval_jaxpr/ct,ckt->ck/dot_general | solution.py:40
  20.1 4.0 %fusion.39 = f32[256,1,32]{2,1,0:T(1,128)S(1)} fusion(f32[256,128,1]{1,2,0:T(1,128)S(1)} %bitcast.96, s32[256,32]{1,0:T(8,128)S(1)} %dynamic-slice_bitcast_fusion.2), kind=kOutput, calls=%fused_computation.1.clone.1 | convolution fusion | flops 13631488 | bytes 196608 | tf_op jit(solution)/shard_map/while/body/eval_jaxpr/ct,ckt->ck/dot_general | solution.py:40
  24.3 4.0 %fusion.39 = f32[256,1,32]{2,1,0:T(1,128)S(1)} fusion(f32[256,128,1]{1,2,0:T(1,128)S(1)} %bitcast.96, s32[256,32]{1,0:T(8,128)S(1)} %dynamic-slice_bitcast_fusion.2), kind=kOutput, calls=%fused_computation.1.clone.1 | convolution fusion | flops 13631488 | bytes 196608 | tf_op jit(solution)/shard_map/while/body/eval_jaxpr/ct,ckt->ck/dot_general | solution.py:40
  28.4 4.0 %fusion.39 = f32[256,1,32]{2,1,0:T(1,128)S(1)} fusion(f32[256,128,1]{1,2,0:T(1,128)S(1)} %bitcast.96, s32[256,32]{1,0:T(8,128)S(1)} %dynamic-slice_bitcast_fusion.2), kind=kOutput, calls=%fused_computation.1.clone.1 | convolution fusion | flops 13631488 | bytes 196608 | tf_op jit(solution)/shard_map/while/body/eval_jaxpr/ct,ckt->ck/dot_general | solution.py:40
  32.5 4.0 %fusion.39 = f32[256,1,32]{2,1,0:T(1,128)S(1)} fusion(f32[256,128,1]{1,2,0:T(1,128)S(1)} %bitcast.96, s32[256,32]{1,0:T(8,128)S(1)} %dynamic-slice_bitcast_fusion.2), kind=kOutput, calls=%fused_computation.1.clone.1 | convolution fusion | flops 13631488 | bytes 196608 | tf_op jit(solution)/shard_map/while/body/eval_jaxpr/ct,ckt->ck/dot_general | solution.py:40
  36.5 0.3 copy.29
  36.8 9.9 %all_gather.6 = f32[2,2048,32]{1,2,0:T(8,128)S(1)} all-gather(f32[1,2048,32]{1,2,0:T(8,128)S(1)} %copy.29), channel_id=1, replica_groups=mesh['island'=2,'fsdp'=16] {'island'}, dimensions={0}, use_global_device_ids=true | all-gather | bytes 786432 | tf_op jit(solution)/shard_map/all_gather | solution.py:77
  46.8 0.2 copy.36
  46.9 8.2 %all_gather.7 = s32[2,2048,32]{1,2,0:T(8,128)S(1)} all-gather(s32[1,2048,32]{1,2,0:T(8,128)S(1)} %copy-done.1), channel_id=1, replica_groups=mesh['island'=2,'fsdp'=16] {'island'}, dimensions={0}, use_global_device_ids=true | all-gather | bytes 786432 | tf_op jit(solution)/shard_map/all_gather | solution.py:78
  55.1 0.2 copy.37
  55.3 56.8 %while.21 = (s32[]{:T(128)}, f32[8,256,128]{2,1,0:T(8,128)}, f32[8,2,256,32]{2,0,3,1:T(8,128)S(1)}, s32[8,2,256,32]{2,0,3,1:T(8,128)S(1)}, s32[]{:T(128)}, /*index=5*/s32[]{:T(128)}, s32[]{}) while((s32[]{:T(128)}, f32[8,256,128]{2,1,0:T(8,128)}, f32[8,2,256,32]{2,0,3,1:T(8,128)S(1)}, s32[8,2,256,32]{2,0,3,1:T(8,128)S(1)}, s32[]{:T(128)}, ...), condition=%wide.region_4.5_spmd, body=%wide.region_3.4_spmd.sunk | while | flops 27295748 | bytes 1311337 | solution.py:60
  55.3 0.1 copy.42
  55.5 0.1 copy.43
  55.6 2.9 %fusion.42 = f32[256,1,128]{2,1,0:T(1,128)S(1)} fusion(f32[256,32,1]{1,2,0:T(1,128)S(1)} %bitcast.89, s32[256,32]{1,0:T(8,128)S(1)} %bitcast.91), kind=kOutput, calls=%fused_computation.8.clone.1 | convolution fusion | flops 13631488 | bytes 196608 | tf_op jit(solution)/shard_map/while/body/eval_jaxpr/ck,ckt->ct/dot_general | solution.py:55
  58.5 0.1 copy.44
  58.8 2.9 %fusion.43 = f32[256,1,128]{2,1,0:T(1,128)S(1)} fusion(f32[256,32,1]{1,2,0:T(1,128)S(1)} %bitcast.90, s32[256,32]{1,0:T(8,128)S(1)} %bitcast.92), kind=kOutput, calls=%fused_computation.9.clone.1 | convolution fusion | flops 13631488 | bytes 196608 | tf_op jit(solution)/shard_map/while/body/eval_jaxpr/ck,ckt->ct/dot_general | solution.py:55
  61.7 0.7 bitcast_dynamic-update-slice_fusion.5
  62.4 0.1 copy.42
  62.6 0.1 copy.43
  62.7 2.9 %fusion.42 = f32[256,1,128]{2,1,0:T(1,128)S(1)} fusion(f32[256,32,1]{1,2,0:T(1,128)S(1)} %bitcast.89, s32[256,32]{1,0:T(8,128)S(1)} %bitcast.91), kind=kOutput, calls=%fused_computation.8.clone.1 | convolution fusion | flops 13631488 | bytes 196608 | tf_op jit(solution)/shard_map/while/body/eval_jaxpr/ck,ckt->ct/dot_general | solution.py:55
  65.6 0.1 copy.44
  65.9 2.9 %fusion.43 = f32[256,1,128]{2,1,0:T(1,128)S(1)} fusion(f32[256,32,1]{1,2,0:T(1,128)S(1)} %bitcast.90, s32[256,32]{1,0:T(8,128)S(1)} %bitcast.92), kind=kOutput, calls=%fused_computation.9.clone.1 | convolution fusion | flops 13631488 | bytes 196608 | tf_op jit(solution)/shard_map/while/body/eval_jaxpr/ck,ckt->ct/dot_general | solution.py:55
  68.8 0.7 bitcast_dynamic-update-slice_fusion.5
  69.5 0.1 copy.42
  69.7 0.1 copy.43
  69.8 2.9 %fusion.42 = f32[256,1,128]{2,1,0:T(1,128)S(1)} fusion(f32[256,32,1]{1,2,0:T(1,128)S(1)} %bitcast.89, s32[256,32]{1,0:T(8,128)S(1)} %bitcast.91), kind=kOutput, calls=%fused_computation.8.clone.1 | convolution fusion | flops 13631488 | bytes 196608 | tf_op jit(solution)/shard_map/while/body/eval_jaxpr/ck,ckt->ct/dot_general | solution.py:55
  72.7 0.1 copy.44
  73.0 2.9 %fusion.43 = f32[256,1,128]{2,1,0:T(1,128)S(1)} fusion(f32[256,32,1]{1,2,0:T(1,128)S(1)} %bitcast.90, s32[256,32]{1,0:T(8,128)S(1)} %bitcast.92), kind=kOutput, calls=%fused_computation.9.clone.1 | convolution fusion | flops 13631488 | bytes 196608 | tf_op jit(solution)/shard_map/while/body/eval_jaxpr/ck,ckt->ct/dot_general | solution.py:55
  75.9 0.7 bitcast_dynamic-update-slice_fusion.5
  76.6 0.1 copy.42
  76.8 0.1 copy.43
  76.9 2.9 %fusion.42 = f32[256,1,128]{2,1,0:T(1,128)S(1)} fusion(f32[256,32,1]{1,2,0:T(1,128)S(1)} %bitcast.89, s32[256,32]{1,0:T(8,128)S(1)} %bitcast.91), kind=kOutput, calls=%fused_computation.8.clone.1 | convolution fusion | flops 13631488 | bytes 196608 | tf_op jit(solution)/shard_map/while/body/eval_jaxpr/ck,ckt->ct/dot_general | solution.py:55
  79.8 0.1 copy.44
  80.1 2.9 %fusion.43 = f32[256,1,128]{2,1,0:T(1,128)S(1)} fusion(f32[256,32,1]{1,2,0:T(1,128)S(1)} %bitcast.90, s32[256,32]{1,0:T(8,128)S(1)} %bitcast.92), kind=kOutput, calls=%fused_computation.9.clone.1 | convolution fusion | flops 13631488 | bytes 196608 | tf_op jit(solution)/shard_map/while/body/eval_jaxpr/ck,ckt->ct/dot_general | solution.py:55
  83.0 0.7 bitcast_dynamic-update-slice_fusion.5
  83.7 0.1 copy.42
  83.9 0.1 copy.43
  84.0 2.9 %fusion.42 = f32[256,1,128]{2,1,0:T(1,128)S(1)} fusion(f32[256,32,1]{1,2,0:T(1,128)S(1)} %bitcast.89, s32[256,32]{1,0:T(8,128)S(1)} %bitcast.91), kind=kOutput, calls=%fused_computation.8.clone.1 | convolution fusion | flops 13631488 | bytes 196608 | tf_op jit(solution)/shard_map/while/body/eval_jaxpr/ck,ckt->ct/dot_general | solution.py:55
  86.9 0.1 copy.44
  87.2 2.9 %fusion.43 = f32[256,1,128]{2,1,0:T(1,128)S(1)} fusion(f32[256,32,1]{1,2,0:T(1,128)S(1)} %bitcast.90, s32[256,32]{1,0:T(8,128)S(1)} %bitcast.92), kind=kOutput, calls=%fused_computation.9.clone.1 | convolution fusion | flops 13631488 | bytes 196608 | tf_op jit(solution)/shard_map/while/body/eval_jaxpr/ck,ckt->ct/dot_general | solution.py:55
  90.1 0.7 bitcast_dynamic-update-slice_fusion.5
  91.1 2.9 %fusion.42 = f32[256,1,128]{2,1,0:T(1,128)S(1)} fusion(f32[256,32,1]{1,2,0:T(1,128)S(1)} %bitcast.89, s32[256,32]{1,0:T(8,128)S(1)} %bitcast.91), kind=kOutput, calls=%fused_computation.8.clone.1 | convolution fusion | flops 13631488 | bytes 196608 | tf_op jit(solution)/shard_map/while/body/eval_jaxpr/ck,ckt->ct/dot_general | solution.py:55
  94.2 2.9 %fusion.43 = f32[256,1,128]{2,1,0:T(1,128)S(1)} fusion(f32[256,32,1]{1,2,0:T(1,128)S(1)} %bitcast.90, s32[256,32]{1,0:T(8,128)S(1)} %bitcast.92), kind=kOutput, calls=%fused_computation.9.clone.1 | convolution fusion | flops 13631488 | bytes 196608 | tf_op jit(solution)/shard_map/while/body/eval_jaxpr/ck,ckt->ct/dot_general | solution.py:55
  97.2 0.7 bitcast_dynamic-update-slice_fusion.5
  98.2 2.9 %fusion.42 = f32[256,1,128]{2,1,0:T(1,128)S(1)} fusion(f32[256,32,1]{1,2,0:T(1,128)S(1)} %bitcast.89, s32[256,32]{1,0:T(8,128)S(1)} %bitcast.91), kind=kOutput, calls=%fused_computation.8.clone.1 | convolution fusion | flops 13631488 | bytes 196608 | tf_op jit(solution)/shard_map/while/body/eval_jaxpr/ck,ckt->ct/dot_general | solution.py:55
  101.1 0.1 copy.44
  101.3 2.9 %fusion.43 = f32[256,1,128]{2,1,0:T(1,128)S(1)} fusion(f32[256,32,1]{1,2,0:T(1,128)S(1)} %bitcast.90, s32[256,32]{1,0:T(8,128)S(1)} %bitcast.92), kind=kOutput, calls=%fused_computation.9.clone.1 | convolution fusion | flops 13631488 | bytes 196608 | tf_op jit(solution)/shard_map/while/body/eval_jaxpr/ck,ckt->ct/dot_general | solution.py:55
  104.3 0.7 bitcast_dynamic-update-slice_fusion.5
  105.3 2.9 %fusion.42 = f32[256,1,128]{2,1,0:T(1,128)S(1)} fusion(f32[256,32,1]{1,2,0:T(1,128)S(1)} %bitcast.89, s32[256,32]{1,0:T(8,128)S(1)} %bitcast.91), kind=kOutput, calls=%fused_computation.8.clone.1 | convolution fusion | flops 13631488 | bytes 196608 | tf_op jit(solution)/shard_map/while/body/eval_jaxpr/ck,ckt->ct/dot_general | solution.py:55
  108.2 0.1 copy.44
  108.4 2.9 %fusion.43 = f32[256,1,128]{2,1,0:T(1,128)S(1)} fusion(f32[256,32,1]{1,2,0:T(1,128)S(1)} %bitcast.90, s32[256,32]{1,0:T(8,128)S(1)} %bitcast.92), kind=kOutput, calls=%fused_computation.9.clone.1 | convolution fusion | flops 13631488 | bytes 196608 | tf_op jit(solution)/shard_map/while/body/eval_jaxpr/ck,ckt->ct/dot_general | solution.py:55
  111.4 0.7 bitcast_dynamic-update-slice_fusion.5
  112.1 1.4 %broadcast_multiply_fusion = f32[8,256,128]{2,1,0:T(8,128)S(1)} fusion(f32[8,256,128]{2,1,0:T(8,128)} %get-tuple-element.47), kind=kLoop, calls=%fused_computation.27 | loop fusion | flops 262144 | bytes 2097152 | tf_op jit(solution)/shard_map/div | solution.py:82
  113.5 0.1 copy-done.3
  113.6 2.0 %fusion.8 = bf16[2048,128]{1,0:T(8,128)(2,1)} fusion(f32[2048,128]{1,0:T(8,128)S(1)} %copy-done.3, f32[2048,128]{1,0:T(8,128)S(1)} %bitcast.88, f32[128]{0:T(128)S(1)} %get-tuple-element.81, f32[128]{0:T(128)S(1)} %get-tuple-element.80), kind=kOutput, calls=%fused_computation.22 | convolution fusion | flops 403226624 | bytes 2622464 | tf_op jit(solution)/shard_map/dot_general | solution.py:81
  115.6 0.3 copy.18
  116.0 12.4 %fusion.6 = pred[2048,128]{1,0:T(8,128)(4,1)S(1)} fusion(s32[2048,32]{1,0:T(8,128)S(1)} %copy.18), kind=kLoop, calls=%fused_computation.18 | loop fusion | flops 16515072 | bytes 524288 | tf_op jit(solution)/shard_map/reduce_or | solution.py:18
  128.4 2.2 %fusion.7 = f32[1,2048,128]{2,1,0:T(8,128)} fusion(pred[2048,128]{1,0:T(8,128)(4,1)S(1)} %fusion.6, f32[2048,128]{1,0:T(8,128)S(1)} %bitcast.87, bf16[1,2048,128]{2,1,0:T(8,128)(2,1)S(1)} %copy-done.2, f32[1,2048,128]{2,1,0:T(8,128)S(1)} %copy-done, f32[128]{0:T(128)S(1)} %get-tuple-element.81, f32[128]{0:T(128)S(1)} %get-tuple-element.80), kind=kOutput, calls=%fused_computation.21 | convolution fusion | flops 404013056 | bytes 3933184 | tf_op jit(solution)/shard_map/dot_general | solution.py:71
  (65 shorter events, 2.8 us)
Async XLA Ops:
  0.6 2.7 %copy-start.1 = (s32[1,2048,32]{1,2,0:T(8,128)S(1)}, s32[1,2048,32]{1,2,0:T(8,128)}, u32[]{:S(2)}) copy-start(s32[1,2048,32]{1,2,0:T(8,128)} %param.11) | copy-start | bytes 786436
  112.1 1.5 %copy-start.3 = (f32[2048,128]{1,0:T(8,128)S(1)}, f32[2048,128]{1,0:T(8,128)}, u32[]{:S(2)}) copy-start(f32[2048,128]{1,0:T(8,128)} %param.10) | copy-start | bytes 3145732
  115.6 12.7 %copy-start = (f32[1,2048,128]{2,1,0:T(8,128)S(1)}, f32[1,2048,128]{2,1,0:T(8,128)}, u32[]{:S(2)}) copy-start(f32[1,2048,128]{2,1,0:T(8,128)} %param.8) | copy-start | bytes 3145732
  116.0 12.4 %copy-start.2 = (bf16[1,2048,128]{2,1,0:T(8,128)(2,1)S(1)}, bf16[1,2048,128]{2,1,0:T(8,128)(2,1)}, u32[]{:S(2)}) copy-start(bf16[1,2048,128]{2,1,0:T(8,128)(2,1)} %param.9) | copy-start | bytes 1572868
where the time goes:
time: 131 us
  matrix products  86 us (66%)
  other arithmetic  19.2 us (15%)
  blocking collectives  18.1 us (14%)
  local copies, waits for them, and re-layouts  5.95 us (5%)
    dot_general x16, matrix products, place(): jnp.einsum('ck,ckt->ct', pair[0][other], onehot, precision=lax.Precision....  47 us
    dot_general x8, matrix products, pick(): jnp.einsum('ct,ckt->ck', pair[0], onehot, precision=lax.Precision.HIGHEST)  32.1 us
    reduce_or x1, other arithmetic, keep_mask(): hits = jnp.any(numbers[:, :, None] == counter, axis=1)  12.4 us
    all_gather x1, blocking collectives, local(): lax.all_gather(values[None], 'island', axis=0, tiled=True)  9.93 us
    all_gather x1, blocking collectives, local(): lax.all_gather(indices, 'island', axis=0, tiled=True)  8.17 us
    dynamic_update_slice x8, other arithmetic, spread_total(): return lax.map(place, (value_blocks, number_blocks)).reshape(count, length)  5.41 us
    while x32, local copies, waits for them, and re-layouts  3.31 us
    dot_general x1, matrix products, local(): jnp.dot(mom, table.T, precision=lax.Precision.HIGHEST, preferred_element_...  2.64 us

commit v1 on v0

v1 whole, which is shorter than its diff:
```python
import functools

import jax
import jax.numpy as jnp
import numpy as np
from jax import lax
from jax.experimental import pallas as pl
from jax.experimental.pallas import tpu as pltpu
from jax.sharding import PartitionSpec as P

STEPS = 32000.0
GROUPS = 4
TINY = 1e-30


def dct_weights(length):
    freq = np.arange(length, dtype=np.float64)[:, None]
    place = np.arange(length, dtype=np.float64)[None, :]
    scale = np.where(freq == 0, np.sqrt(1.0 / length), np.sqrt(2.0 / length))
    table = scale * np.cos(np.pi * (place + 0.5) * freq / length)

    def pair(a):
        hi = a.astype(jnp.bfloat16)
        lo = (a - hi.astype(np.float64)).astype(jnp.bfloat16)
        return np.block([[hi, lo], [hi, np.zeros_like(hi)]]).astype(jnp.bfloat16)

    return pair(table.T), pair(table)


def transform(x, weights):
    hi = x.astype(jnp.bfloat16)
    lo = (x - hi.astype(jnp.float32)).astype(jnp.bfloat16)
    both = jnp.dot(
        jnp.concatenate([hi, lo], axis=1), weights, preferred_element_type=jnp.float32
    )
    length = x.shape[1]
    return both[:, :length] + both[:, length:]


def lanes_of(x, index):
    return jnp.take_along_axis(x, index, axis=1, mode="promise_in_bounds")


def stack_groups(numbers, length):
    return jnp.concatenate(
        [numbers[:, g * length : (g + 1) * length] for g in range(GROUPS)], axis=0
    )


def encode_kernel(w_ref, idx_ref, m_ref, g_ref, msg_ref, scale_ref):
    step = pl.program_id(0)
    length = m_ref.shape[1]
    keep = idx_ref.shape[0]
    mom = 0.999 * m_ref[...] + g_ref[...].astype(jnp.float32)
    coef = transform(mom, w_ref[...])
    picks = stack_groups(idx_ref[...], length).T
    group = lax.broadcasted_iota(jnp.int32, (length, length), 1) // keep
    values = lanes_of(coef[:length], picks)
    for g in range(1, GROUPS):
        values = jnp.where(group == g, lanes_of(coef[g * length : (g + 1) * length], picks), values)
    turned = values.T
    coded = []
    for g in range(GROUPS):
        part = turned[g * keep : (g + 1) * keep]
        top = jnp.max(jnp.abs(part), axis=0, keepdims=True)
        power = jnp.ceil(jnp.log2(jnp.maximum(top, TINY)))
        scale_ref[pl.ds(step * GROUPS + g, 1), :] = power
        coded.append(jnp.round(part * (STEPS * jnp.exp2(-power))))
    rows = pl.ds(pl.multiple_of(step * length, length), length)
    msg_ref[rows, :] = jnp.concatenate(coded, axis=0).astype(jnp.int32).astype(jnp.int16)

    @pl.when(step == pl.num_programs(0) - 1)
    def _():
        tail = scale_ref.shape[0]
        msg_ref[pl.ds(msg_ref.shape[0] - tail, tail), :] = (
            scale_ref[...].astype(jnp.int32).astype(jnp.int16)
        )


def positions(numbers, length):
    keep, blocks = numbers.shape
    out = []
    for b in range(blocks // length):
        part = numbers[:, b * length : (b + 1) * length]
        place = lax.broadcasted_iota(jnp.int32, (length, length), 0)
        found = jnp.full((length, length), -1, jnp.int32)
        for k in range(keep):
            found = jnp.where(part[k : k + 1] == place, (b % GROUPS) * keep + k, found)
        out.append(found.T)
    return jnp.concatenate(out, axis=0)


def decode(coded, powers, keep):
    values = coded.astype(jnp.int32).astype(jnp.float32)
    unit = jnp.exp2(powers) * (1.0 / STEPS)
    parts = [values[g * keep : (g + 1) * keep] * unit[g : g + 1] for g in range(GROUPS)]
    return jnp.concatenate(parts, axis=0).T


def spread(values, lanes):
    length = values.shape[0]
    out = []
    for g in range(GROUPS):
        at = lanes[g * length : (g + 1) * length]
        out.append(jnp.where(at >= 0, lanes_of(values, at & (length - 1)), 0.0))
    return jnp.concatenate(out, axis=0)


def message_part(msg_ref, step, length, keep):
    rows = pl.ds(pl.multiple_of(step * length, length), length)
    tail = scale_rows(msg_ref.shape[0] * length // keep, length)
    base = msg_ref.shape[0] - tail
    powers = msg_ref[pl.ds(base, tail), :].astype(jnp.int32).astype(jnp.float32)
    mine = []
    row = lax.broadcasted_iota(jnp.int32, powers.shape, 0)
    for g in range(GROUPS):
        mine.append(
            jnp.sum(jnp.where(row == step * GROUPS + g, powers, 0.0), axis=0, keepdims=True)
        )
    return msg_ref[rows, :], jnp.concatenate(mine, axis=0)


def own_kernel(w_ref, idx_ref, msg_ref, m_ref, g_ref, new_ref, back_ref):
    step = pl.program_id(0)
    length = m_ref.shape[1]
    keep = idx_ref.shape[0]
    coded, powers = message_part(msg_ref, step, length, keep)
    kept = spread(decode(coded, powers, keep), positions(idx_ref[...], length))
    back = transform(kept, w_ref[...])
    back_ref[...] = back
    new_ref[...] = 0.999 * m_ref[...] + g_ref[...].astype(jnp.float32) - back


def positions_kernel(idx_ref, lanes_ref):
    length = lanes_ref.shape[1]
    lanes_ref[...] = positions(idx_ref[...].astype(jnp.int32), length)


def finish_kernel(islands, me_ref, w_ref, back_ref, p_ref, *refs):
    out_ref = refs[-1]
    msgs, lanes = refs[: islands - 1], refs[islands - 1 : 2 * islands - 2]
    step = pl.program_id(0)
    length = p_ref.shape[1]
    keep = length // GROUPS
    terms = [back_ref[...]]
    for msg_ref, lanes_ref in zip(msgs, lanes):
        coded, powers = message_part(msg_ref, step, length, keep)
        kept = spread(decode(coded, powers, keep), lanes_ref[...])
        terms.append(transform(kept, w_ref[...]))
    if islands == 2:
        total = terms[0] + terms[1]
    else:
        total = None
        for island in range(islands):
            term = terms[0]
            for away in range(1, islands):
                origin = lax.rem(me_ref[0] + islands - away, islands)
                term = jnp.where(origin == island, terms[away], term)
            total = term if total is None else total + term
    out_ref[...] = (p_ref[...] - total * (1.0 / islands)).astype(out_ref.dtype)


def scale_rows(blocks, length):
    return -(-(blocks // length) // 16) * 16


def local(momentum, gradient, params, indices):
    islands = lax.axis_size("island")
    _, count, length = momentum.shape
    keep = indices.shape[2]
    chunk = GROUPS * length
    grid = (count // chunk,)
    forward, inverse = (jnp.asarray(w) for w in dct_weights(length))
    numbers = indices[0].T
    short = numbers.astype(jnp.int16)
    rings = [
        [(i, (i + away) % islands) for i in range(islands)] for away in range(1, islands)
    ]
    other_numbers = [lax.ppermute(short, "island", ring) for ring in rings]

    tail = scale_rows(count, length)
    msg_rows = count * keep // length + tail
    weights_spec = pl.BlockSpec((2 * length, 2 * length), lambda i: (0, 0))
    numbers_spec = pl.BlockSpec((keep, chunk), lambda i: (0, i))
    rows_spec = pl.BlockSpec((chunk, length), lambda i: (i, 0))
    msg_spec = pl.BlockSpec((msg_rows, length), lambda i: (0, 0))
    wide = jax.ShapeDtypeStruct((count, length), jnp.float32)

    msg = pl.pallas_call(
        encode_kernel,
        grid=grid,
        in_specs=[weights_spec, numbers_spec, rows_spec, rows_spec],
        out_specs=msg_spec,
        out_shape=jax.ShapeDtypeStruct((msg_rows, length), jnp.int16),
        scratch_shapes=[pltpu.VMEM((tail, length), jnp.float32)],
        name="encode",
    )(forward, numbers, momentum[0], gradient[0])
    other_msgs = [lax.ppermute(msg, "island", ring) for ring in rings]

    new_momentum, back = pl.pallas_call(
        own_kernel,
        grid=grid,
        in_specs=[weights_spec, numbers_spec, msg_spec, rows_spec, rows_spec],
        out_specs=(rows_spec, rows_spec),
        out_shape=(wide, wide),
        cost_estimate=pl.CostEstimate(flops=10**9, bytes_accessed=6 * 2**20, transcendentals=0),
        name="own",
    )(inverse, numbers, msg, momentum[0], gradient[0])

    lanes = [
        pl.pallas_call(
            positions_kernel,
            grid=grid,
            in_specs=[numbers_spec],
            out_specs=rows_spec,
            out_shape=jax.ShapeDtypeStruct((count, length), jnp.int32),
            cost_estimate=pl.CostEstimate(flops=10**9, bytes_accessed=2 * 2**20, transcendentals=0),
            name="positions",
        )(other)
        for other in other_numbers
    ]

    me = lax.axis_index("island").astype(jnp.int32)[None]
    new_params = pl.pallas_call(
        functools.partial(finish_kernel, islands),
        grid=grid,
        in_specs=[pl.BlockSpec(memory_space=pltpu.SMEM), weights_spec, rows_spec, rows_spec]
        + [msg_spec] * (islands - 1)
        + [rows_spec] * (islands - 1),
        out_specs=rows_spec,
        out_shape=jax.ShapeDtypeStruct((count, length), jnp.bfloat16),
        name="finish",
    )(me, inverse, back, params, *other_msgs, *lanes)
    return new_momentum[None], new_params


def solution(mesh):
    in_specs = (
        P("island", "fsdp", None),
        P("island", "fsdp", None),
        P("fsdp", None),
        P("island", "fsdp", None),
    )
    out_specs = (P("island", "fsdp", None), P("fsdp", None))
    return jax.shard_map(local, mesh=mesh, in_specs=in_specs, out_specs=out_specs, check_vma=False)
```

time: 131 us -> 27.2 us (0.21)
  matrix products: 86 us -> 0 us
  Pallas kernels: 0 us -> 20.8 us
  other arithmetic: 19.2 us -> 0.97 us
  blocking collectives: 18.1 us -> 0 us
  local copies, waits for them, and re-layouts: 5.95 us -> 1.3 us
  starting transfers between devices: 0 us -> 3.07 us
    dot_general x27 -> x0, matrix products: 86 us -> none  [the longest x16 47 us: place(): jnp.einsum('ck,ckt->ct', pair[0][other], onehot, precision=lax.Precision....]
    pallas_call x0 -> x4, Pallas kernels: none -> 20.8 us  [the longest x1 6.79 us: local(): pl.pallas_call(own_kernel, grid=grid, in_specs=[weights_spec, numbers_spe...]
    all_gather x2 -> x0, blocking collectives: 18.1 us -> none  [the longest x1 9.93 us: local(): lax.all_gather(values[None], 'island', axis=0, tiled=True)]
    reduce_or x1 -> x0, other arithmetic: 12.4 us -> none  [keep_mask(): hits = jnp.any(numbers[:, :, None] == counter, axis=1)]
    dynamic_update_slice x8 -> x0, other arithmetic: 5.41 us -> none  [spread_total(): return lax.map(place, (value_blocks, number_blocks)).reshape(count, length)]
    while x32 -> x0, local copies, waits for them, and re-layouts: 3.31 us -> none
    ppermute x0 -> x2, starting transfers between devices: none -> 3.07 us  [the longest x1 3.03 us: local(): other_numbers = [lax.ppermute(short, 'island', ring) for ring in rings]]
    div x1 -> x0, other arithmetic: 1.39 us -> none  [local(): total / islands]
  transfers between devices with their start and end apart: 0 -> 2, of which waited for: 0 -> 0; matrix products, arithmetic and copies ran while one was open for 0% -> 0% of each run, Pallas kernels for 0% -> 60%
where the time goes in v1:
time: 27.2 us; the launch traced here: 26.8 us
  Pallas kernels  20.8 us (76%)
  starting transfers between devices  3.07 us (11%)
  local copies, waits for them, and re-layouts  1.3 us (5%)
  other arithmetic  0.97 us (4%)
  between operations  0.65 us (2%)
    pallas_call x1, Pallas kernels, local(): pl.pallas_call(own_kernel, grid=grid, in_specs=[weights_spec, numbers_spe...  6.79 us
    pallas_call x1, Pallas kernels, local(): pl.pallas_call(positions_kernel, grid=grid, in_specs=[numbers_spec], out_...  4.91 us
    pallas_call x1, Pallas kernels, local(): pl.pallas_call(functools.partial(finish_kernel, islands), grid=grid, in_s...  4.74 us
    pallas_call x1, Pallas kernels, local(): pl.pallas_call(encode_kernel, grid=grid, in_specs=[weights_spec, numbers_...  4.4 us
    ppermute x1, starting transfers between devices, local(): other_numbers = [lax.ppermute(short, 'island', ring) for ring in rings]  3.03 us
    unnamed x4, local copies, waits for them, and re-layouts  1.3 us
    convert_element_type x1, other arithmetic, local(): short = numbers.astype(jnp.int16)  0.97 us
  transfers between devices with their start and end apart: 2, of which 0 were waited for; matrix products, arithmetic and copies ran while one was open for 0% of the time, Pallas kernels for 60%

profile of v1, /device:TPU:0, one launch (start us, length us, event | category | flops | bytes accessed | tf_op | source)
XLA Modules:
  0.0 26.8 jit_solution(10624024133893189172)
XLA Ops:
  0.6 1.0 %bitcast_convert_fusion = s16[32,2048]{1,0:T(8,128)(2,1)S(1)} fusion(s32[1,2048,32]{1,2,0:T(8,128)} %param.9), kind=kLoop, calls=%fused_computation | loop fusion | flops 65536 | bytes 393216 | tf_op jit(solution)/shard_map/convert_element_type | solution.py:175
  1.6 3.0 %collective-permute-start.1 = (s16[32,2048]{1,0:T(8,128)(2,1)S(1)}, s16[32,2048]{1,0:T(8,128)(2,1)S(1)}, u32[]{:S(2)}, u32[]{:S(2)}) collective-permute-start(s16[32,2048]{1,0:T(8,128)(2,1)S(1)} %bitcast_convert_fusion), channel_id=1, source_target_pairs={{0,16},{16,0},{1,17},{17,1},{2,18},{18,2},{3,19},{19,3},{4,20},{20... | collective-permute-start | bytes 393224 | tf_op jit(solution)/shard_map/ppermute | solution.py:179
  4.6 4.4 %encode.1.msg_ref = s16[528,128]{1,0:T(8,128)(2,1)} custom-call(bf16[256,256]{1,0:T(8,128)(2,1)} %constant.10.clone.w_ref, s32[32,2048]{1,0:T(8,128)} %bitcast.10, f32[2048,128]{1,0:T(8,128)} %bitcast.8, bf16[2048,128]{1,0:T(8,128)(2,1)} %bitcast.12), custom_call_target="tpu_custom_call" | custom-call | tf_op jit(solution)/shard_map/encode/pallas_call | solution.py:189
  9.0 0.0 collective-permute-start
  9.1 6.8 %own.1 = (f32[2048,128]{1,0:T(8,128)}, f32[2048,128]{1,0:T(8,128)}) custom-call(bf16[256,256]{1,0:T(8,128)(2,1)} %constant.11.clone.w_ref, s32[32,2048]{1,0:T(8,128)} %bitcast.11, s16[528,128]{1,0:T(8,128)(2,1)} %encode.1.msg_ref, f32[2048,128]{1,0:T(8,128)} %bitcast.9, bf16[2048,128]{1,0:T(8,128)(2,1)} %bitcast.13), custom_call_target="tpu_custom_call" | custom-call | flops 1000000000 | bytes 6291456 | tf_op jit(solution)/shard_map/own/pallas_call | solution.py:200
  15.9 0.0 collective-permute-done.1.idx_ref
  15.9 0.0 copy-start.1
  15.9 0.6 %copy-done.1 = s16[32,2048]{1,0:T(8,128)(2,1)} copy-done((s16[32,2048]{1,0:T(8,128)(2,1)}, s16[32,2048]{1,0:T(8,128)(2,1)S(1)}, u32[]{:S(2)}) %copy-start.1) | copy-done | bytes 131096
  16.5 4.9 %positions.1.refs_1_ = s32[2048,128]{1,0:T(8,128)} custom-call(s16[32,2048]{1,0:T(8,128)(2,1)} %copy-done.1), custom_call_target="tpu_custom_call" | custom-call | flops 1000000000 | bytes 2097152 | tf_op jit(solution)/shard_map/positions/pallas_call | solution.py:211
  21.4 0.0 collective-permute-done.refs_0_
  21.4 0.0 copy-start
  21.4 0.7 %copy-done = s16[528,128]{1,0:T(8,128)(2,1)} copy-done((s16[528,128]{1,0:T(8,128)(2,1)}, s16[528,128]{1,0:T(8,128)(2,1)S(1)}, u32[]{:S(2)}) %copy-start) | copy-done | bytes 135192
  22.1 4.7 %finish.1 = bf16[2048,128]{1,0:T(8,128)(2,1)} custom-call(s32[1]{0:T(128)} %bitcast.6.me_ref, bf16[256,256]{1,0:T(8,128)(2,1)} %constant.11.clone.w_ref, f32[2048,128]{1,0:T(8,128)} %get-tuple-element.5.back_ref, f32[2048,128]{1,0:T(8,128)} %p_ref.1, s16[528,128]{1,0:T(8,128)(2,1)} %copy-done, s32[2048,128]{1,0:T(8,128)} %positions.1.refs_1_), custom_call_target="tpu_custom_call" | custom-call | tf_op jit(solution)/shard_map/finish/pallas_call | solution.py:224
Async XLA Ops:
  1.6 14.3 %collective-permute-start.1 = (s16[32,2048]{1,0:T(8,128)(2,1)S(1)}, s16[32,2048]{1,0:T(8,128)(2,1)S(1)}, u32[]{:S(2)}, u32[]{:S(2)}) collective-permute-start(s16[32,2048]{1,0:T(8,128)(2,1)S(1)} %bitcast_convert_fusion), channel_id=1, source_target_pairs={{0,16},{16,0},{1,17},{17,1},{2,18},{18,2},{3,19},{19,3},{4,20},{20... | collective-permute-start | bytes 393224 | tf_op jit(solution)/shard_map/ppermute | solution.py:179
  9.0 12.4 %collective-permute-start = (s16[528,128]{1,0:T(8,128)(2,1)}, s16[528,128]{1,0:T(8,128)(2,1)S(1)}, u32[]{:S(2)}, u32[]{:S(2)}) collective-permute-start(s16[528,128]{1,0:T(8,128)(2,1)} %encode.1.msg_ref), channel_id=1, source_target_pairs={{0,16},{16,0},{1,17},{17,1},{2,18},{18,2},{3,19},{19,3},{4,20},{20... | collective-permute-start | bytes 405512 | tf_op jit(solution)/shard_map/ppermute | solution.py:198
  15.9 0.7 %copy-start.1 = (s16[32,2048]{1,0:T(8,128)(2,1)}, s16[32,2048]{1,0:T(8,128)(2,1)S(1)}, u32[]{:S(2)}) copy-start(s16[32,2048]{1,0:T(8,128)(2,1)S(1)} %collective-permute-done.1.idx_ref) | copy-start | bytes 393220
  21.4 0.7 %copy-start = (s16[528,128]{1,0:T(8,128)(2,1)}, s16[528,128]{1,0:T(8,128)(2,1)S(1)}, u32[]{:S(2)}) copy-start(s16[528,128]{1,0:T(8,128)(2,1)S(1)} %collective-permute-done.refs_0_) | copy-start | bytes 405508

commit v2 on v0

v2 whole, which is shorter than its diff:
```python
import functools

import jax
import jax.numpy as jnp
import numpy as np
from jax import lax
from jax.experimental import pallas as pl
from jax.experimental.pallas import tpu as pltpu
from jax.sharding import PartitionSpec as P

STEPS = 32000.0
GROUPS = 4
TINY = 1e-30
WORD = 32
SUB = 8
VMEM_LIMIT = 16 * 2**20


def dct_table(length):
    freq = np.arange(length, dtype=np.float64)[:, None]
    place = np.arange(length, dtype=np.float64)[None, :]
    scale = np.where(freq == 0, np.sqrt(1.0 / length), np.sqrt(2.0 / length))
    return (scale * np.cos(np.pi * (place + 0.5) * freq / length)).astype(np.float32)


def two_parts(x):
    hi = x.astype(jnp.bfloat16)
    return hi, (x - hi.astype(jnp.float32)).astype(jnp.bfloat16)


def weights_of(table):
    hi, lo = two_parts(table)
    return jnp.concatenate(
        [jnp.concatenate([hi, lo], axis=1), jnp.concatenate([hi, jnp.zeros_like(hi)], axis=1)],
        axis=0,
    )


def transform(x, weights):
    both = jnp.dot(
        jnp.concatenate(two_parts(x), axis=1), weights, preferred_element_type=jnp.float32
    )
    length = x.shape[1]
    return both[:, :length] + both[:, length:]


def lanes_of(x, index):
    return jnp.take_along_axis(x, index, axis=1, mode="promise_in_bounds")


def row_iota():
    return lax.broadcasted_iota(jnp.int32, (SUB, 128), 0)


def mask_words(part, length):
    rows = [part[v : v + SUB] for v in range(0, part.shape[0], SUB)]
    bits = [lax.shift_left(jnp.ones_like(r), r & (WORD - 1)) for r in rows]
    words = []
    for w in range(length // WORD):
        total = None
        for r, bit in zip(rows, bits):
            term = jnp.where(lax.shift_right_logical(r, 5) == w, bit, 0)
            total = term if total is None else total + term
        for shift in (4, 2, 1):
            total = total + pltpu.roll(total, shift, 0)
        words.append(total)
    return words


def bases_of(words):
    bases = [jnp.zeros_like(words[0])]
    for word in words[:-1]:
        bases.append(bases[-1] + lax.population_count(word))
    return bases


def sorted_numbers(part, length):
    words = mask_words(part, length)
    bases = bases_of(words)
    out = []
    for v in range(0, part.shape[0], SUB):
        rank = row_iota() + v
        word, base, place = words[0], bases[0], jnp.zeros_like(rank)
        for w in range(1, len(words)):
            up = rank >= bases[w]
            word = jnp.where(up, words[w], word)
            base = jnp.where(up, bases[w], base)
            place = jnp.where(up, w * WORD, place)
        rank = rank - base
        half = WORD // 2
        while half:
            below = lax.population_count(word & ((1 << half) - 1))
            up = rank >= below
            rank = jnp.where(up, rank - below, rank)
            word = jnp.where(up, lax.shift_right_logical(word, half), word)
            place = jnp.where(up, place + half, place)
            half //= 2
        out.append(place)
    return jnp.concatenate(out, axis=0)


def positions(part, group, length):
    keep = part.shape[0]
    words = mask_words(part, length)
    bases = bases_of(words)
    out = []
    for t in range(0, length, SUB):
        place = row_iota() + t % WORD
        word = words[t // WORD]
        low = lax.shift_left(jnp.ones_like(place), place) - 1
        rank = lax.population_count(word & low) + (bases[t // WORD] + group * keep)
        held = lax.shift_right_logical(word, place) & 1
        out.append(jnp.where(held == 1, rank, -1))
    return jnp.concatenate(out, axis=0).T


def all_positions(numbers, length):
    return [
        positions(numbers[:, b * length : (b + 1) * length], b % GROUPS, length)
        for b in range(numbers.shape[1] // length)
    ]


def encode_kernel(table_ref, idx_ref, m_ref, g_ref, msg_ref):
    count, length = m_ref.shape
    keep = idx_ref.shape[0]
    weights = weights_of(table_ref[...].T)
    group = lax.broadcasted_iota(jnp.int32, (length, length), 1) // keep
    scales = []
    for c in range(count // (GROUPS * length)):
        picks = jnp.concatenate(
            [
                sorted_numbers(idx_ref[:, b * length : (b + 1) * length], length)
                for b in range(c * GROUPS, (c + 1) * GROUPS)
            ],
            axis=0,
        ).T
        rows = slice(c * GROUPS * length, (c + 1) * GROUPS * length)
        mom = 0.999 * m_ref[rows] + g_ref[rows].astype(jnp.float32)
        coef = transform(mom, weights)
        values = lanes_of(coef[:length], picks)
        for g in range(1, GROUPS):
            other = lanes_of(coef[g * length : (g + 1) * length], picks)
            values = jnp.where(group == g, other, values)
        turned = values.T
        coded = []
        for g in range(GROUPS):
            part = turned[g * keep : (g + 1) * keep]
            top = jnp.max(jnp.abs(part), axis=0, keepdims=True)
            power = jnp.ceil(jnp.log2(jnp.maximum(top, TINY)))
            scales.append(power)
            coded.append(jnp.round(part * (STEPS * jnp.exp2(-power))))
        msg_ref[c * length : (c + 1) * length] = (
            jnp.concatenate(coded, axis=0).astype(jnp.int32).astype(jnp.int16)
        )
    rows = msg_ref.shape[0] - count * keep // length
    if rows > len(scales):
        scales.append(jnp.zeros((rows - len(scales), length), jnp.float32))
    msg_ref[msg_ref.shape[0] - rows :] = (
        jnp.concatenate(scales, axis=0).astype(jnp.int32).astype(jnp.int16)
    )


def spread(msg_ref, lanes, c, keep):
    length = msg_ref.shape[1]
    rows = msg_ref[c * length : (c + 1) * length].astype(jnp.int32).astype(jnp.float32)
    chunks = msg_ref.shape[0] // length
    tail = msg_ref[chunks * length :].astype(jnp.int32).astype(jnp.float32)
    unit = jnp.exp2(tail[c * GROUPS : (c + 1) * GROUPS]) * (1.0 / STEPS)
    values = jnp.concatenate(
        [rows[g * keep : (g + 1) * keep] * unit[g : g + 1] for g in range(GROUPS)], axis=0
    ).T
    return jnp.concatenate(
        [jnp.where(at >= 0, lanes_of(values, at & (length - 1)), 0.0) for at in lanes], axis=0
    )


def own_kernel(table_ref, idx_ref, msg_ref, m_ref, g_ref, new_ref, back_ref):
    count, length = m_ref.shape
    keep = idx_ref.shape[0]
    weights = weights_of(table_ref[...])
    for c in range(count // (GROUPS * length)):
        rows = slice(c * GROUPS * length, (c + 1) * GROUPS * length)
        lanes = all_positions(idx_ref[:, rows], length)
        back = transform(spread(msg_ref, lanes, c, keep), weights)
        back_ref[rows] = back
        new_ref[rows] = 0.999 * m_ref[rows] + g_ref[rows].astype(jnp.float32) - back


def positions_kernel(idx_ref, lanes_ref):
    length = lanes_ref.shape[1]
    numbers = idx_ref[...].astype(jnp.int32)
    for b, lanes in enumerate(all_positions(numbers, length)):
        lanes_ref[b * length : (b + 1) * length] = lanes


def finish_kernel(islands, me_ref, table_ref, back_ref, p_ref, *refs):
    out_ref = refs[-1]
    msgs, places = refs[: islands - 1], refs[islands - 1 : 2 * islands - 2]
    count, length = p_ref.shape
    keep = length // GROUPS
    weights = weights_of(table_ref[...])
    for c in range(count // (GROUPS * length)):
        rows = slice(c * GROUPS * length, (c + 1) * GROUPS * length)
        terms = [back_ref[rows]]
        for msg_ref, lanes_ref in zip(msgs, places):
            lanes = [
                lanes_ref[b * length : (b + 1) * length]
                for b in range(c * GROUPS, (c + 1) * GROUPS)
            ]
            terms.append(transform(spread(msg_ref, lanes, c, keep), weights))
        if islands == 2:
            total = terms[0] + terms[1]
        else:
            total = None
            for island in range(islands):
                term = terms[0]
                for away in range(1, islands):
                    origin = lax.rem(me_ref[0] + islands - away, islands)
                    term = jnp.where(origin == island, terms[away], term)
                total = term if total is None else total + term
        out_ref[rows] = (p_ref[rows] - total * (1.0 / islands)).astype(out_ref.dtype)


def on_chip(kernel, out_shape, *args, name, scalars=0):
    vmem = pl.BlockSpec(memory_space=pltpu.VMEM)
    smem = pl.BlockSpec(memory_space=pltpu.SMEM)
    return pl.pallas_call(
        kernel,
        in_specs=[smem] * scalars + [vmem] * (len(args) - scalars),
        out_specs=jax.tree.map(lambda _: vmem, out_shape),
        out_shape=out_shape,
        compiler_params=pltpu.CompilerParams(vmem_limit_bytes=VMEM_LIMIT),
        cost_estimate=pl.CostEstimate(
            flops=5 * 10**8, bytes_accessed=4 * 2**20, transcendentals=0
        ),
        name=name,
    )(*args)


def local(momentum, gradient, params, indices):
    islands = lax.axis_size("island")
    _, count, length = momentum.shape
    keep = indices.shape[2]
    table = jnp.asarray(dct_table(length))
    numbers = indices[0].T
    short = numbers.astype(jnp.int16)
    rings = [
        [(i, (i + away) % islands) for i in range(islands)] for away in range(1, islands)
    ]
    other_numbers = [lax.ppermute(short, "island", ring) for ring in rings]

    tail = -(-(count // length) // 16) * 16
    packed = jax.ShapeDtypeStruct((count * keep // length + tail, length), jnp.int16)
    wide = jax.ShapeDtypeStruct((count, length), jnp.float32)
    lanes = jax.ShapeDtypeStruct((count, length), jnp.int32)
    fresh = jax.ShapeDtypeStruct((count, length), jnp.bfloat16)

    msg = on_chip(encode_kernel, packed, table, numbers, momentum[0], gradient[0], name="encode")
    other_msgs = [lax.ppermute(msg, "island", ring) for ring in rings]
    new_momentum, back = on_chip(
        own_kernel, (wide, wide), table, numbers, msg, momentum[0], gradient[0], name="own"
    )
    places = [on_chip(positions_kernel, lanes, other, name="positions") for other in other_numbers]
    me = lax.axis_index("island").astype(jnp.int32)[None]
    new_params = on_chip(
        functools.partial(finish_kernel, islands),
        fresh, me, table, back, params, *other_msgs, *places, name="finish", scalars=1,
    )
    return new_momentum[None], new_params


def solution(mesh):
    in_specs = (
        P("island", "fsdp", None),
        P("island", "fsdp", None),
        P("fsdp", None),
        P("island", "fsdp", None),
    )
    out_specs = (P("island", "fsdp", None), P("fsdp", None))
    return jax.shard_map(local, mesh=mesh, in_specs=in_specs, out_specs=out_specs, check_vma=False)
```

time: 131 us -> 16 us (0.12)
  matrix products: 86 us -> 0 us
  other arithmetic: 19.2 us -> 1.03 us
  blocking collectives: 18.1 us -> 0 us
  Pallas kernels: 0 us -> 6.62 us
  local copies, waits for them, and re-layouts: 5.95 us -> 2.29 us
  starting transfers between devices: 0 us -> 3.13 us
  waiting for transfers between devices: 0 us -> 2.06 us
    dot_general x27 -> x0, matrix products: 86 us -> none  [the longest x16 47 us: place(): jnp.einsum('ck,ckt->ct', pair[0][other], onehot, precision=lax.Precision....]
    all_gather x2 -> x0, blocking collectives: 18.1 us -> none  [the longest x1 9.93 us: local(): lax.all_gather(values[None], 'island', axis=0, tiled=True)]
    reduce_or x1 -> x0, other arithmetic: 12.4 us -> none  [keep_mask(): hits = jnp.any(numbers[:, :, None] == counter, axis=1)]
    pallas_call x0 -> x4, Pallas kernels: none -> 6.62 us  [on_chip(): pl.pallas_call(kernel, in_specs=[smem] * scalars + [vmem] * (len(args) -...]
    dynamic_update_slice x8 -> x0, other arithmetic: 5.41 us -> none  [spread_total(): return lax.map(place, (value_blocks, number_blocks)).reshape(count, length)]
    while x32 -> x0, local copies, waits for them, and re-layouts: 3.31 us -> none
    ppermute x0 -> x2, starting transfers between devices: none -> 3.13 us  [the longest x1 3.03 us: local(): other_numbers = [lax.ppermute(short, 'island', ring) for ring in rings]]
    ppermute x0 -> x2, waiting for transfers between devices: none -> 2.06 us  [the longest x1 2.06 us: local(): other_msgs = [lax.ppermute(msg, 'island', ring) for ring in rings]]
  transfers between devices with their start and end apart: 0 -> 2, of which waited for: 0 -> 1; matrix products, arithmetic and copies ran while one was open for 0% -> 0% of each run, Pallas kernels for 0% -> 30%
where the time goes in v2:
time: 16 us; the launch traced here: 15.8 us
  Pallas kernels  6.62 us (41%)
  starting transfers between devices  3.13 us (20%)
  local copies, waits for them, and re-layouts  2.29 us (14%)
  waiting for transfers between devices  2.06 us (13%)
  other arithmetic  1.03 us (6%)
  between operations  0.67 us (4%)
    pallas_call x4, Pallas kernels, on_chip(): pl.pallas_call(kernel, in_specs=[smem] * scalars + [vmem] * (len(args) -...  6.62 us
    ppermute x1, starting transfers between devices, local(): other_numbers = [lax.ppermute(short, 'island', ring) for ring in rings]  3.03 us
    unnamed x14, local copies, waits for them, and re-layouts  2.29 us
    ppermute x1, waiting for transfers between devices, local(): other_msgs = [lax.ppermute(msg, 'island', ring) for ring in rings]  2.06 us
    convert_element_type x1, other arithmetic, local(): short = numbers.astype(jnp.int16)  1.03 us
  transfers between devices with their start and end apart: 2, of which 1 were waited for; matrix products, arithmetic and copies ran while one was open for 0% of the time, Pallas kernels for 30%

profile of v2, /device:TPU:0, one launch (start us, length us, event | category | flops | bytes accessed | tf_op | source)
XLA Modules:
  0.0 15.8 jit_solution(1544955043028942882)
XLA Ops:
  0.6 0.0 copy-start.6
  0.6 0.0 copy-start.2
  0.7 1.0 %bitcast_convert_fusion = s16[32,2048]{1,0:T(8,128)(2,1)S(1)} fusion(s32[1,2048,32]{1,2,0:T(8,128)} %param.8), kind=kLoop, calls=%fused_computation | loop fusion | flops 65536 | bytes 393216 | tf_op jit(solution)/shard_map/convert_element_type | solution.py:247
  1.7 3.0 %collective-permute-start.1 = (s16[32,2048]{1,0:T(8,128)(2,1)S(1)}, s16[32,2048]{1,0:T(8,128)(2,1)S(1)}, u32[]{:S(2)}, u32[]{:S(2)}) collective-permute-start(s16[32,2048]{1,0:T(8,128)(2,1)S(1)} %bitcast_convert_fusion), channel_id=1, source_target_pairs={{0,16},{16,0},{1,17},{17,1},{2,18},{18,2},{3,19},{19,3},{4,20},{20... | collective-permute-start | bytes 393224 | tf_op jit(solution)/shard_map/ppermute | solution.py:251
  4.7 0.0 copy-done.6
  4.7 0.0 copy-done.2
  4.7 0.0 copy-start
  4.7 1.2 %copy-done = f32[1,2048,128]{2,1,0:T(8,128)S(1)} copy-done((f32[1,2048,128]{2,1,0:T(8,128)S(1)}, f32[1,2048,128]{2,1,0:T(8,128)}, u32[]{:S(2)}) %copy-start) | copy-done | bytes 1048600
  5.9 0.0 copy-start.3
  6.0 1.0 %copy-done.3 = bf16[1,2048,128]{2,1,0:T(8,128)(2,1)S(1)} copy-done((bf16[1,2048,128]{2,1,0:T(8,128)(2,1)S(1)}, bf16[1,2048,128]{2,1,0:T(8,128)(2,1)}, u32[]{:S(2)}) %copy-start.3) | copy-done | bytes 524312
  7.0 0.0 copy-start.1
  7.0 0.0 copy-start.4
  7.0 1.8 %encode.1.msg_ref = s16[528,128]{1,0:T(8,128)(2,1)S(1)} custom-call(f32[128,128]{1,0:T(8,128)S(1)} %copy-done.6, s32[32,2048]{1,0:T(8,128)S(1)} %bitcast.10, f32[2048,128]{1,0:T(8,128)S(1)} %bitcast.8, bf16[2048,128]{1,0:T(8,128)(2,1)S(1)} %bitcast.12), custom_call_target="tpu_custom_call" | custom-call | flops 500000000 | bytes 4194304 | tf_op jit(solution)/shard_map/encode/pallas_call | solution.py:228
  8.8 0.1 collective-permute-start
  8.9 0.0 copy-done.1
  8.9 0.0 copy-done.4
  8.9 2.4 %own.1 = (f32[2048,128]{1,0:T(8,128)}, f32[2048,128]{1,0:T(8,128)S(1)}) custom-call(f32[128,128]{1,0:T(8,128)S(1)} %copy-done.6, s32[32,2048]{1,0:T(8,128)S(1)} %bitcast.11, s16[528,128]{1,0:T(8,128)(2,1)S(1)} %encode.1.msg_ref, f32[2048,128]{1,0:T(8,128)S(1)} %bitcast.9, bf16[2048,128]{1,0:T(8,128)(2,1)S(1)} %bitcast.13), custom_call_target="tpu_custom_call" | custom-call | flops 500000000 | bytes 4194304 | tf_op jit(solution)/shard_map/own/pallas_call | solution.py:228
  11.3 0.0 copy-start.5
  11.4 0.0 collective-permute-done.1.idx_ref
  11.4 0.5 %positions.1.refs_1_ = s32[2048,128]{1,0:T(8,128)S(1)} custom-call(s16[32,2048]{1,0:T(8,128)(2,1)S(1)} %collective-permute-done.1.idx_ref), custom_call_target="tpu_custom_call" | custom-call | flops 500000000 | bytes 4194304 | tf_op jit(solution)/shard_map/positions/pallas_call | solution.py:228
  11.9 2.1 %collective-permute-done.refs_0_ = s16[528,128]{1,0:T(8,128)(2,1)S(1)} collective-permute-done((s16[528,128]{1,0:T(8,128)(2,1)S(1)}, s16[528,128]{1,0:T(8,128)(2,1)S(1)}, u32[]{:S(2)}, u32[]{:S(2)}) %collective-permute-start) | collective-permute-done | bytes 135200 | tf_op jit(solution)/shard_map/ppermute | solution.py:260
  13.9 0.0 copy-done.5
  13.9 1.9 %finish.1 = bf16[2048,128]{1,0:T(8,128)(2,1)} custom-call(s32[1]{0:T(128)} %bitcast.6.me_ref, f32[128,128]{1,0:T(8,128)S(1)} %copy-done.6, f32[2048,128]{1,0:T(8,128)S(1)} %get-tuple-element.5.back_ref, f32[2048,128]{1,0:T(8,128)S(1)} %copy-done.5, s16[528,128]{1,0:T(8,128)(2,1)S(1)} %collective-permute-done.refs_0_, s32[2048,128]{1,0:T(8,128)S(1)} %positions.1.refs_1_), custom_call_target="tpu_custom_call" | custom-call | flops 500000000 | bytes 4194304 | tf_op jit(solution)/shard_map/finish/pallas_call | solution.py:228
Async XLA Ops:
  0.6 4.1 %copy-start.6 = (f32[128,128]{1,0:T(8,128)S(1)}, f32[128,128]{1,0:T(8,128)}, u32[]{:S(2)}) copy-start(f32[128,128]{1,0:T(8,128)} %constant.8.clone.table_ref) | copy-start | bytes 196612
  0.6 4.1 %copy-start.2 = (s32[1,2048,32]{1,2,0:T(8,128)S(1)}, s32[1,2048,32]{1,2,0:T(8,128)}, u32[]{:S(2)}) copy-start(s32[1,2048,32]{1,2,0:T(8,128)} %param.8) | copy-start | bytes 786436
  1.7 9.7 %collective-permute-start.1 = (s16[32,2048]{1,0:T(8,128)(2,1)S(1)}, s16[32,2048]{1,0:T(8,128)(2,1)S(1)}, u32[]{:S(2)}, u32[]{:S(2)}) collective-permute-start(s16[32,2048]{1,0:T(8,128)(2,1)S(1)} %bitcast_convert_fusion), channel_id=1, source_target_pairs={{0,16},{16,0},{1,17},{17,1},{2,18},{18,2},{3,19},{19,3},{4,20},{20... | collective-permute-start | bytes 393224 | tf_op jit(solution)/shard_map/ppermute | solution.py:251
  4.7 1.2 %copy-start = (f32[1,2048,128]{2,1,0:T(8,128)S(1)}, f32[1,2048,128]{2,1,0:T(8,128)}, u32[]{:S(2)}) copy-start(f32[1,2048,128]{2,1,0:T(8,128)} %param.5) | copy-start | bytes 3145732
  5.9 1.0 %copy-start.3 = (bf16[1,2048,128]{2,1,0:T(8,128)(2,1)S(1)}, bf16[1,2048,128]{2,1,0:T(8,128)(2,1)}, u32[]{:S(2)}) copy-start(bf16[1,2048,128]{2,1,0:T(8,128)(2,1)} %param.6) | copy-start | bytes 1572868
  7.0 1.9 %copy-start.1 = (f32[1,2048,128]{2,1,0:T(8,128)S(1)}, f32[1,2048,128]{2,1,0:T(8,128)}, u32[]{:S(2)}) copy-start(f32[1,2048,128]{2,1,0:T(8,128)} %param.5) | copy-start | bytes 3145732
  7.0 1.9 %copy-start.4 = (bf16[1,2048,128]{2,1,0:T(8,128)(2,1)S(1)}, bf16[1,2048,128]{2,1,0:T(8,128)(2,1)}, u32[]{:S(2)}) copy-start(bf16[1,2048,128]{2,1,0:T(8,128)(2,1)} %param.6) | copy-start | bytes 1572868
  8.8 5.1 %collective-permute-start = (s16[528,128]{1,0:T(8,128)(2,1)S(1)}, s16[528,128]{1,0:T(8,128)(2,1)S(1)}, u32[]{:S(2)}, u32[]{:S(2)}) collective-permute-start(s16[528,128]{1,0:T(8,128)(2,1)S(1)} %encode.1.msg_ref), channel_id=1, source_target_pairs={{0,16},{16,0},{1,17},{17,1},{2,18},{18,2},{3,19},{19,3},{4,20},{20... | collective-permute-start | bytes 405512 | tf_op jit(solution)/shard_map/ppermute | solution.py:260
  11.3 2.6 %copy-start.5 = (f32[2048,128]{1,0:T(8,128)S(1)}, f32[2048,128]{1,0:T(8,128)}, u32[]{:S(2)}) copy-start(f32[2048,128]{1,0:T(8,128)} %p_ref.1) | copy-start | bytes 3145732

commit v3 on v2

--- a/solution.py
+++ b/solution.py
@@ -121,20 +121,30 @@
     ]
 
 
-def encode_kernel(table_ref, idx_ref, m_ref, g_ref, msg_ref):
-    count, length = m_ref.shape
-    keep = idx_ref.shape[0]
-    weights = weights_of(table_ref[...].T)
-    group = lax.broadcasted_iota(jnp.int32, (length, length), 1) // keep
-    scales = []
-    for c in range(count // (GROUPS * length)):
-        picks = jnp.concatenate(
+def shorten_kernel(idx_ref, short_ref):
+    short_ref[...] = idx_ref[...].astype(jnp.int16)
+
+
+def order_kernel(idx_ref, picks_ref):
+    length = picks_ref.shape[1]
+    for c in range(picks_ref.shape[0] // length):
+        picks_ref[c * length : (c + 1) * length] = jnp.concatenate(
             [
                 sorted_numbers(idx_ref[:, b * length : (b + 1) * length], length)
                 for b in range(c * GROUPS, (c + 1) * GROUPS)
             ],
             axis=0,
         ).T
+
+
+def encode_kernel(table_ref, picks_ref, m_ref, g_ref, msg_ref):
+    count, length = m_ref.shape
+    keep = length // GROUPS
+    weights = weights_of(table_ref[...].T)
+    group = lax.broadcasted_iota(jnp.int32, (length, length), 1) // keep
+    scales = []
+    for c in range(count // (GROUPS * length)):
+        picks = picks_ref[c * length : (c + 1) * length]
         rows = slice(c * GROUPS * length, (c + 1) * GROUPS * length)
         mom = 0.999 * m_ref[rows] + g_ref[rows].astype(jnp.float32)
         coef = transform(mom, weights)
@@ -175,7 +185,13 @@
     )
 
 
-def own_kernel(table_ref, idx_ref, msg_ref, m_ref, g_ref, new_ref, back_ref):
+def copy_out(held_ref, out_ref, sems, c):
+    size = held_ref.shape[0] // sems.shape[0]
+    rows = pl.ds(c * size, size)
+    return pltpu.make_async_copy(held_ref.at[rows], out_ref.at[rows], sems.at[c])
+
+
+def own_kernel(table_ref, idx_ref, msg_ref, m_ref, g_ref, new_ref, back_ref, held_ref, sems):
     count, length = m_ref.shape
     keep = idx_ref.shape[0]
     weights = weights_of(table_ref[...])
@@ -184,7 +200,10 @@
         lanes = all_positions(idx_ref[:, rows], length)
         back = transform(spread(msg_ref, lanes, c, keep), weights)
         back_ref[rows] = back
-        new_ref[rows] = 0.999 * m_ref[rows] + g_ref[rows].astype(jnp.float32) - back
+        held_ref[rows] = 0.999 * m_ref[rows] + g_ref[rows].astype(jnp.float32) - back
+        copy_out(held_ref, new_ref, sems, c).start()
+    for c in range(sems.shape[0]):
+        copy_out(held_ref, new_ref, sems, c).wait()
 
 
 def positions_kernel(idx_ref, lanes_ref):
@@ -195,7 +214,7 @@
 
 
 def finish_kernel(islands, me_ref, table_ref, back_ref, p_ref, *refs):
-    out_ref = refs[-1]
+    out_ref, held_ref, sems = refs[-3:]
     msgs, places = refs[: islands - 1], refs[islands - 1 : 2 * islands - 2]
     count, length = p_ref.shape
     keep = length // GROUPS
@@ -219,21 +238,31 @@
                     origin = lax.rem(me_ref[0] + islands - away, islands)
                     term = jnp.where(origin == island, terms[away], term)
                 total = term if total is None else total + term
-        out_ref[rows] = (p_ref[rows] - total * (1.0 / islands)).astype(out_ref.dtype)
-
-
-def on_chip(kernel, out_shape, *args, name, scalars=0):
+        held_ref[rows] = (p_ref[rows] - total * (1.0 / islands)).astype(out_ref.dtype)
+        copy_out(held_ref, out_ref, sems, c).start()
+    for c in range(sems.shape[0]):
+        copy_out(held_ref, out_ref, sems, c).wait()
+
+
+def on_chip(kernel, out_shape, *args, name, flops=5 * 10**8, scalars=0, written=None):
     vmem = pl.BlockSpec(memory_space=pltpu.VMEM)
     smem = pl.BlockSpec(memory_space=pltpu.SMEM)
+    out_specs = [vmem] * len(out_shape)
+    scratch = []
+    if written:
+        out_specs[0] = pl.BlockSpec(memory_space=pl.ANY)
+        scratch = [
+            pltpu.VMEM(out_shape[0].shape, out_shape[0].dtype),
+            pltpu.SemaphoreType.DMA((written,)),
+        ]
     return pl.pallas_call(
         kernel,
         in_specs=[smem] * scalars + [vmem] * (len(args) - scalars),
-        out_specs=jax.tree.map(lambda _: vmem, out_shape),
+        out_specs=out_specs,
         out_shape=out_shape,
+        scratch_shapes=scratch,
         compiler_params=pltpu.CompilerParams(vmem_limit_bytes=VMEM_LIMIT),
-        cost_estimate=pl.CostEstimate(
-            flops=5 * 10**8, bytes_accessed=4 * 2**20, transcendentals=0
-        ),
+        cost_estimate=pl.CostEstimate(flops=flops, bytes_accessed=4 * 2**20, transcendentals=0),
         name=name,
     )(*args)
 
@@ -244,28 +273,38 @@
     keep = indices.shape[2]
     table = jnp.asarray(dct_table(length))
     numbers = indices[0].T
-    short = numbers.astype(jnp.int16)
+    chunks = count // (GROUPS * length)
     rings = [
         [(i, (i + away) % islands) for i in range(islands)] for away in range(1, islands)
     ]
+
+    def array(rows, dtype):
+        return jax.ShapeDtypeStruct((rows, length), dtype)
+
+    short_shape = jax.ShapeDtypeStruct(numbers.shape, jnp.int16)
+    (short,) = on_chip(shorten_kernel, [short_shape], numbers, name="shorten", flops=5 * 10**9)
     other_numbers = [lax.ppermute(short, "island", ring) for ring in rings]
-
+    (picks,) = on_chip(order_kernel, [array(chunks * length, jnp.int32)], numbers, name="order")
     tail = -(-(count // length) // 16) * 16
-    packed = jax.ShapeDtypeStruct((count * keep // length + tail, length), jnp.int16)
-    wide = jax.ShapeDtypeStruct((count, length), jnp.float32)
-    lanes = jax.ShapeDtypeStruct((count, length), jnp.int32)
-    fresh = jax.ShapeDtypeStruct((count, length), jnp.bfloat16)
-
-    msg = on_chip(encode_kernel, packed, table, numbers, momentum[0], gradient[0], name="encode")
+    packed = array(chunks * length + tail, jnp.int16)
+    (msg,) = on_chip(
+        encode_kernel, [packed], table, picks, momentum[0], gradient[0], name="encode"
+    )
     other_msgs = [lax.ppermute(msg, "island", ring) for ring in rings]
+    wide = array(count, jnp.float32)
     new_momentum, back = on_chip(
-        own_kernel, (wide, wide), table, numbers, msg, momentum[0], gradient[0], name="own"
-    )
-    places = [on_chip(positions_kernel, lanes, other, name="positions") for other in other_numbers]
+        own_kernel, [wide, wide], table, numbers, msg, momentum[0], gradient[0],
+        name="own", written=chunks,
+    )
+    places = [
+        on_chip(positions_kernel, [array(count, jnp.int32)], other, name="positions")[0]
+        for other in other_numbers
+    ]
     me = lax.axis_index("island").astype(jnp.int32)[None]
-    new_params = on_chip(
+    (new_params,) = on_chip(
         functools.partial(finish_kernel, islands),
-        fresh, me, table, back, params, *other_msgs, *places, name="finish", scalars=1,
+        [array(count, jnp.bfloat16)], me, table, back, params, *other_msgs, *places,
+        name="finish", scalars=1, written=chunks,
     )
     return new_momentum[None], new_params
 

time: 16 us -> 13.9 us (0.87)
  local copies, waits for them, and re-layouts: 2.29 us -> 0.98 us
  other arithmetic: 1.03 us -> 0 us
  starting transfers between devices: 3.13 us -> 3.6 us
  waiting for transfers between devices: 2.06 us -> 1.71 us
    unnamed x14 -> x12, local copies, waits for them, and re-layouts: 2.29 us -> 0.98 us
    convert_element_type x1 -> x0, other arithmetic: 1.03 us -> none  [local(): short = numbers.astype(jnp.int16)]
    ppermute x1, starting transfers between devices: 0.09 us -> 0.57 us  [local(): other_msgs = [lax.ppermute(msg, 'island', ring) for ring in rings]]
    ppermute x1, waiting for transfers between devices: 2.06 us -> 1.71 us  [local(): other_msgs = [lax.ppermute(msg, 'island', ring) for ring in rings]]
    pallas_call x4 -> x6, Pallas kernels: 6.62 us -> 6.71 us  [on_chip(): pl.pallas_call(kernel, in_specs=[smem] * scalars + [vmem] * (len(args) -...]
  transfers between devices with their start and end apart: 2 -> 2, of which waited for: 1 -> 1; matrix products, arithmetic and copies ran while one was open for 0% -> 0% of each run, Pallas kernels for 30% -> 36%
where the time goes in v3:
time: 13.9 us; the launch traced here: 13.7 us
  Pallas kernels  6.71 us (48%)
  starting transfers between devices  3.6 us (26%)
  waiting for transfers between devices  1.71 us (12%)
  local copies, waits for them, and re-layouts  0.98 us (7%)
  between operations  0.73 us (5%)
    pallas_call x6, Pallas kernels, on_chip(): pl.pallas_call(kernel, in_specs=[smem] * scalars + [vmem] * (len(args) -...  6.71 us
    ppermute x1, starting transfers between devices, local(): other_numbers = [lax.ppermute(short, 'island', ring) for ring in rings]  3.03 us
    ppermute x1, waiting for transfers between devices, local(): other_msgs = [lax.ppermute(msg, 'island', ring) for ring in rings]  1.71 us
    unnamed x12, local copies, waits for them, and re-layouts  0.98 us
    ppermute x1, starting transfers between devices, local(): other_msgs = [lax.ppermute(msg, 'island', ring) for ring in rings]  0.57 us
  transfers between devices with their start and end apart: 2, of which 1 were waited for; matrix products, arithmetic and copies ran while one was open for 0% of the time, Pallas kernels for 36%

profile of v3, /device:TPU:0, one launch (start us, length us, event | category | flops | bytes accessed | tf_op | source)
XLA Modules:
  0.0 13.7 jit_solution(771622443945096848)
XLA Ops:
  0.6 0.0 copy-start.4
  0.6 0.9 %copy-done.4 = s32[1,2048,32]{1,2,0:T(8,128)S(1)} copy-done((s32[1,2048,32]{1,2,0:T(8,128)S(1)}, s32[1,2048,32]{1,2,0:T(8,128)}, u32[]{:S(2)}) %copy-start.4) | copy-done | bytes 262168
  1.6 0.0 copy-start
  1.6 0.0 copy-start.1
  1.6 0.0 copy-start.3
  1.6 3.0 %collective-permute-start.1 = (s16[32,2048]{1,0:T(8,128)(2,1)S(1)}, s16[32,2048]{1,0:T(8,128)(2,1)S(1)}, u32[]{:S(2)}, u32[]{:S(2)}) collective-permute-start(s16[32,2048]{1,0:T(8,128)(2,1)S(1)} %shorten.1), channel_id=1, source_target_pairs={{0,16},{16,0},{1,17},{17,1},{2,18},{18,2},{3,19},{19,3},{4,20},{20... | collective-permute-start | bytes 393224 | tf_op jit(solution)/shard_map/ppermute | solution.py:286
  4.7 0.7 %order.1.picks_ref = s32[512,128]{1,0:T(8,128)S(1)} custom-call(s32[32,2048]{1,0:T(8,128)S(1)} %bitcast.12), custom_call_target="tpu_custom_call" | custom-call | flops 500000000 | bytes 4194304 | tf_op jit(solution)/shard_map/order/pallas_call | solution.py:258
  5.4 0.0 copy-done
  5.4 0.0 copy-done.1
  5.4 0.0 copy-done.3
  5.4 0.0 copy-start.5
  5.4 1.4 %encode.1.msg_ref = s16[528,128]{1,0:T(8,128)(2,1)S(1)} custom-call(f32[128,128]{1,0:T(8,128)S(1)} %copy-done.3, s32[512,128]{1,0:T(8,128)S(1)} %order.1.picks_ref, f32[2048,128]{1,0:T(8,128)S(1)} %bitcast.7, bf16[2048,128]{1,0:T(8,128)(2,1)S(1)} %bitcast.9), custom_call_target="tpu_custom_call" | custom-call | flops 500000000 | bytes 4194304 | tf_op jit(solution)/shard_map/encode/pallas_call | solution.py:258
  6.8 0.6 %collective-permute-start = (s16[528,128]{1,0:T(8,128)(2,1)S(1)}, s16[528,128]{1,0:T(8,128)(2,1)S(1)}, u32[]{:S(2)}, u32[]{:S(2)}) collective-permute-start(s16[528,128]{1,0:T(8,128)(2,1)S(1)} %encode.1.msg_ref), channel_id=1, source_target_pairs={{0,16},{16,0},{1,17},{17,1},{2,18},{18,2},{3,19},{19,3},{4,20},{20... | collective-permute-start | bytes 405512 | tf_op jit(solution)/shard_map/ppermute | solution.py:293
  7.4 0.0 copy-done.5
  7.4 2.3 %own.1 = (f32[2048,128]{1,0:T(8,128)}, f32[2048,128]{1,0:T(8,128)S(1)}) custom-call(f32[128,128]{1,0:T(8,128)S(1)} %copy-done.3, s32[32,2048]{1,0:T(8,128)S(1)} %bitcast.13, s16[528,128]{1,0:T(8,128)(2,1)S(1)} %encode.1.msg_ref, f32[2048,128]{1,0:T(8,128)S(1)} %bitcast.8, bf16[2048,128]{1,0:T(8,128)(2,1)S(1)} %bitcast.10), custom_call_target="tpu_custom_call" | custom-call | flops 500000000 | bytes 4194304 | tf_op jit(solution)/shard_map/own/pallas_call | solution.py:258
  9.7 0.0 copy-start.2
  9.7 0.0 collective-permute-done.1.idx_ref
  9.7 0.5 %positions.1.refs_1_ = s32[2048,128]{1,0:T(8,128)S(1)} custom-call(s16[32,2048]{1,0:T(8,128)(2,1)S(1)} %collective-permute-done.1.idx_ref), custom_call_target="tpu_custom_call" | custom-call | flops 500000000 | bytes 4194304 | tf_op jit(solution)/shard_map/positions/pallas_call | solution.py:258
  10.2 1.7 %collective-permute-done.refs_0_ = s16[528,128]{1,0:T(8,128)(2,1)S(1)} collective-permute-done((s16[528,128]{1,0:T(8,128)(2,1)S(1)}, s16[528,128]{1,0:T(8,128)(2,1)S(1)}, u32[]{:S(2)}, u32[]{:S(2)}) %collective-permute-start) | collective-permute-done | bytes 135200 | tf_op jit(solution)/shard_map/ppermute | solution.py:293
  11.9 0.0 copy-done.2
  11.9 1.8 %finish.1 = bf16[2048,128]{1,0:T(8,128)(2,1)} custom-call(s32[1]{0:T(128)} %bitcast.6.me_ref, f32[128,128]{1,0:T(8,128)S(1)} %copy-done.3, f32[2048,128]{1,0:T(8,128)S(1)} %get-tuple-element.5.back_ref, f32[2048,128]{1,0:T(8,128)S(1)} %copy-done.2, s16[528,128]{1,0:T(8,128)(2,1)S(1)} %collective-permute-done.refs_0_, s32[2048,128]{1,0:T(8,128)S(1)} %positions.1.refs_1_), custom_call_target="tpu_custom_call" | custom-call | flops 500000000 | bytes 4194304 | tf_op jit(solution)/shard_map/finish/pallas_call | solution.py:258
  (1 shorter events, 0.0 us)
Async XLA Ops:
  0.6 1.0 %copy-start.4 = (s32[1,2048,32]{1,2,0:T(8,128)S(1)}, s32[1,2048,32]{1,2,0:T(8,128)}, u32[]{:S(2)}) copy-start(s32[1,2048,32]{1,2,0:T(8,128)} %param.8) | copy-start | bytes 786436
  1.6 3.8 %copy-start = (f32[1,2048,128]{2,1,0:T(8,128)S(1)}, f32[1,2048,128]{2,1,0:T(8,128)}, u32[]{:S(2)}) copy-start(f32[1,2048,128]{2,1,0:T(8,128)} %param.5) | copy-start | bytes 3145732
  1.6 3.8 %copy-start.1 = (bf16[1,2048,128]{2,1,0:T(8,128)(2,1)S(1)}, bf16[1,2048,128]{2,1,0:T(8,128)(2,1)}, u32[]{:S(2)}) copy-start(bf16[1,2048,128]{2,1,0:T(8,128)(2,1)} %param.6) | copy-start | bytes 1572868
  1.6 3.8 %copy-start.3 = (f32[128,128]{1,0:T(8,128)S(1)}, f32[128,128]{1,0:T(8,128)}, u32[]{:S(2)}) copy-start(f32[128,128]{1,0:T(8,128)} %constant.8.clone.table_ref) | copy-start | bytes 196612
  1.6 8.1 %collective-permute-start.1 = (s16[32,2048]{1,0:T(8,128)(2,1)S(1)}, s16[32,2048]{1,0:T(8,128)(2,1)S(1)}, u32[]{:S(2)}, u32[]{:S(2)}) collective-permute-start(s16[32,2048]{1,0:T(8,128)(2,1)S(1)} %shorten.1), channel_id=1, source_target_pairs={{0,16},{16,0},{1,17},{17,1},{2,18},{18,2},{3,19},{19,3},{4,20},{20... | collective-permute-start | bytes 393224 | tf_op jit(solution)/shard_map/ppermute | solution.py:286
  5.4 2.0 %copy-start.5 = (s32[1,2048,32]{1,2,0:T(8,128)S(1)}, s32[1,2048,32]{1,2,0:T(8,128)}, u32[]{:S(2)}) copy-start(s32[1,2048,32]{1,2,0:T(8,128)} %param.8) | copy-start | bytes 786436
  6.8 5.1 %collective-permute-start = (s16[528,128]{1,0:T(8,128)(2,1)S(1)}, s16[528,128]{1,0:T(8,128)(2,1)S(1)}, u32[]{:S(2)}, u32[]{:S(2)}) collective-permute-start(s16[528,128]{1,0:T(8,128)(2,1)S(1)} %encode.1.msg_ref), channel_id=1, source_target_pairs={{0,16},{16,0},{1,17},{17,1},{2,18},{18,2},{3,19},{19,3},{4,20},{20... | collective-permute-start | bytes 405512 | tf_op jit(solution)/shard_map/ppermute | solution.py:293
  9.7 2.2 %copy-start.2 = (f32[2048,128]{1,0:T(8,128)S(1)}, f32[2048,128]{1,0:T(8,128)}, u32[]{:S(2)}) copy-start(f32[2048,128]{1,0:T(8,128)} %p_ref.1) | copy-start | bytes 3145732

commit v4 on v3

--- a/solution.py
+++ b/solution.py
@@ -44,8 +44,8 @@
     return both[:, :length] + both[:, length:]
 
 
-def lanes_of(x, index):
-    return jnp.take_along_axis(x, index, axis=1, mode="promise_in_bounds")
+def rows_of(x, index):
+    return jnp.take_along_axis(x, index, axis=0, mode="promise_in_bounds")
 
 
 def row_iota():
@@ -80,27 +80,25 @@
     out = []
     for v in range(0, part.shape[0], SUB):
         rank = row_iota() + v
-        word, base, place = words[0], bases[0], jnp.zeros_like(rank)
+        word, base, end = words[0], bases[0], jnp.full_like(rank, WORD)
         for w in range(1, len(words)):
             up = rank >= bases[w]
             word = jnp.where(up, words[w], word)
             base = jnp.where(up, bases[w], base)
-            place = jnp.where(up, w * WORD, place)
+            end = jnp.where(up, (w + 1) * WORD, end)
         rank = rank - base
+        left = jnp.full_like(rank, WORD)
         half = WORD // 2
         while half:
-            below = lax.population_count(word & ((1 << half) - 1))
-            up = rank >= below
-            rank = jnp.where(up, rank - below, rank)
-            word = jnp.where(up, lax.shift_right_logical(word, half), word)
-            place = jnp.where(up, place + half, place)
+            less = left - half
+            below = lax.population_count(lax.shift_left(word, less))
+            left = jnp.where(rank >= below, less, left)
             half //= 2
-        out.append(place)
+        out.append(end - left)
     return jnp.concatenate(out, axis=0)
 
 
-def positions(part, group, length):
-    keep = part.shape[0]
+def positions(part, length):
     words = mask_words(part, length)
     bases = bases_of(words)
     out = []
@@ -108,17 +106,28 @@
         place = row_iota() + t % WORD
         word = words[t // WORD]
         low = lax.shift_left(jnp.ones_like(place), place) - 1
-        rank = lax.population_count(word & low) + (bases[t // WORD] + group * keep)
+        rank = lax.population_count(word & low) + bases[t // WORD]
         held = lax.shift_right_logical(word, place) & 1
         out.append(jnp.where(held == 1, rank, -1))
-    return jnp.concatenate(out, axis=0).T
-
-
-def all_positions(numbers, length):
-    return [
-        positions(numbers[:, b * length : (b + 1) * length], b % GROUPS, length)
-        for b in range(numbers.shape[1] // length)
-    ]
+    return jnp.concatenate(out, axis=0)
+
+
+def choose(pieces, index):
+    inner = index & (SUB - 1)
+    found = {p: rows_of(x, inner) for p, x in pieces.items()}
+    bit = SUB
+    while len(found) > 1:
+        up = (index & bit) != 0
+        halves = {}
+        for p in sorted({p // 2 for p in found}):
+            low, high = found.get(2 * p), found.get(2 * p + 1)
+            if low is None or high is None:
+                halves[p] = high if low is None else low
+            else:
+                halves[p] = jnp.where(up, high, low)
+        found = halves
+        bit *= 2
+    return next(iter(found.values()))
 
 
 def shorten_kernel(idx_ref, short_ref):
@@ -134,28 +143,28 @@
                 for b in range(c * GROUPS, (c + 1) * GROUPS)
             ],
             axis=0,
-        ).T
+        )
 
 
 def encode_kernel(table_ref, picks_ref, m_ref, g_ref, msg_ref):
     count, length = m_ref.shape
     keep = length // GROUPS
+    spare = (length - keep) // SUB
     weights = weights_of(table_ref[...].T)
-    group = lax.broadcasted_iota(jnp.int32, (length, length), 1) // keep
     scales = []
     for c in range(count // (GROUPS * length)):
-        picks = picks_ref[c * length : (c + 1) * length]
         rows = slice(c * GROUPS * length, (c + 1) * GROUPS * length)
         mom = 0.999 * m_ref[rows] + g_ref[rows].astype(jnp.float32)
         coef = transform(mom, weights)
-        values = lanes_of(coef[:length], picks)
-        for g in range(1, GROUPS):
-            other = lanes_of(coef[g * length : (g + 1) * length], picks)
-            values = jnp.where(group == g, other, values)
-        turned = values.T
         coded = []
         for g in range(GROUPS):
-            part = turned[g * keep : (g + 1) * keep]
+            turned = coef[g * length : (g + 1) * length].T
+            values = []
+            for v in range(keep // SUB):
+                at = c * length + g * keep + v * SUB
+                pieces = {p: turned[p * SUB : (p + 1) * SUB] for p in range(v, v + spare + 1)}
+                values.append(choose(pieces, picks_ref[at : at + SUB]))
+            part = jnp.concatenate(values, axis=0)
             top = jnp.max(jnp.abs(part), axis=0, keepdims=True)
             power = jnp.ceil(jnp.log2(jnp.maximum(top, TINY)))
             scales.append(power)
@@ -171,18 +180,26 @@
     )
 
 
-def spread(msg_ref, lanes, c, keep):
+def spread(msg_ref, ranks, c, base):
     length = msg_ref.shape[1]
+    keep = length // GROUPS
+    spare = (length - keep) // SUB
     rows = msg_ref[c * length : (c + 1) * length].astype(jnp.int32).astype(jnp.float32)
-    chunks = msg_ref.shape[0] // length
-    tail = msg_ref[chunks * length :].astype(jnp.int32).astype(jnp.float32)
+    tail = msg_ref[base:].astype(jnp.int32).astype(jnp.float32)
     unit = jnp.exp2(tail[c * GROUPS : (c + 1) * GROUPS]) * (1.0 / STEPS)
-    values = jnp.concatenate(
-        [rows[g * keep : (g + 1) * keep] * unit[g : g + 1] for g in range(GROUPS)], axis=0
-    ).T
-    return jnp.concatenate(
-        [jnp.where(at >= 0, lanes_of(values, at & (length - 1)), 0.0) for at in lanes], axis=0
-    )
+    out = []
+    for g, rank in enumerate(ranks):
+        values = rows[g * keep : (g + 1) * keep] * unit[g : g + 1]
+        dense = []
+        for t in range(length // SUB):
+            at = rank[t * SUB : (t + 1) * SUB]
+            pieces = {
+                p: values[p * SUB : (p + 1) * SUB]
+                for p in range(max(0, t - spare), min(keep // SUB - 1, t) + 1)
+            }
+            dense.append(jnp.where(at >= 0, choose(pieces, at), 0.0))
+        out.append(jnp.concatenate(dense, axis=0).T)
+    return jnp.concatenate(out, axis=0)
 
 
 def copy_out(held_ref, out_ref, sems, c):
@@ -193,12 +210,16 @@
 
 def own_kernel(table_ref, idx_ref, msg_ref, m_ref, g_ref, new_ref, back_ref, held_ref, sems):
     count, length = m_ref.shape
-    keep = idx_ref.shape[0]
+    size = GROUPS * length
+    base = count // GROUPS
     weights = weights_of(table_ref[...])
-    for c in range(count // (GROUPS * length)):
-        rows = slice(c * GROUPS * length, (c + 1) * GROUPS * length)
-        lanes = all_positions(idx_ref[:, rows], length)
-        back = transform(spread(msg_ref, lanes, c, keep), weights)
+    for c in range(count // size):
+        ranks = [
+            positions(idx_ref[:, b * length : (b + 1) * length], length)
+            for b in range(c * GROUPS, (c + 1) * GROUPS)
+        ]
+        rows = slice(c * size, (c + 1) * size)
+        back = transform(spread(msg_ref, ranks, c, base), weights)
         back_ref[rows] = back
         held_ref[rows] = 0.999 * m_ref[rows] + g_ref[rows].astype(jnp.float32) - back
         copy_out(held_ref, new_ref, sems, c).start()
@@ -206,28 +227,30 @@
         copy_out(held_ref, new_ref, sems, c).wait()
 
 
-def positions_kernel(idx_ref, lanes_ref):
-    length = lanes_ref.shape[1]
+def positions_kernel(idx_ref, ranks_ref):
+    length, count = ranks_ref.shape
     numbers = idx_ref[...].astype(jnp.int32)
-    for b, lanes in enumerate(all_positions(numbers, length)):
-        lanes_ref[b * length : (b + 1) * length] = lanes
+    for b in range(count // length):
+        lanes = slice(b * length, (b + 1) * length)
+        ranks_ref[:, lanes] = positions(numbers[:, lanes], length)
 
 
 def finish_kernel(islands, me_ref, table_ref, back_ref, p_ref, *refs):
     out_ref, held_ref, sems = refs[-3:]
     msgs, places = refs[: islands - 1], refs[islands - 1 : 2 * islands - 2]
     count, length = p_ref.shape
-    keep = length // GROUPS
+    size = GROUPS * length
+    base = count // GROUPS
     weights = weights_of(table_ref[...])
-    for c in range(count // (GROUPS * length)):
-        rows = slice(c * GROUPS * length, (c + 1) * GROUPS * length)
+    for c in range(count // size):
+        rows = slice(c * size, (c + 1) * size)
         terms = [back_ref[rows]]
-        for msg_ref, lanes_ref in zip(msgs, places):
-            lanes = [
-                lanes_ref[b * length : (b + 1) * length]
+        for msg_ref, ranks_ref in zip(msgs, places):
+            ranks = [
+                ranks_ref[:, b * length : (b + 1) * length]
                 for b in range(c * GROUPS, (c + 1) * GROUPS)
             ]
-            terms.append(transform(spread(msg_ref, lanes, c, keep), weights))
+            terms.append(transform(spread(msg_ref, ranks, c, base), weights))
         if islands == 2:
             total = terms[0] + terms[1]
         else:
@@ -297,7 +320,10 @@
         name="own", written=chunks,
     )
     places = [
-        on_chip(positions_kernel, [array(count, jnp.int32)], other, name="positions")[0]
+        on_chip(
+            positions_kernel, [jax.ShapeDtypeStruct((length, count), jnp.int32)], other,
+            name="positions",
+        )[0]
         for other in other_numbers
     ]
     me = lax.axis_index("island").astype(jnp.int32)[None]

time: 13.9 us -> 13 us (0.935)
  Pallas kernels: 6.71 us -> 5.75 us
  starting transfers between devices: 3.6 us -> 3.81 us
    pallas_call x6, Pallas kernels: 6.71 us -> 5.75 us  [on_chip(): pl.pallas_call(kernel, in_specs=[smem] * scalars + [vmem] * (len(args) -...]
    ppermute x1, starting transfers between devices: 0.57 us -> 0.77 us  [local(): other_msgs = [lax.ppermute(msg, 'island', ring) for ring in rings]]
  transfers between devices with their start and end apart: 2 -> 2, of which waited for: 1 -> 1; matrix products, arithmetic and copies ran while one was open for 0% -> 0% of each run, Pallas kernels for 36% -> 32%
where the time goes in v4:
time: 13 us; the launch traced here: 12.9 us
  Pallas kernels  5.75 us (44%)
  starting transfers between devices  3.81 us (29%)
  waiting for transfers between devices  1.6 us (12%)
  local copies, waits for them, and re-layouts  0.98 us (8%)
  between operations  0.74 us (6%)
    pallas_call x6, Pallas kernels, on_chip(): pl.pallas_call(kernel, in_specs=[smem] * scalars + [vmem] * (len(args) -...  5.75 us
    ppermute x1, starting transfers between devices, local(): other_numbers = [lax.ppermute(short, 'island', ring) for ring in rings]  3.03 us
    ppermute x1, waiting for transfers between devices, local(): other_msgs = [lax.ppermute(msg, 'island', ring) for ring in rings]  1.6 us
    unnamed x12, local copies, waits for them, and re-layouts  0.98 us
    ppermute x1, starting transfers between devices, local(): other_msgs = [lax.ppermute(msg, 'island', ring) for ring in rings]  0.77 us
  transfers between devices with their start and end apart: 2, of which 1 were waited for; matrix products, arithmetic and copies ran while one was open for 0% of the time, Pallas kernels for 32%

profile of v4, /device:TPU:0, one launch (start us, length us, event | category | flops | bytes accessed | tf_op | source)
XLA Modules:
  0.0 12.9 jit_solution(4536347798528487945)
XLA Ops:
  0.6 0.0 copy-start.4
  0.6 0.9 %copy-done.4 = s32[1,2048,32]{1,2,0:T(8,128)S(1)} copy-done((s32[1,2048,32]{1,2,0:T(8,128)S(1)}, s32[1,2048,32]{1,2,0:T(8,128)}, u32[]{:S(2)}) %copy-start.4) | copy-done | bytes 262168
  1.6 0.0 copy-start
  1.6 0.0 copy-start.1
  1.6 0.0 copy-start.3
  1.6 3.0 %collective-permute-start.1 = (s16[32,2048]{1,0:T(8,128)(2,1)S(1)}, s16[32,2048]{1,0:T(8,128)(2,1)S(1)}, u32[]{:S(2)}, u32[]{:S(2)}) collective-permute-start(s16[32,2048]{1,0:T(8,128)(2,1)S(1)} %shorten.1), channel_id=1, source_target_pairs={{0,16},{16,0},{1,17},{17,1},{2,18},{18,2},{3,19},{19,3},{4,20},{20... | collective-permute-start | bytes 393224 | tf_op jit(solution)/shard_map/ppermute | solution.py:309
  4.7 0.5 %order.1.picks_ref = s32[512,128]{1,0:T(8,128)S(1)} custom-call(s32[32,2048]{1,0:T(8,128)S(1)} %bitcast.12), custom_call_target="tpu_custom_call" | custom-call | flops 500000000 | bytes 4194304 | tf_op jit(solution)/shard_map/order/pallas_call | solution.py:281
  5.2 0.0 copy-done
  5.2 0.0 copy-done.1
  5.2 0.0 copy-done.3
  5.2 0.0 copy-start.5
  5.2 0.9 %encode.1.msg_ref = s16[528,128]{1,0:T(8,128)(2,1)S(1)} custom-call(f32[128,128]{1,0:T(8,128)S(1)} %copy-done.3, s32[512,128]{1,0:T(8,128)S(1)} %order.1.picks_ref, f32[2048,128]{1,0:T(8,128)S(1)} %bitcast.7, bf16[2048,128]{1,0:T(8,128)(2,1)S(1)} %bitcast.9), custom_call_target="tpu_custom_call" | custom-call | flops 500000000 | bytes 4194304 | tf_op jit(solution)/shard_map/encode/pallas_call | solution.py:281
  6.1 0.8 %collective-permute-start = (s16[528,128]{1,0:T(8,128)(2,1)S(1)}, s16[528,128]{1,0:T(8,128)(2,1)S(1)}, u32[]{:S(2)}, u32[]{:S(2)}) collective-permute-start(s16[528,128]{1,0:T(8,128)(2,1)S(1)} %encode.1.msg_ref), channel_id=1, source_target_pairs={{0,16},{16,0},{1,17},{17,1},{2,18},{18,2},{3,19},{19,3},{4,20},{20... | collective-permute-start | bytes 405512 | tf_op jit(solution)/shard_map/ppermute | solution.py:316
  6.9 0.0 copy-done.5
  6.9 2.3 %own.1 = (f32[2048,128]{1,0:T(8,128)}, f32[2048,128]{1,0:T(8,128)S(1)}) custom-call(f32[128,128]{1,0:T(8,128)S(1)} %copy-done.3, s32[32,2048]{1,0:T(8,128)S(1)} %bitcast.13, s16[528,128]{1,0:T(8,128)(2,1)S(1)} %encode.1.msg_ref, f32[2048,128]{1,0:T(8,128)S(1)} %bitcast.8, bf16[2048,128]{1,0:T(8,128)(2,1)S(1)} %bitcast.10), custom_call_target="tpu_custom_call" | custom-call | flops 500000000 | bytes 4194304 | tf_op jit(solution)/shard_map/own/pallas_call | solution.py:281
  9.2 0.0 copy-start.2
  9.2 0.0 collective-permute-done.1.idx_ref
  9.2 0.4 %positions.1.refs_1_ = s32[128,2048]{1,0:T(8,128)S(1)} custom-call(s16[32,2048]{1,0:T(8,128)(2,1)S(1)} %collective-permute-done.1.idx_ref), custom_call_target="tpu_custom_call" | custom-call | flops 500000000 | bytes 4194304 | tf_op jit(solution)/shard_map/positions/pallas_call | solution.py:281
  9.6 1.6 %collective-permute-done.refs_0_ = s16[528,128]{1,0:T(8,128)(2,1)S(1)} collective-permute-done((s16[528,128]{1,0:T(8,128)(2,1)S(1)}, s16[528,128]{1,0:T(8,128)(2,1)S(1)}, u32[]{:S(2)}, u32[]{:S(2)}) %collective-permute-start) | collective-permute-done | bytes 135200 | tf_op jit(solution)/shard_map/ppermute | solution.py:316
  11.2 0.0 copy-done.2
  11.2 1.7 %finish.1 = bf16[2048,128]{1,0:T(8,128)(2,1)} custom-call(s32[1]{0:T(128)} %bitcast.6.me_ref, f32[128,128]{1,0:T(8,128)S(1)} %copy-done.3, f32[2048,128]{1,0:T(8,128)S(1)} %get-tuple-element.5.back_ref, f32[2048,128]{1,0:T(8,128)S(1)} %copy-done.2, s16[528,128]{1,0:T(8,128)(2,1)S(1)} %collective-permute-done.refs_0_, s32[128,2048]{1,0:T(8,128)S(1)} %positions.1.refs_1_), custom_call_target="tpu_custom_call" | custom-call | flops 500000000 | bytes 4194304 | tf_op jit(solution)/shard_map/finish/pallas_call | solution.py:281
  (1 shorter events, 0.0 us)
Async XLA Ops:
  0.6 1.0 %copy-start.4 = (s32[1,2048,32]{1,2,0:T(8,128)S(1)}, s32[1,2048,32]{1,2,0:T(8,128)}, u32[]{:S(2)}) copy-start(s32[1,2048,32]{1,2,0:T(8,128)} %param.8) | copy-start | bytes 786436
  1.6 3.6 %copy-start = (f32[1,2048,128]{2,1,0:T(8,128)S(1)}, f32[1,2048,128]{2,1,0:T(8,128)}, u32[]{:S(2)}) copy-start(f32[1,2048,128]{2,1,0:T(8,128)} %param.5) | copy-start | bytes 3145732
  1.6 3.6 %copy-start.1 = (bf16[1,2048,128]{2,1,0:T(8,128)(2,1)S(1)}, bf16[1,2048,128]{2,1,0:T(8,128)(2,1)}, u32[]{:S(2)}) copy-start(bf16[1,2048,128]{2,1,0:T(8,128)(2,1)} %param.6) | copy-start | bytes 1572868
  1.6 3.6 %copy-start.3 = (f32[128,128]{1,0:T(8,128)S(1)}, f32[128,128]{1,0:T(8,128)}, u32[]{:S(2)}) copy-start(f32[128,128]{1,0:T(8,128)} %constant.8.clone.table_ref) | copy-start | bytes 196612
  1.6 7.5 %collective-permute-start.1 = (s16[32,2048]{1,0:T(8,128)(2,1)S(1)}, s16[32,2048]{1,0:T(8,128)(2,1)S(1)}, u32[]{:S(2)}, u32[]{:S(2)}) collective-permute-start(s16[32,2048]{1,0:T(8,128)(2,1)S(1)} %shorten.1), channel_id=1, source_target_pairs={{0,16},{16,0},{1,17},{17,1},{2,18},{18,2},{3,19},{19,3},{4,20},{20... | collective-permute-start | bytes 393224 | tf_op jit(solution)/shard_map/ppermute | solution.py:309
  5.2 1.7 %copy-start.5 = (s32[1,2048,32]{1,2,0:T(8,128)S(1)}, s32[1,2048,32]{1,2,0:T(8,128)}, u32[]{:S(2)}) copy-start(s32[1,2048,32]{1,2,0:T(8,128)} %param.8) | copy-start | bytes 786436
  6.1 5.1 %collective-permute-start = (s16[528,128]{1,0:T(8,128)(2,1)S(1)}, s16[528,128]{1,0:T(8,128)(2,1)S(1)}, u32[]{:S(2)}, u32[]{:S(2)}) collective-permute-start(s16[528,128]{1,0:T(8,128)(2,1)S(1)} %encode.1.msg_ref), channel_id=1, source_target_pairs={{0,16},{16,0},{1,17},{17,1},{2,18},{18,2},{3,19},{19,3},{4,20},{20... | collective-permute-start | bytes 405512 | tf_op jit(solution)/shard_map/ppermute | solution.py:316
  9.2 2.1 %copy-start.2 = (f32[2048,128]{1,0:T(8,128)S(1)}, f32[2048,128]{1,0:T(8,128)}, u32[]{:S(2)}) copy-start(f32[2048,128]{1,0:T(8,128)} %p_ref.1) | copy-start | bytes 3145732

commit v5 on v4

--- a/solution.py
+++ b/solution.py
@@ -134,25 +134,26 @@
     short_ref[...] = idx_ref[...].astype(jnp.int16)
 
 
-def order_kernel(idx_ref, picks_ref):
+def order_kernel(short_ref, picks_ref):
     length = picks_ref.shape[1]
+    numbers = short_ref[...].astype(jnp.int32)
     for c in range(picks_ref.shape[0] // length):
         picks_ref[c * length : (c + 1) * length] = jnp.concatenate(
             [
-                sorted_numbers(idx_ref[:, b * length : (b + 1) * length], length)
+                sorted_numbers(numbers[:, b * length : (b + 1) * length], length)
                 for b in range(c * GROUPS, (c + 1) * GROUPS)
             ],
             axis=0,
         )
 
 
-def encode_kernel(table_ref, picks_ref, m_ref, g_ref, msg_ref):
-    count, length = m_ref.shape
+def encode_kernel(chunks, table_ref, picks_ref, m_ref, g_ref, msg_ref):
+    length = m_ref.shape[1]
     keep = length // GROUPS
     spare = (length - keep) // SUB
     weights = weights_of(table_ref[...].T)
     scales = []
-    for c in range(count // (GROUPS * length)):
+    for i, c in enumerate(chunks):
         rows = slice(c * GROUPS * length, (c + 1) * GROUPS * length)
         mom = 0.999 * m_ref[rows] + g_ref[rows].astype(jnp.float32)
         coef = transform(mom, weights)
@@ -169,24 +170,23 @@
             power = jnp.ceil(jnp.log2(jnp.maximum(top, TINY)))
             scales.append(power)
             coded.append(jnp.round(part * (STEPS * jnp.exp2(-power))))
-        msg_ref[c * length : (c + 1) * length] = (
+        msg_ref[i * length : (i + 1) * length] = (
             jnp.concatenate(coded, axis=0).astype(jnp.int32).astype(jnp.int16)
         )
-    rows = msg_ref.shape[0] - count * keep // length
+    base = len(chunks) * length
+    rows = msg_ref.shape[0] - base
     if rows > len(scales):
         scales.append(jnp.zeros((rows - len(scales), length), jnp.float32))
-    msg_ref[msg_ref.shape[0] - rows :] = (
-        jnp.concatenate(scales, axis=0).astype(jnp.int32).astype(jnp.int16)
-    )
-
-
-def spread(msg_ref, ranks, c, base):
+    msg_ref[base:] = jnp.concatenate(scales, axis=0).astype(jnp.int32).astype(jnp.int16)
+
+
+def spread(msg_ref, ranks, i, base):
     length = msg_ref.shape[1]
     keep = length // GROUPS
     spare = (length - keep) // SUB
-    rows = msg_ref[c * length : (c + 1) * length].astype(jnp.int32).astype(jnp.float32)
+    rows = msg_ref[i * length : (i + 1) * length].astype(jnp.int32).astype(jnp.float32)
     tail = msg_ref[base:].astype(jnp.int32).astype(jnp.float32)
-    unit = jnp.exp2(tail[c * GROUPS : (c + 1) * GROUPS]) * (1.0 / STEPS)
+    unit = jnp.exp2(tail[i * GROUPS : (i + 1) * GROUPS]) * (1.0 / STEPS)
     out = []
     for g, rank in enumerate(ranks):
         values = rows[g * keep : (g + 1) * keep] * unit[g : g + 1]
@@ -202,47 +202,60 @@
     return jnp.concatenate(out, axis=0)
 
 
-def copy_out(held_ref, out_ref, sems, c):
-    size = held_ref.shape[0] // sems.shape[0]
-    rows = pl.ds(c * size, size)
-    return pltpu.make_async_copy(held_ref.at[rows], out_ref.at[rows], sems.at[c])
-
-
-def own_kernel(table_ref, idx_ref, msg_ref, m_ref, g_ref, new_ref, back_ref, held_ref, sems):
-    count, length = m_ref.shape
+def copy_out(held_ref, out_ref, sem, base, rows):
+    place = pl.ds(base + rows.start, rows.stop - rows.start)
+    return pltpu.make_async_copy(
+        held_ref.at[pl.ds(rows.start, rows.stop - rows.start)], out_ref.at[place], sem
+    )
+
+
+def own_kernel(parts, islands, table_ref, short_ref, m_ref, g_ref, *refs):
+    msgs, refs = refs[: len(parts)], refs[len(parts) :]
+    others, refs = refs[: islands - 1], refs[islands - 1 :]
+    new_ref, back_ref = refs[:2]
+    places = refs[2:]
+    length = m_ref.shape[1]
     size = GROUPS * length
-    base = count // GROUPS
     weights = weights_of(table_ref[...])
-    for c in range(count // size):
-        ranks = [
-            positions(idx_ref[:, b * length : (b + 1) * length], length)
-            for b in range(c * GROUPS, (c + 1) * GROUPS)
-        ]
-        rows = slice(c * size, (c + 1) * size)
-        back = transform(spread(msg_ref, ranks, c, base), weights)
-        back_ref[rows] = back
-        held_ref[rows] = 0.999 * m_ref[rows] + g_ref[rows].astype(jnp.float32) - back
-        copy_out(held_ref, new_ref, sems, c).start()
-    for c in range(sems.shape[0]):
-        copy_out(held_ref, new_ref, sems, c).wait()
-
-
-def positions_kernel(idx_ref, ranks_ref):
-    length, count = ranks_ref.shape
-    numbers = idx_ref[...].astype(jnp.int32)
-    for b in range(count // length):
-        lanes = slice(b * length, (b + 1) * length)
-        ranks_ref[:, lanes] = positions(numbers[:, lanes], length)
-
-
-def finish_kernel(islands, me_ref, table_ref, back_ref, p_ref, *refs):
-    out_ref, held_ref, sems = refs[-3:]
-    msgs, places = refs[: islands - 1], refs[islands - 1 : 2 * islands - 2]
-    count, length = p_ref.shape
+    numbers = short_ref[...].astype(jnp.int32)
+    for chunks, msg_ref in zip(parts, msgs):
+        for i, c in enumerate(chunks):
+            ranks = [
+                positions(numbers[:, b * length : (b + 1) * length], length)
+                for b in range(c * GROUPS, (c + 1) * GROUPS)
+            ]
+            rows = slice(c * size, (c + 1) * size)
+            back = transform(spread(msg_ref, ranks, i, len(chunks) * length), weights)
+            back_ref[rows] = back
+            new_ref[rows] = 0.999 * m_ref[rows] + g_ref[rows].astype(jnp.float32) - back
+    for other_ref, ranks_ref in zip(others, places):
+        numbers = other_ref[...].astype(jnp.int32)
+        for b in range(numbers.shape[1] // length):
+            lanes = slice(b * length, (b + 1) * length)
+            ranks_ref[:, lanes] = positions(numbers[:, lanes], length)
+
+
+def finish_kernel(parts, islands, me_ref, table_ref, back_ref, p_ref, *refs):
+    msgs, refs = refs[: islands - 1], refs[islands - 1 :]
+    places, refs = refs[: islands - 1], refs[islands - 1 :]
+    chunks = parts[-1]
+    length = p_ref.shape[1]
     size = GROUPS * length
-    base = count // GROUPS
+    last = chunks.stop * size == p_ref.shape[0]
+    first = chunks.start * size
+    copies = []
+    if last:
+        new_ref, *earlier, out_ref, new_out_ref, held_ref, sems = refs
+        copies.append(pltpu.make_async_copy(new_ref, new_out_ref, sems.at[sems.shape[0] - 1]))
+        copies[-1].start()
+        for i, (part, early_ref) in enumerate(zip(parts, earlier)):
+            rows = slice(0, early_ref.shape[0])
+            copies.append(copy_out(early_ref, out_ref, sems.at[i], part.start * size, rows))
+            copies[-1].start()
+    else:
+        (held_ref,) = refs
     weights = weights_of(table_ref[...])
-    for c in range(count // size):
+    for i, c in enumerate(chunks):
         rows = slice(c * size, (c + 1) * size)
         terms = [back_ref[rows]]
         for msg_ref, ranks_ref in zip(msgs, places):
@@ -250,7 +263,8 @@
                 ranks_ref[:, b * length : (b + 1) * length]
                 for b in range(c * GROUPS, (c + 1) * GROUPS)
             ]
-            terms.append(transform(spread(msg_ref, ranks, c, base), weights))
+            kept = spread(msg_ref, ranks, i, len(chunks) * length)
+            terms.append(transform(kept, weights))
         if islands == 2:
             total = terms[0] + terms[1]
         else:
@@ -261,23 +275,24 @@
                     origin = lax.rem(me_ref[0] + islands - away, islands)
                     term = jnp.where(origin == island, terms[away], term)
                 total = term if total is None else total + term
-        held_ref[rows] = (p_ref[rows] - total * (1.0 / islands)).astype(out_ref.dtype)
-        copy_out(held_ref, out_ref, sems, c).start()
-    for c in range(sems.shape[0]):
-        copy_out(held_ref, out_ref, sems, c).wait()
-
-
-def on_chip(kernel, out_shape, *args, name, flops=5 * 10**8, scalars=0, written=None):
+        done = slice(i * size, (i + 1) * size)
+        held_ref[done] = (p_ref[rows] - total * (1.0 / islands)).astype(held_ref.dtype)
+        if last:
+            sem = sems.at[len(parts) - 1 + i]
+            copies.append(copy_out(held_ref, out_ref, sem, first, done))
+            copies[-1].start()
+    for copy in copies:
+        copy.wait()
+
+
+def on_chip(kernel, out_shape, *args, name, flops=5 * 10**8, scalars=0, held=None, copies=0):
     vmem = pl.BlockSpec(memory_space=pltpu.VMEM)
     smem = pl.BlockSpec(memory_space=pltpu.SMEM)
     out_specs = [vmem] * len(out_shape)
     scratch = []
-    if written:
-        out_specs[0] = pl.BlockSpec(memory_space=pl.ANY)
-        scratch = [
-            pltpu.VMEM(out_shape[0].shape, out_shape[0].dtype),
-            pltpu.SemaphoreType.DMA((written,)),
-        ]
+    if copies:
+        out_specs = [pl.BlockSpec(memory_space=pl.ANY)] * len(out_shape)
+        scratch = [pltpu.VMEM(held.shape, held.dtype), pltpu.SemaphoreType.DMA((copies,))]
     return pl.pallas_call(
         kernel,
         in_specs=[smem] * scalars + [vmem] * (len(args) - scalars),
@@ -293,45 +308,58 @@
 def local(momentum, gradient, params, indices):
     islands = lax.axis_size("island")
     _, count, length = momentum.shape
-    keep = indices.shape[2]
     table = jnp.asarray(dct_table(length))
     numbers = indices[0].T
     chunks = count // (GROUPS * length)
+    parts = [part for part in (range(chunks - 1), range(chunks - 1, chunks)) if len(part)]
     rings = [
         [(i, (i + away) % islands) for i in range(islands)] for away in range(1, islands)
     ]
 
-    def array(rows, dtype):
-        return jax.ShapeDtypeStruct((rows, length), dtype)
-
-    short_shape = jax.ShapeDtypeStruct(numbers.shape, jnp.int16)
-    (short,) = on_chip(shorten_kernel, [short_shape], numbers, name="shorten", flops=5 * 10**9)
-    other_numbers = [lax.ppermute(short, "island", ring) for ring in rings]
-    (picks,) = on_chip(order_kernel, [array(chunks * length, jnp.int32)], numbers, name="order")
-    tail = -(-(count // length) // 16) * 16
-    packed = array(chunks * length + tail, jnp.int16)
-    (msg,) = on_chip(
-        encode_kernel, [packed], table, picks, momentum[0], gradient[0], name="encode"
-    )
-    other_msgs = [lax.ppermute(msg, "island", ring) for ring in rings]
+    def array(rows, dtype, lanes=length):
+        return jax.ShapeDtypeStruct((rows, lanes), dtype)
+
+    def to_others(x):
+        return [lax.ppermute(x, "island", ring) for ring in rings]
+
+    (short,) = on_chip(
+        shorten_kernel, [array(numbers.shape[0], jnp.int16, count)], numbers,
+        name="shorten", flops=5 * 10**9,
+    )
+    other_numbers = to_others(short)
+    (picks,) = on_chip(order_kernel, [array(chunks * length, jnp.int32)], short, name="order")
+    msgs = []
+    other_msgs = []
+    for part in parts:
+        tail = -(-(len(part) * GROUPS) // 16) * 16
+        (msg,) = on_chip(
+            functools.partial(encode_kernel, part),
+            [array(len(part) * length + tail, jnp.int16)],
+            table, picks, momentum[0], gradient[0],
+            name="encode",
+        )
+        msgs.append(msg)
+        other_msgs.append(to_others(msg))
     wide = array(count, jnp.float32)
-    new_momentum, back = on_chip(
-        own_kernel, [wide, wide], table, numbers, msg, momentum[0], gradient[0],
-        name="own", written=chunks,
-    )
-    places = [
-        on_chip(
-            positions_kernel, [jax.ShapeDtypeStruct((length, count), jnp.int32)], other,
-            name="positions",
-        )[0]
-        for other in other_numbers
-    ]
+    new, back, *places = on_chip(
+        functools.partial(own_kernel, parts, islands),
+        [wide, wide] + [array(length, jnp.int32, count)] * (islands - 1),
+        table, short, momentum[0], gradient[0], *msgs, *other_numbers,
+        name="own",
+    )
     me = lax.axis_index("island").astype(jnp.int32)[None]
-    (new_params,) = on_chip(
-        functools.partial(finish_kernel, islands),
-        [array(count, jnp.bfloat16)], me, table, back, params, *other_msgs, *places,
-        name="finish", scalars=1, written=chunks,
-    )
+    fresh = []
+    for i, (part, others) in enumerate(zip(parts, other_msgs)):
+        last = i == len(parts) - 1
+        mine = array(len(part) * GROUPS * length, jnp.bfloat16)
+        results = on_chip(
+            functools.partial(finish_kernel, parts[: i + 1], islands),
+            [array(count, jnp.bfloat16), wide] if last else [mine],
+            me, table, back, params, *others, *places, *([new] + fresh if last else []),
+            name="finish", scalars=1, held=mine, copies=(i + len(part) + 1) * last,
+        )
+        fresh.append(results[0])
+    new_params, new_momentum = results
     return new_momentum[None], new_params
 
 

time: 13 us -> 12.9 us (level)
  starting transfers between devices: 3.81 us -> 5.19 us
  waiting for transfers between devices: 1.6 us -> 0.45 us
  Pallas kernels: 5.75 us -> 5.46 us
    ppermute x2 -> x3, starting transfers between devices: 3.81 us -> 5.19 us  [to_others(): return [lax.ppermute(x, 'island', ring) for ring in rings]]
    ppermute x2 -> x3, waiting for transfers between devices: 1.6 us -> 0.45 us  [to_others(): return [lax.ppermute(x, 'island', ring) for ring in rings]]
    pallas_call x6 -> x7, Pallas kernels: 5.75 us -> 5.46 us  [on_chip(): pl.pallas_call(kernel, in_specs=[smem] * scalars + [vmem] * (len(args) -...]
    unnamed x12 -> x10, local copies, waits for them, and re-layouts: 0.98 us -> 0.97 us
  transfers between devices with their start and end apart: 2 -> 3, of which waited for: 1 -> 1; matrix products, arithmetic and copies ran while one was open for 0% -> 0% of each run, Pallas kernels for 32% -> 33%
where the time goes in v5:
time: 12.9 us; the launch traced here: 12.8 us
  Pallas kernels  5.46 us (42%)
  starting transfers between devices  5.19 us (40%)
  local copies, waits for them, and re-layouts  0.97 us (8%)
  between operations  0.73 us (6%)
  waiting for transfers between devices  0.45 us (3%)
    pallas_call x7, Pallas kernels, on_chip(): pl.pallas_call(kernel, in_specs=[smem] * scalars + [vmem] * (len(args) -...  5.46 us
    ppermute x3, starting transfers between devices, to_others(): return [lax.ppermute(x, 'island', ring) for ring in rings]  5.19 us
    unnamed x10, local copies, waits for them, and re-layouts  0.97 us
    ppermute x3, waiting for transfers between devices, to_others(): return [lax.ppermute(x, 'island', ring) for ring in rings]  0.45 us
  transfers between devices with their start and end apart: 3, of which 1 were waited for; matrix products, arithmetic and copies ran while one was open for 0% of the time, Pallas kernels for 33%

profile of v5, /device:TPU:0, one launch (start us, length us, event | category | flops | bytes accessed | tf_op | source)
XLA Modules:
  0.0 12.8 jit_solution(8638597260386288558)
XLA Ops:
  0.6 0.0 copy-start.4
  0.6 0.9 %copy-done.4 = s32[1,2048,32]{1,2,0:T(8,128)S(1)} copy-done((s32[1,2048,32]{1,2,0:T(8,128)S(1)}, s32[1,2048,32]{1,2,0:T(8,128)}, u32[]{:S(2)}) %copy-start.4) | copy-done | bytes 262168
  1.6 0.0 copy-start
  1.6 0.0 copy-start.1
  1.6 0.0 copy-start.3
  1.6 3.0 %collective-permute-start = (s16[32,2048]{1,0:T(8,128)(2,1)S(1)}, s16[32,2048]{1,0:T(8,128)(2,1)S(1)}, u32[]{:S(2)}, u32[]{:S(2)}) collective-permute-start(s16[32,2048]{1,0:T(8,128)(2,1)S(1)} %shorten.1.short_ref), channel_id=1, source_target_pairs={{0,16},{16,0},{1,17},{17,1},{2,18},{18,2},{3,19},{19,3},{4,20},{20... | collective-permute-start | bytes 393224 | tf_op jit(solution)/shard_map/ppermute | solution.py:323
  4.7 0.5 %order.1.picks_ref = s32[512,128]{1,0:T(8,128)S(1)} custom-call(s16[32,2048]{1,0:T(8,128)(2,1)S(1)} %shorten.1.short_ref), custom_call_target="tpu_custom_call" | custom-call | flops 500000000 | bytes 4194304 | tf_op jit(solution)/shard_map/order/pallas_call | solution.py:296
  5.2 0.0 copy-done
  5.2 0.0 copy-done.1
  5.2 0.0 copy-done.3
  5.2 0.7 %encode.2.refs_0_ = s16[400,128]{1,0:T(8,128)(2,1)S(1)} custom-call(f32[128,128]{1,0:T(8,128)S(1)} %copy-done.3, s32[512,128]{1,0:T(8,128)S(1)} %order.1.picks_ref, f32[2048,128]{1,0:T(8,128)S(1)} %bitcast.7, bf16[2048,128]{1,0:T(8,128)(2,1)S(1)} %bitcast.10), custom_call_target="tpu_custom_call" | custom-call | flops 500000000 | bytes 4194304 | tf_op jit(solution)/shard_map/encode/pallas_call | solution.py:296
  5.9 0.8 %collective-permute-start.2 = (s16[400,128]{1,0:T(8,128)(2,1)S(1)}, s16[400,128]{1,0:T(8,128)(2,1)S(1)}, u32[]{:S(2)}, u32[]{:S(2)}) collective-permute-start(s16[400,128]{1,0:T(8,128)(2,1)S(1)} %encode.2.refs_0_), channel_id=1, source_target_pairs={{0,16},{16,0},{1,17},{17,1},{2,18},{18,2},{3,19},{19,3},{4,20},{20... | collective-permute-start | bytes 307208 | tf_op jit(solution)/shard_map/ppermute | solution.py:323
  6.7 0.5 %encode.3.refs_1_ = s16[144,128]{1,0:T(8,128)(2,1)S(1)} custom-call(f32[128,128]{1,0:T(8,128)S(1)} %copy-done.3, s32[512,128]{1,0:T(8,128)S(1)} %order.1.picks_ref, f32[2048,128]{1,0:T(8,128)S(1)} %bitcast.8, bf16[2048,128]{1,0:T(8,128)(2,1)S(1)} %bitcast.11), custom_call_target="tpu_custom_call" | custom-call | flops 500000000 | bytes 4194304 | tf_op jit(solution)/shard_map/encode/pallas_call | solution.py:296
  7.2 0.0 copy-start.2
  7.2 1.4 %collective-permute-start.1 = (s16[144,128]{1,0:T(8,128)(2,1)S(1)}, s16[144,128]{1,0:T(8,128)(2,1)S(1)}, u32[]{:S(2)}, u32[]{:S(2)}) collective-permute-start(s16[144,128]{1,0:T(8,128)(2,1)S(1)} %encode.3.refs_1_), channel_id=1, source_target_pairs={{0,16},{16,0},{1,17},{17,1},{2,18},{18,2},{3,19},{19,3},{4,20},{20... | collective-permute-start | bytes 110600 | tf_op jit(solution)/shard_map/ppermute | solution.py:323
  8.6 0.0 collective-permute-done.refs_2_
  8.6 1.9 %own.1 = (f32[2048,128]{1,0:T(8,128)S(1)}, f32[2048,128]{1,0:T(8,128)S(1)}, s32[128,2048]{1,0:T(8,128)S(1)}) custom-call(f32[128,128]{1,0:T(8,128)S(1)} %copy-done.3, s16[32,2048]{1,0:T(8,128)(2,1)S(1)} %shorten.1.short_ref, f32[2048,128]{1,0:T(8,128)S(1)} %bitcast.9, bf16[2048,128]{1,0:T(8,128)(2,1)S(1)} %bitcast.12, s16[400,128]{1,0:T(8,128)(2,1)S(1)} %encode.2.refs_0_, ...), custom_call_target="tpu_custom_call" | custom-call | flops 500000000 | bytes 4194304 | tf_op jit(solution)/shard_map/own/pallas_call | solution.py:296
  10.4 0.4 %collective-permute-done.2.refs_0_ = s16[400,128]{1,0:T(8,128)(2,1)S(1)} collective-permute-done((s16[400,128]{1,0:T(8,128)(2,1)S(1)}, s16[400,128]{1,0:T(8,128)(2,1)S(1)}, u32[]{:S(2)}, u32[]{:S(2)}) %collective-permute-start.2) | collective-permute-done | bytes 102432 | tf_op jit(solution)/shard_map/ppermute | solution.py:323
  10.9 0.0 copy-done.2
  10.9 0.7 %finish.2.refs_3_ = bf16[1536,128]{1,0:T(8,128)(2,1)S(1)} custom-call(s32[1]{0:T(128)} %bitcast.me_ref, f32[128,128]{1,0:T(8,128)S(1)} %copy-done.3, f32[2048,128]{1,0:T(8,128)S(1)} %get-tuple-element.7.back_ref, f32[2048,128]{1,0:T(8,128)S(1)} %copy-done.2, s16[400,128]{1,0:T(8,128)(2,1)S(1)} %collective-permute-done.2.refs_0_, ...), custom_call_target="tpu_custom_call" | custom-call | flops 500000000 | bytes 4194304 | tf_op jit(solution)/shard_map/finish/pallas_call | solution.py:296
  11.6 0.0 collective-permute-done.1.refs_0_
  11.6 1.2 %finish.3 = (bf16[2048,128]{1,0:T(8,128)(2,1)}, f32[2048,128]{1,0:T(8,128)}) custom-call(s32[1]{0:T(128)} %bitcast.me_ref, f32[128,128]{1,0:T(8,128)S(1)} %copy-done.3, f32[2048,128]{1,0:T(8,128)S(1)} %get-tuple-element.7.back_ref, f32[2048,128]{1,0:T(8,128)S(1)} %copy-done.2, s16[144,128]{1,0:T(8,128)(2,1)S(1)} %collective-permute-done.1.refs_0_, ...), custom_call_target="tpu_custom_call" | custom-call | flops 500000000 | bytes 4194304 | tf_op jit(solution)/shard_map/finish/pallas_call | solution.py:296
  (1 shorter events, 0.0 us)
Async XLA Ops:
  0.6 1.0 %copy-start.4 = (s32[1,2048,32]{1,2,0:T(8,128)S(1)}, s32[1,2048,32]{1,2,0:T(8,128)}, u32[]{:S(2)}) copy-start(s32[1,2048,32]{1,2,0:T(8,128)} %param.8) | copy-start | bytes 786436
  1.6 3.6 %copy-start = (f32[1,2048,128]{2,1,0:T(8,128)S(1)}, f32[1,2048,128]{2,1,0:T(8,128)}, u32[]{:S(2)}) copy-start(f32[1,2048,128]{2,1,0:T(8,128)} %param.5) | copy-start | bytes 3145732
  1.6 3.6 %copy-start.1 = (bf16[1,2048,128]{2,1,0:T(8,128)(2,1)S(1)}, bf16[1,2048,128]{2,1,0:T(8,128)(2,1)}, u32[]{:S(2)}) copy-start(bf16[1,2048,128]{2,1,0:T(8,128)(2,1)} %param.6) | copy-start | bytes 1572868
  1.6 3.6 %copy-start.3 = (f32[128,128]{1,0:T(8,128)S(1)}, f32[128,128]{1,0:T(8,128)}, u32[]{:S(2)}) copy-start(f32[128,128]{1,0:T(8,128)} %constant.8.clone.table_ref) | copy-start | bytes 196612
  1.6 6.9 %collective-permute-start = (s16[32,2048]{1,0:T(8,128)(2,1)S(1)}, s16[32,2048]{1,0:T(8,128)(2,1)S(1)}, u32[]{:S(2)}, u32[]{:S(2)}) collective-permute-start(s16[32,2048]{1,0:T(8,128)(2,1)S(1)} %shorten.1.short_ref), channel_id=1, source_target_pairs={{0,16},{16,0},{1,17},{17,1},{2,18},{18,2},{3,19},{19,3},{4,20},{20... | collective-permute-start | bytes 393224 | tf_op jit(solution)/shard_map/ppermute | solution.py:323
  5.9 5.0 %collective-permute-start.2 = (s16[400,128]{1,0:T(8,128)(2,1)S(1)}, s16[400,128]{1,0:T(8,128)(2,1)S(1)}, u32[]{:S(2)}, u32[]{:S(2)}) collective-permute-start(s16[400,128]{1,0:T(8,128)(2,1)S(1)} %encode.2.refs_0_), channel_id=1, source_target_pairs={{0,16},{16,0},{1,17},{17,1},{2,18},{18,2},{3,19},{19,3},{4,20},{20... | collective-permute-start | bytes 307208 | tf_op jit(solution)/shard_map/ppermute | solution.py:323
  7.2 3.7 %copy-start.2 = (f32[2048,128]{1,0:T(8,128)S(1)}, f32[2048,128]{1,0:T(8,128)}, u32[]{:S(2)}) copy-start(f32[2048,128]{1,0:T(8,128)} %p_ref.3) | copy-start | bytes 3145732
  7.2 4.4 %collective-permute-start.1 = (s16[144,128]{1,0:T(8,128)(2,1)S(1)}, s16[144,128]{1,0:T(8,128)(2,1)S(1)}, u32[]{:S(2)}, u32[]{:S(2)}) collective-permute-start(s16[144,128]{1,0:T(8,128)(2,1)S(1)} %encode.3.refs_1_), channel_id=1, source_target_pairs={{0,16},{16,0},{1,17},{17,1},{2,18},{18,2},{3,19},{19,3},{4,20},{20... | collective-permute-start | bytes 110600 | tf_op jit(solution)/shard_map/ppermute | solution.py:323

commit v6 on v5

--- a/solution.py
+++ b/solution.py
@@ -1,8 +1,8 @@
 import functools
+import math
 
 import jax
 import jax.numpy as jnp
-import numpy as np
 from jax import lax
 from jax.experimental import pallas as pl
 from jax.experimental.pallas import tpu as pltpu
@@ -17,10 +17,16 @@
 
 
 def dct_table(length):
-    freq = np.arange(length, dtype=np.float64)[:, None]
-    place = np.arange(length, dtype=np.float64)[None, :]
-    scale = np.where(freq == 0, np.sqrt(1.0 / length), np.sqrt(2.0 / length))
-    return (scale * np.cos(np.pi * (place + 0.5) * freq / length)).astype(np.float32)
+    freq = lax.broadcasted_iota(jnp.int32, (length, length), 0)
+    place = lax.broadcasted_iota(jnp.int32, (length, length), 1)
+    turn = ((2 * place + 1) * freq) & (4 * length - 1)
+    x = (jnp.abs(turn - 2 * length) - length).astype(jnp.float32) * (math.pi / (2 * length))
+    square = x * x
+    series = jnp.full_like(x, 1.0 / math.factorial(15))
+    for n in range(13, 0, -2):
+        series = 1.0 / math.factorial(n) - square * series
+    scale = jnp.where(freq == 0, math.sqrt(1.0 / length), math.sqrt(2.0 / length))
+    return scale * (x * series)
 
 
 def two_parts(x):
@@ -130,13 +136,11 @@
     return next(iter(found.values()))
 
 
-def shorten_kernel(idx_ref, short_ref):
-    short_ref[...] = idx_ref[...].astype(jnp.int16)
-
-
-def order_kernel(short_ref, picks_ref):
+def prepare(numbers, picks_ref, forward_ref, inverse_ref):
     length = picks_ref.shape[1]
-    numbers = short_ref[...].astype(jnp.int32)
+    table = dct_table(length)
+    forward_ref[...] = weights_of(table.T)
+    inverse_ref[...] = weights_of(table)
     for c in range(picks_ref.shape[0] // length):
         picks_ref[c * length : (c + 1) * length] = jnp.concatenate(
             [
@@ -147,11 +151,25 @@
         )
 
 
-def encode_kernel(chunks, table_ref, picks_ref, m_ref, g_ref, msg_ref):
+def shorten_kernel(idx_ref, short_ref, *prepared):
+    short_ref[...] = idx_ref[...].astype(jnp.int16)
+
+    @pl.when(lax.axis_index("island") == 0)
+    def _():
+        prepare(idx_ref[...], *prepared)
+
+
+def order_kernel(short_ref, *refs):
+    @pl.when(lax.axis_index("island") != 0)
+    def _():
+        prepare(short_ref[...].astype(jnp.int32), *refs[len(refs) // 2 :])
+
+
+def encode_kernel(chunks, weights_ref, picks_ref, m_ref, g_ref, msg_ref):
     length = m_ref.shape[1]
     keep = length // GROUPS
     spare = (length - keep) // SUB
-    weights = weights_of(table_ref[...].T)
+    weights = weights_ref[...]
     scales = []
     for i, c in enumerate(chunks):
         rows = slice(c * GROUPS * length, (c + 1) * GROUPS * length)
@@ -209,14 +227,12 @@
     )
 
 
-def own_kernel(parts, islands, table_ref, short_ref, m_ref, g_ref, *refs):
+def own_kernel(parts, weights_ref, short_ref, m_ref, g_ref, *refs):
     msgs, refs = refs[: len(parts)], refs[len(parts) :]
-    others, refs = refs[: islands - 1], refs[islands - 1 :]
-    new_ref, back_ref = refs[:2]
-    places = refs[2:]
+    new_ref, back_ref = refs
     length = m_ref.shape[1]
     size = GROUPS * length
-    weights = weights_of(table_ref[...])
+    weights = weights_ref[...]
     numbers = short_ref[...].astype(jnp.int32)
     for chunks, msg_ref in zip(parts, msgs):
         for i, c in enumerate(chunks):
@@ -228,14 +244,22 @@
             back = transform(spread(msg_ref, ranks, i, len(chunks) * length), weights)
             back_ref[rows] = back
             new_ref[rows] = 0.999 * m_ref[rows] + g_ref[rows].astype(jnp.float32) - back
-    for other_ref, ranks_ref in zip(others, places):
-        numbers = other_ref[...].astype(jnp.int32)
-        for b in range(numbers.shape[1] // length):
+
+
+def positions_kernel(others, new_ref, *refs):
+    shorts, (new_out_ref, *places, sem) = refs[:others], refs[others:]
+    copy = pltpu.make_async_copy(new_ref, new_out_ref, sem.at[0])
+    copy.start()
+    for short_ref, ranks_ref in zip(shorts, places):
+        length, count = ranks_ref.shape
+        numbers = short_ref[...].astype(jnp.int32)
+        for b in range(count // length):
             lanes = slice(b * length, (b + 1) * length)
             ranks_ref[:, lanes] = positions(numbers[:, lanes], length)
-
-
-def finish_kernel(parts, islands, me_ref, table_ref, back_ref, p_ref, *refs):
+    copy.wait()
+
+
+def finish_kernel(parts, islands, me_ref, weights_ref, back_ref, p_ref, *refs):
     msgs, refs = refs[: islands - 1], refs[islands - 1 :]
     places, refs = refs[: islands - 1], refs[islands - 1 :]
     chunks = parts[-1]
@@ -245,16 +269,14 @@
     first = chunks.start * size
     copies = []
     if last:
-        new_ref, *earlier, out_ref, new_out_ref, held_ref, sems = refs
-        copies.append(pltpu.make_async_copy(new_ref, new_out_ref, sems.at[sems.shape[0] - 1]))
-        copies[-1].start()
+        *earlier, out_ref, held_ref, sems = refs
         for i, (part, early_ref) in enumerate(zip(parts, earlier)):
             rows = slice(0, early_ref.shape[0])
             copies.append(copy_out(early_ref, out_ref, sems.at[i], part.start * size, rows))
             copies[-1].start()
     else:
         (held_ref,) = refs
-    weights = weights_of(table_ref[...])
+    weights = weights_ref[...]
     for i, c in enumerate(chunks):
         rows = slice(c * size, (c + 1) * size)
         terms = [back_ref[rows]]
@@ -285,22 +307,26 @@
         copy.wait()
 
 
-def on_chip(kernel, out_shape, *args, name, flops=5 * 10**8, scalars=0, held=None, copies=0):
+def on_chip(
+    kernel, out_shape, *args, name, flops=5 * 10**8, scalars=0, held=None, copies=0, onto={}
+):
     vmem = pl.BlockSpec(memory_space=pltpu.VMEM)
     smem = pl.BlockSpec(memory_space=pltpu.SMEM)
     out_specs = [vmem] * len(out_shape)
     scratch = []
     if copies:
-        out_specs = [pl.BlockSpec(memory_space=pl.ANY)] * len(out_shape)
-        scratch = [pltpu.VMEM(held.shape, held.dtype), pltpu.SemaphoreType.DMA((copies,))]
+        out_specs[0] = pl.BlockSpec(memory_space=pl.ANY)
+        scratch = [] if held is None else [pltpu.VMEM(held.shape, held.dtype)]
+        scratch.append(pltpu.SemaphoreType.DMA((copies,)))
     return pl.pallas_call(
         kernel,
         in_specs=[smem] * scalars + [vmem] * (len(args) - scalars),
         out_specs=out_specs,
         out_shape=out_shape,
         scratch_shapes=scratch,
+        input_output_aliases=onto,
         compiler_params=pltpu.CompilerParams(vmem_limit_bytes=VMEM_LIMIT),
-        cost_estimate=pl.CostEstimate(flops=flops, bytes_accessed=4 * 2**20, transcendentals=0),
+        cost_estimate=pl.CostEstimate(flops=flops, bytes_accessed=flops // 128, transcendentals=0),
         name=name,
     )(*args)
 
@@ -308,7 +334,6 @@
 def local(momentum, gradient, params, indices):
     islands = lax.axis_size("island")
     _, count, length = momentum.shape
-    table = jnp.asarray(dct_table(length))
     numbers = indices[0].T
     chunks = count // (GROUPS * length)
     parts = [part for part in (range(chunks - 1), range(chunks - 1, chunks)) if len(part)]
@@ -322,12 +347,17 @@
     def to_others(x):
         return [lax.ppermute(x, "island", ring) for ring in rings]
 
-    (short,) = on_chip(
-        shorten_kernel, [array(numbers.shape[0], jnp.int16, count)], numbers,
+    weights = array(2 * length, jnp.bfloat16, 2 * length)
+    prepared = [array(chunks * length, jnp.int32), weights, weights]
+    short, *early = on_chip(
+        shorten_kernel, [array(numbers.shape[0], jnp.int16, count)] + prepared, numbers,
         name="shorten", flops=5 * 10**9,
     )
     other_numbers = to_others(short)
-    (picks,) = on_chip(order_kernel, [array(chunks * length, jnp.int32)], short, name="order")
+    picks, forward, inverse = on_chip(
+        order_kernel, prepared, short, *early,
+        name="order", flops=10**4, onto={1: 0, 2: 1, 3: 2},
+    )
     msgs = []
     other_msgs = []
     for part in parts:
@@ -335,32 +365,35 @@
         (msg,) = on_chip(
             functools.partial(encode_kernel, part),
             [array(len(part) * length + tail, jnp.int16)],
-            table, picks, momentum[0], gradient[0],
+            forward, picks, momentum[0], gradient[0],
             name="encode",
         )
         msgs.append(msg)
         other_msgs.append(to_others(msg))
     wide = array(count, jnp.float32)
-    new, back, *places = on_chip(
-        functools.partial(own_kernel, parts, islands),
-        [wide, wide] + [array(length, jnp.int32, count)] * (islands - 1),
-        table, short, momentum[0], gradient[0], *msgs, *other_numbers,
+    new, back = on_chip(
+        functools.partial(own_kernel, parts), [wide, wide],
+        inverse, short, momentum[0], gradient[0], *msgs,
         name="own",
+    )
+    new_momentum, *places = on_chip(
+        functools.partial(positions_kernel, islands - 1),
+        [wide] + [array(length, jnp.int32, count)] * (islands - 1), new, *other_numbers,
+        name="positions", copies=1,
     )
     me = lax.axis_index("island").astype(jnp.int32)[None]
     fresh = []
     for i, (part, others) in enumerate(zip(parts, other_msgs)):
         last = i == len(parts) - 1
         mine = array(len(part) * GROUPS * length, jnp.bfloat16)
-        results = on_chip(
+        (done,) = on_chip(
             functools.partial(finish_kernel, parts[: i + 1], islands),
-            [array(count, jnp.bfloat16), wide] if last else [mine],
-            me, table, back, params, *others, *places, *([new] + fresh if last else []),
-            name="finish", scalars=1, held=mine, copies=(i + len(part) + 1) * last,
+            [array(count, jnp.bfloat16) if last else mine],
+            me, inverse, back, params, *others, *places, *(fresh if last else []),
+            name="finish", scalars=1, held=mine, copies=(i + len(part)) * last,
         )
-        fresh.append(results[0])
-    new_params, new_momentum = results
-    return new_momentum[None], new_params
+        fresh.append(done)
+    return new_momentum[None], fresh[-1]
 
 
 def solution(mesh):

time: 12.9 us -> 12.8 us (level)
  starting transfers between devices: 5.19 us -> 4.57 us
  Pallas kernels: 5.46 us -> 5.79 us
    ppermute x3, starting transfers between devices: 5.19 us -> 4.57 us  [to_others(): return [lax.ppermute(x, 'island', ring) for ring in rings]]
    pallas_call x7 -> x8, Pallas kernels: 5.46 us -> 5.79 us  [on_chip(): pl.pallas_call(kernel, in_specs=[smem] * scalars + [vmem] * (len(args) -...]
    unnamed x10 -> x8, local copies, waits for them, and re-layouts: 0.97 us -> 1.06 us
where the time goes in v6:
time: 12.8 us; the launch traced here: 12.6 us
  Pallas kernels  5.79 us (45%)
  starting transfers between devices  4.57 us (36%)
  local copies, waits for them, and re-layouts  1.06 us (8%)
  between operations  0.7 us (5%)
  waiting for transfers between devices  0.5 us (4%)
    pallas_call x8, Pallas kernels, on_chip(): pl.pallas_call(kernel, in_specs=[smem] * scalars + [vmem] * (len(args) -...  5.79 us
    ppermute x3, starting transfers between devices, to_others(): return [lax.ppermute(x, 'island', ring) for ring in rings]  4.57 us
    unnamed x8, local copies, waits for them, and re-layouts  1.06 us
    ppermute x3, waiting for transfers between devices, to_others(): return [lax.ppermute(x, 'island', ring) for ring in rings]  0.5 us
  transfers between devices with their start and end apart: 3, of which 1 were waited for; matrix products, arithmetic and copies ran while one was open for 0% of the time, Pallas kernels for 33%

profile of v6, /device:TPU:0, one launch (start us, length us, event | category | flops | bytes accessed | tf_op | source)
XLA Modules:
  0.0 12.6 jit_solution(16842553369257963469)
XLA Ops:
  0.6 0.0 copy-start.3
  0.6 0.9 %copy-done.3 = s32[1,2048,32]{1,2,0:T(8,128)S(1)} copy-done((s32[1,2048,32]{1,2,0:T(8,128)S(1)}, s32[1,2048,32]{1,2,0:T(8,128)}, u32[]{:S(2)}) %copy-start.3) | copy-done | bytes 262168
  1.6 0.0 copy-start
  1.6 0.6 %shorten.1 = (s16[32,2048]{1,0:T(8,128)(2,1)S(1)}, s32[512,128]{1,0:T(8,128)S(1)}, bf16[256,256]{1,0:T(8,128)(2,1)S(1)}, bf16[256,256]{1,0:T(8,128)(2,1)S(1)}) custom-call(s32[32,2048]{1,0:T(8,128)S(1)} %bitcast.13), custom_call_target="tpu_custom_call" | custom-call | flops 5000000000 | bytes 39062500 | tf_op jit(solution)/shard_map/shorten/pallas_call | solution.py:321
  2.2 0.0 copy-start.1
  2.2 2.4 %collective-permute-start = (s16[32,2048]{1,0:T(8,128)(2,1)S(1)}, s16[32,2048]{1,0:T(8,128)(2,1)S(1)}, u32[]{:S(2)}, u32[]{:S(2)}) collective-permute-start(s16[32,2048]{1,0:T(8,128)(2,1)S(1)} %get-tuple-element.13.short_ref), channel_id=1, source_target_pairs={{0,16},{16,0},{1,17},{17,1},{2,18},{18,2},{3,19},{19,3},{4,20},{20... | collective-permute-start | bytes 393224 | tf_op jit(solution)/shard_map/ppermute | solution.py:348
  4.6 0.0 copy-done
  4.6 0.0 copy-done.1
  4.7 0.6 %encode.2.refs_0_ = s16[400,128]{1,0:T(8,128)(2,1)S(1)} custom-call(bf16[256,256]{1,0:T(8,128)(2,1)S(1)} %get-tuple-element.18.weights_ref, s32[512,128]{1,0:T(8,128)S(1)} %get-tuple-element.19.picks_ref, f32[2048,128]{1,0:T(8,128)S(1)} %bitcast.7, bf16[2048,128]{1,0:T(8,128)(2,1)S(1)} %bitcast.10), custom_call_target="tpu_custom_call" | custom-call | flops 500000000 | bytes 3906250 | tf_op jit(solution)/shard_map/encode/pallas_call | solution.py:321
  5.3 1.3 %collective-permute-start.2 = (s16[400,128]{1,0:T(8,128)(2,1)S(1)}, s16[400,128]{1,0:T(8,128)(2,1)S(1)}, u32[]{:S(2)}, u32[]{:S(2)}) collective-permute-start(s16[400,128]{1,0:T(8,128)(2,1)S(1)} %encode.2.refs_0_), channel_id=1, source_target_pairs={{0,16},{16,0},{1,17},{17,1},{2,18},{18,2},{3,19},{19,3},{4,20},{20... | collective-permute-start | bytes 307208 | tf_op jit(solution)/shard_map/ppermute | solution.py:348
  6.6 0.4 %encode.3.refs_1_ = s16[144,128]{1,0:T(8,128)(2,1)S(1)} custom-call(bf16[256,256]{1,0:T(8,128)(2,1)S(1)} %get-tuple-element.18.weights_ref, s32[512,128]{1,0:T(8,128)S(1)} %get-tuple-element.19.picks_ref, f32[2048,128]{1,0:T(8,128)S(1)} %bitcast.8, bf16[2048,128]{1,0:T(8,128)(2,1)S(1)} %bitcast.11), custom_call_target="tpu_custom_call" | custom-call | flops 500000000 | bytes 3906250 | tf_op jit(solution)/shard_map/encode/pallas_call | solution.py:321
  7.0 0.8 %collective-permute-start.1 = (s16[144,128]{1,0:T(8,128)(2,1)S(1)}, s16[144,128]{1,0:T(8,128)(2,1)S(1)}, u32[]{:S(2)}, u32[]{:S(2)}) collective-permute-start(s16[144,128]{1,0:T(8,128)(2,1)S(1)} %encode.3.refs_1_), channel_id=1, source_target_pairs={{0,16},{16,0},{1,17},{17,1},{2,18},{18,2},{3,19},{19,3},{4,20},{20... | collective-permute-start | bytes 110600 | tf_op jit(solution)/shard_map/ppermute | solution.py:348
  7.8 1.4 %own.1 = (f32[2048,128]{1,0:T(8,128)S(1)}, f32[2048,128]{1,0:T(8,128)S(1)}) custom-call(bf16[256,256]{1,0:T(8,128)(2,1)S(1)} %get-tuple-element.17.weights_ref, s16[32,2048]{1,0:T(8,128)(2,1)S(1)} %get-tuple-element.13.short_ref, f32[2048,128]{1,0:T(8,128)S(1)} %bitcast.9, bf16[2048,128]{1,0:T(8,128)(2,1)S(1)} %bitcast.12, ...), custom_call_target="tpu_custom_call" | custom-call | flops 500000000 | bytes 3906250 | tf_op jit(solution)/shard_map/own/pallas_call | solution.py:321
  9.2 0.0 copy-start.2
  9.2 0.0 collective-permute-done.refs_0_
  9.3 1.0 %positions.1 = (f32[2048,128]{1,0:T(8,128)}, s32[128,2048]{1,0:T(8,128)S(1)}) custom-call(f32[2048,128]{1,0:T(8,128)S(1)} %get-tuple-element.20.new_ref, s16[32,2048]{1,0:T(8,128)(2,1)S(1)} %collective-permute-done.refs_0_), custom_call_target="tpu_custom_call" | custom-call | flops 500000000 | bytes 3906250 | tf_op jit(solution)/shard_map/positions/pallas_call | solution.py:321
  10.2 0.5 %collective-permute-done.2.refs_0_ = s16[400,128]{1,0:T(8,128)(2,1)S(1)} collective-permute-done((s16[400,128]{1,0:T(8,128)(2,1)S(1)}, s16[400,128]{1,0:T(8,128)(2,1)S(1)}, u32[]{:S(2)}, u32[]{:S(2)}) %collective-permute-start.2) | collective-permute-done | bytes 102432 | tf_op jit(solution)/shard_map/ppermute | solution.py:348
  10.7 0.1 copy-done.2
  10.8 0.7 %finish.2.refs_2_ = bf16[1536,128]{1,0:T(8,128)(2,1)S(1)} custom-call(s32[1]{0:T(128)} %bitcast.5.me_ref, bf16[256,256]{1,0:T(8,128)(2,1)S(1)} %get-tuple-element.17.weights_ref, f32[2048,128]{1,0:T(8,128)S(1)} %get-tuple-element.22.back_ref, f32[2048,128]{1,0:T(8,128)S(1)} %copy-done.2, s16[400,128]{1,0:T(8,128)(2,1)S(1)} %collective-permute-done.2.refs_0_, ...), custom_call_target="tpu_custom_call" | custom-call | flops 500000000 | bytes 3906250 | tf_op jit(solution)/shard_map/finish/pallas_call | solution.py:321
  11.6 0.0 collective-permute-done.1.refs_0_
  11.6 1.0 %finish.3 = bf16[2048,128]{1,0:T(8,128)(2,1)} custom-call(s32[1]{0:T(128)} %bitcast.5.me_ref, bf16[256,256]{1,0:T(8,128)(2,1)S(1)} %get-tuple-element.17.weights_ref, f32[2048,128]{1,0:T(8,128)S(1)} %get-tuple-element.22.back_ref, f32[2048,128]{1,0:T(8,128)S(1)} %copy-done.2, s16[144,128]{1,0:T(8,128)(2,1)S(1)} %collective-permute-done.1.refs_0_, ...), custom_call_target="tpu_custom_call" | custom-call | flops 500000000 | bytes 3906250 | tf_op jit(solution)/shard_map/finish/pallas_call | solution.py:321
  (1 shorter events, 0.0 us)
Async XLA Ops:
  0.6 1.0 %copy-start.3 = (s32[1,2048,32]{1,2,0:T(8,128)S(1)}, s32[1,2048,32]{1,2,0:T(8,128)}, u32[]{:S(2)}) copy-start(s32[1,2048,32]{1,2,0:T(8,128)} %param.7) | copy-start | bytes 786436
  1.6 3.1 %copy-start = (f32[1,2048,128]{2,1,0:T(8,128)S(1)}, f32[1,2048,128]{2,1,0:T(8,128)}, u32[]{:S(2)}) copy-start(f32[1,2048,128]{2,1,0:T(8,128)} %param.4) | copy-start | bytes 3145732
  2.2 2.4 %copy-start.1 = (bf16[1,2048,128]{2,1,0:T(8,128)(2,1)S(1)}, bf16[1,2048,128]{2,1,0:T(8,128)(2,1)}, u32[]{:S(2)}) copy-start(bf16[1,2048,128]{2,1,0:T(8,128)(2,1)} %param.5) | copy-start | bytes 1572868
  2.2 7.0 %collective-permute-start = (s16[32,2048]{1,0:T(8,128)(2,1)S(1)}, s16[32,2048]{1,0:T(8,128)(2,1)S(1)}, u32[]{:S(2)}, u32[]{:S(2)}) collective-permute-start(s16[32,2048]{1,0:T(8,128)(2,1)S(1)} %get-tuple-element.13.short_ref), channel_id=1, source_target_pairs={{0,16},{16,0},{1,17},{17,1},{2,18},{18,2},{3,19},{19,3},{4,20},{20... | collective-permute-start | bytes 393224 | tf_op jit(solution)/shard_map/ppermute | solution.py:348
  5.3 5.5 %collective-permute-start.2 = (s16[400,128]{1,0:T(8,128)(2,1)S(1)}, s16[400,128]{1,0:T(8,128)(2,1)S(1)}, u32[]{:S(2)}, u32[]{:S(2)}) collective-permute-start(s16[400,128]{1,0:T(8,128)(2,1)S(1)} %encode.2.refs_0_), channel_id=1, source_target_pairs={{0,16},{16,0},{1,17},{17,1},{2,18},{18,2},{3,19},{19,3},{4,20},{20... | collective-permute-start | bytes 307208 | tf_op jit(solution)/shard_map/ppermute | solution.py:348
  7.0 4.6 %collective-permute-start.1 = (s16[144,128]{1,0:T(8,128)(2,1)S(1)}, s16[144,128]{1,0:T(8,128)(2,1)S(1)}, u32[]{:S(2)}, u32[]{:S(2)}) collective-permute-start(s16[144,128]{1,0:T(8,128)(2,1)S(1)} %encode.3.refs_1_), channel_id=1, source_target_pairs={{0,16},{16,0},{1,17},{17,1},{2,18},{18,2},{3,19},{19,3},{4,20},{20... | collective-permute-start | bytes 110600 | tf_op jit(solution)/shard_map/ppermute | solution.py:348
  9.2 1.6 %copy-start.2 = (f32[2048,128]{1,0:T(8,128)S(1)}, f32[2048,128]{1,0:T(8,128)}, u32[]{:S(2)}) copy-start(f32[2048,128]{1,0:T(8,128)} %p_ref.3) | copy-start | bytes 3145732

commit v7 on v6

--- a/solution.py
+++ b/solution.py
@@ -227,7 +227,8 @@
     )
 
 
-def own_kernel(parts, weights_ref, short_ref, m_ref, g_ref, *refs):
+def own_kernel(parts, weights_ref, short_ref, m_ref, g_ref, p_ref, *refs):
+    del p_ref
     msgs, refs = refs[: len(parts)], refs[len(parts) :]
     new_ref, back_ref = refs
     length = m_ref.shape[1]
@@ -259,7 +260,7 @@
     copy.wait()
 
 
-def finish_kernel(parts, islands, me_ref, weights_ref, back_ref, p_ref, *refs):
+def finish_kernel(parts, islands, weights_ref, back_ref, p_ref, *refs):
     msgs, refs = refs[: islands - 1], refs[islands - 1 :]
     places, refs = refs[: islands - 1], refs[islands - 1 :]
     chunks = parts[-1]
@@ -294,7 +295,7 @@
             for island in range(islands):
                 term = terms[0]
                 for away in range(1, islands):
-                    origin = lax.rem(me_ref[0] + islands - away, islands)
+                    origin = lax.rem(lax.axis_index("island") + islands - away, islands)
                     term = jnp.where(origin == island, terms[away], term)
                 total = term if total is None else total + term
         done = slice(i * size, (i + 1) * size)
@@ -308,10 +309,9 @@
 
 
 def on_chip(
-    kernel, out_shape, *args, name, flops=5 * 10**8, scalars=0, held=None, copies=0, onto={}
+    kernel, out_shape, *args, name, flops=5 * 10**8, held=None, copies=0, onto={}
 ):
     vmem = pl.BlockSpec(memory_space=pltpu.VMEM)
-    smem = pl.BlockSpec(memory_space=pltpu.SMEM)
     out_specs = [vmem] * len(out_shape)
     scratch = []
     if copies:
@@ -320,7 +320,7 @@
         scratch.append(pltpu.SemaphoreType.DMA((copies,)))
     return pl.pallas_call(
         kernel,
-        in_specs=[smem] * scalars + [vmem] * (len(args) - scalars),
+        in_specs=[vmem] * len(args),
         out_specs=out_specs,
         out_shape=out_shape,
         scratch_shapes=scratch,
@@ -336,7 +336,7 @@
     _, count, length = momentum.shape
     numbers = indices[0].T
     chunks = count // (GROUPS * length)
-    parts = [part for part in (range(chunks - 1), range(chunks - 1, chunks)) if len(part)]
+    parts = [part for part in (range(chunks - 2), range(chunks - 2, chunks)) if len(part)]
     rings = [
         [(i, (i + away) % islands) for i in range(islands)] for away in range(1, islands)
     ]
@@ -373,7 +373,7 @@
     wide = array(count, jnp.float32)
     new, back = on_chip(
         functools.partial(own_kernel, parts), [wide, wide],
-        inverse, short, momentum[0], gradient[0], *msgs,
+        inverse, short, momentum[0], gradient[0], params, *msgs,
         name="own",
     )
     new_momentum, *places = on_chip(
@@ -381,7 +381,6 @@
         [wide] + [array(length, jnp.int32, count)] * (islands - 1), new, *other_numbers,
         name="positions", copies=1,
     )
-    me = lax.axis_index("island").astype(jnp.int32)[None]
     fresh = []
     for i, (part, others) in enumerate(zip(parts, other_msgs)):
         last = i == len(parts) - 1
@@ -389,8 +388,8 @@
         (done,) = on_chip(
             functools.partial(finish_kernel, parts[: i + 1], islands),
             [array(count, jnp.bfloat16) if last else mine],
-            me, inverse, back, params, *others, *places, *(fresh if last else []),
-            name="finish", scalars=1, held=mine, copies=(i + len(part)) * last,
+            inverse, back, params, *others, *places, *(fresh if last else []),
+            name="finish", held=mine, copies=(i + len(part)) * last,
         )
         fresh.append(done)
     return new_momentum[None], fresh[-1]

time: 12.8 us -> 12.8 us (level)
  transfers between devices with their start and end apart: 3 -> 3, of which waited for: 1 -> 1; matrix products, arithmetic and copies ran while one was open for 0% -> 0% of each run, Pallas kernels for 33% -> 31%
where the time goes in v7:
time: 12.8 us; the launch traced here: 12.6 us
  Pallas kernels  5.84 us (46%)
  starting transfers between devices  4.57 us (36%)
  local copies, waits for them, and re-layouts  0.96 us (8%)
  between operations  0.7 us (5%)
  waiting for transfers between devices  0.55 us (4%)
    pallas_call x8, Pallas kernels, on_chip(): pl.pallas_call(kernel, in_specs=[vmem] * len(args), out_specs=out_specs,...  5.84 us
    ppermute x3, starting transfers between devices, to_others(): return [lax.ppermute(x, 'island', ring) for ring in rings]  4.57 us
    unnamed x8, local copies, waits for them, and re-layouts  0.96 us
    ppermute x3, waiting for transfers between devices, to_others(): return [lax.ppermute(x, 'island', ring) for ring in rings]  0.55 us
  transfers between devices with their start and end apart: 3, of which 1 were waited for; matrix products, arithmetic and copies ran while one was open for 0% of the time, Pallas kernels for 31%

profile of v7, /device:TPU:0, one launch (start us, length us, event | category | flops | bytes accessed | tf_op | source)
XLA Modules:
  0.0 12.6 jit_solution(14976678662843981711)
XLA Ops:
  0.6 0.0 copy-start.3
  0.6 0.9 %copy-done.3 = s32[1,2048,32]{1,2,0:T(8,128)S(1)} copy-done((s32[1,2048,32]{1,2,0:T(8,128)S(1)}, s32[1,2048,32]{1,2,0:T(8,128)}, u32[]{:S(2)}) %copy-start.3) | copy-done | bytes 262168
  1.6 0.0 copy-start
  1.6 0.6 %shorten.1 = (s16[32,2048]{1,0:T(8,128)(2,1)S(1)}, s32[512,128]{1,0:T(8,128)S(1)}, bf16[256,256]{1,0:T(8,128)(2,1)S(1)}, bf16[256,256]{1,0:T(8,128)(2,1)S(1)}) custom-call(s32[32,2048]{1,0:T(8,128)S(1)} %bitcast.12), custom_call_target="tpu_custom_call" | custom-call | flops 5000000000 | bytes 39062500 | tf_op jit(solution)/shard_map/shorten/pallas_call | solution.py:321
  2.2 0.0 copy-start.2
  2.2 2.4 %collective-permute-start = (s16[32,2048]{1,0:T(8,128)(2,1)S(1)}, s16[32,2048]{1,0:T(8,128)(2,1)S(1)}, u32[]{:S(2)}, u32[]{:S(2)}) collective-permute-start(s16[32,2048]{1,0:T(8,128)(2,1)S(1)} %get-tuple-element.13.short_ref), channel_id=1, source_target_pairs={{0,16},{16,0},{1,17},{17,1},{2,18},{18,2},{3,19},{19,3},{4,20},{20... | collective-permute-start | bytes 393224 | tf_op jit(solution)/shard_map/ppermute | solution.py:348
  4.6 0.0 copy-done
  4.6 0.0 copy-done.2
  4.7 0.5 %encode.2.refs_0_ = s16[272,128]{1,0:T(8,128)(2,1)S(1)} custom-call(bf16[256,256]{1,0:T(8,128)(2,1)S(1)} %get-tuple-element.18.weights_ref, s32[512,128]{1,0:T(8,128)S(1)} %get-tuple-element.19.picks_ref, f32[2048,128]{1,0:T(8,128)S(1)} %bitcast.6, bf16[2048,128]{1,0:T(8,128)(2,1)S(1)} %bitcast.9), custom_call_target="tpu_custom_call" | custom-call | flops 500000000 | bytes 3906250 | tf_op jit(solution)/shard_map/encode/pallas_call | solution.py:321
  5.2 0.0 copy-start.1
  5.2 1.3 %collective-permute-start.2 = (s16[272,128]{1,0:T(8,128)(2,1)S(1)}, s16[272,128]{1,0:T(8,128)(2,1)S(1)}, u32[]{:S(2)}, u32[]{:S(2)}) collective-permute-start(s16[272,128]{1,0:T(8,128)(2,1)S(1)} %encode.2.refs_0_), channel_id=1, source_target_pairs={{0,16},{16,0},{1,17},{17,1},{2,18},{18,2},{3,19},{19,3},{4,20},{20... | collective-permute-start | bytes 208904 | tf_op jit(solution)/shard_map/ppermute | solution.py:348
  6.5 0.5 %encode.3.refs_1_ = s16[272,128]{1,0:T(8,128)(2,1)S(1)} custom-call(bf16[256,256]{1,0:T(8,128)(2,1)S(1)} %get-tuple-element.18.weights_ref, s32[512,128]{1,0:T(8,128)S(1)} %get-tuple-element.19.picks_ref, f32[2048,128]{1,0:T(8,128)S(1)} %bitcast.7, bf16[2048,128]{1,0:T(8,128)(2,1)S(1)} %bitcast.10), custom_call_target="tpu_custom_call" | custom-call | flops 500000000 | bytes 3906250 | tf_op jit(solution)/shard_map/encode/pallas_call | solution.py:321
  7.0 0.8 %collective-permute-start.1 = (s16[272,128]{1,0:T(8,128)(2,1)S(1)}, s16[272,128]{1,0:T(8,128)(2,1)S(1)}, u32[]{:S(2)}, u32[]{:S(2)}) collective-permute-start(s16[272,128]{1,0:T(8,128)(2,1)S(1)} %encode.3.refs_1_), channel_id=1, source_target_pairs={{0,16},{16,0},{1,17},{17,1},{2,18},{18,2},{3,19},{19,3},{4,20},{20... | collective-permute-start | bytes 208904 | tf_op jit(solution)/shard_map/ppermute | solution.py:348
  7.8 0.0 copy-done.1
  7.8 1.4 %own.1 = (f32[2048,128]{1,0:T(8,128)S(1)}, f32[2048,128]{1,0:T(8,128)S(1)}) custom-call(bf16[256,256]{1,0:T(8,128)(2,1)S(1)} %get-tuple-element.17.weights_ref, s16[32,2048]{1,0:T(8,128)(2,1)S(1)} %get-tuple-element.13.short_ref, f32[2048,128]{1,0:T(8,128)S(1)} %bitcast.8, bf16[2048,128]{1,0:T(8,128)(2,1)S(1)} %bitcast.11, f32[2048,128]{1,0:T(8,128)S(1)} %copy-done.1, ...), custom_call_target="tpu_custom_call" | custom-call | flops 500000000 | bytes 3906250 | tf_op jit(solution)/shard_map/own/pallas_call | solution.py:321
  9.3 0.0 collective-permute-done.refs_0_
  9.3 1.0 %positions.1 = (f32[2048,128]{1,0:T(8,128)}, s32[128,2048]{1,0:T(8,128)S(1)}) custom-call(f32[2048,128]{1,0:T(8,128)S(1)} %get-tuple-element.20.new_ref, s16[32,2048]{1,0:T(8,128)(2,1)S(1)} %collective-permute-done.refs_0_), custom_call_target="tpu_custom_call" | custom-call | flops 500000000 | bytes 3906250 | tf_op jit(solution)/shard_map/positions/pallas_call | solution.py:321
  10.3 0.0 collective-permute-done.2.refs_0_
  10.3 0.5 %finish.2.refs_2_ = bf16[1024,128]{1,0:T(8,128)(2,1)S(1)} custom-call(bf16[256,256]{1,0:T(8,128)(2,1)S(1)} %get-tuple-element.17.weights_ref, f32[2048,128]{1,0:T(8,128)S(1)} %get-tuple-element.22.back_ref, f32[2048,128]{1,0:T(8,128)S(1)} %copy-done.1, s16[272,128]{1,0:T(8,128)(2,1)S(1)} %collective-permute-done.2.refs_0_, ...), custom_call_target="tpu_custom_call" | custom-call | flops 500000000 | bytes 3906250 | tf_op jit(solution)/shard_map/finish/pallas_call | solution.py:321
  10.8 0.5 %collective-permute-done.1.refs_0_ = s16[272,128]{1,0:T(8,128)(2,1)S(1)} collective-permute-done((s16[272,128]{1,0:T(8,128)(2,1)S(1)}, s16[272,128]{1,0:T(8,128)(2,1)S(1)}, u32[]{:S(2)}, u32[]{:S(2)}) %collective-permute-start.1) | collective-permute-done | bytes 69664 | tf_op jit(solution)/shard_map/ppermute | solution.py:348
  11.4 1.2 %finish.3 = bf16[2048,128]{1,0:T(8,128)(2,1)} custom-call(bf16[256,256]{1,0:T(8,128)(2,1)S(1)} %get-tuple-element.17.weights_ref, f32[2048,128]{1,0:T(8,128)S(1)} %get-tuple-element.22.back_ref, f32[2048,128]{1,0:T(8,128)S(1)} %copy-done.1, s16[272,128]{1,0:T(8,128)(2,1)S(1)} %collective-permute-done.1.refs_0_, s32[128,2048]{1,0:T(8,128)S(1)} %get-tuple-element.23.refs_1_, ...), custom_call_target="tpu_custom_call" | custom-call | flops 500000000 | bytes 3906250 | tf_op jit(solution)/shard_map/finish/pallas_call | solution.py:321
  (1 shorter events, 0.0 us)
Async XLA Ops:
  0.6 1.0 %copy-start.3 = (s32[1,2048,32]{1,2,0:T(8,128)S(1)}, s32[1,2048,32]{1,2,0:T(8,128)}, u32[]{:S(2)}) copy-start(s32[1,2048,32]{1,2,0:T(8,128)} %param.7) | copy-start | bytes 786436
  1.6 3.1 %copy-start = (f32[1,2048,128]{2,1,0:T(8,128)S(1)}, f32[1,2048,128]{2,1,0:T(8,128)}, u32[]{:S(2)}) copy-start(f32[1,2048,128]{2,1,0:T(8,128)} %param.4) | copy-start | bytes 3145732
  2.2 2.4 %copy-start.2 = (bf16[1,2048,128]{2,1,0:T(8,128)(2,1)S(1)}, bf16[1,2048,128]{2,1,0:T(8,128)(2,1)}, u32[]{:S(2)}) copy-start(bf16[1,2048,128]{2,1,0:T(8,128)(2,1)} %param.5) | copy-start | bytes 1572868
  2.2 7.1 %collective-permute-start = (s16[32,2048]{1,0:T(8,128)(2,1)S(1)}, s16[32,2048]{1,0:T(8,128)(2,1)S(1)}, u32[]{:S(2)}, u32[]{:S(2)}) collective-permute-start(s16[32,2048]{1,0:T(8,128)(2,1)S(1)} %get-tuple-element.13.short_ref), channel_id=1, source_target_pairs={{0,16},{16,0},{1,17},{17,1},{2,18},{18,2},{3,19},{19,3},{4,20},{20... | collective-permute-start | bytes 393224 | tf_op jit(solution)/shard_map/ppermute | solution.py:348
  5.2 2.7 %copy-start.1 = (f32[2048,128]{1,0:T(8,128)S(1)}, f32[2048,128]{1,0:T(8,128)}, u32[]{:S(2)}) copy-start(f32[2048,128]{1,0:T(8,128)} %p_ref.5) | copy-start | bytes 3145732
  5.2 5.1 %collective-permute-start.2 = (s16[272,128]{1,0:T(8,128)(2,1)S(1)}, s16[272,128]{1,0:T(8,128)(2,1)S(1)}, u32[]{:S(2)}, u32[]{:S(2)}) collective-permute-start(s16[272,128]{1,0:T(8,128)(2,1)S(1)} %encode.2.refs_0_), channel_id=1, source_target_pairs={{0,16},{16,0},{1,17},{17,1},{2,18},{18,2},{3,19},{19,3},{4,20},{20... | collective-permute-start | bytes 208904 | tf_op jit(solution)/shard_map/ppermute | solution.py:348
  7.0 4.4 %collective-permute-start.1 = (s16[272,128]{1,0:T(8,128)(2,1)S(1)}, s16[272,128]{1,0:T(8,128)(2,1)S(1)}, u32[]{:S(2)}, u32[]{:S(2)}) collective-permute-start(s16[272,128]{1,0:T(8,128)(2,1)S(1)} %encode.3.refs_1_), channel_id=1, source_target_pairs={{0,16},{16,0},{1,17},{17,1},{2,18},{18,2},{3,19},{19,3},{4,20},{20... | collective-permute-start | bytes 208904 | tf_op jit(solution)/shard_map/ppermute | solution.py:348

commit v8 on v7

--- a/solution.py
+++ b/solution.py
@@ -165,37 +165,40 @@
         prepare(short_ref[...].astype(jnp.int32), *refs[len(refs) // 2 :])
 
 
-def encode_kernel(chunks, weights_ref, picks_ref, m_ref, g_ref, msg_ref):
+def encode_kernel(parts, weights_ref, picks_ref, m_ref, g_ref, *msgs):
     length = m_ref.shape[1]
     keep = length // GROUPS
     spare = (length - keep) // SUB
     weights = weights_ref[...]
-    scales = []
-    for i, c in enumerate(chunks):
-        rows = slice(c * GROUPS * length, (c + 1) * GROUPS * length)
-        mom = 0.999 * m_ref[rows] + g_ref[rows].astype(jnp.float32)
-        coef = transform(mom, weights)
-        coded = []
-        for g in range(GROUPS):
-            turned = coef[g * length : (g + 1) * length].T
-            values = []
-            for v in range(keep // SUB):
-                at = c * length + g * keep + v * SUB
-                pieces = {p: turned[p * SUB : (p + 1) * SUB] for p in range(v, v + spare + 1)}
-                values.append(choose(pieces, picks_ref[at : at + SUB]))
-            part = jnp.concatenate(values, axis=0)
-            top = jnp.max(jnp.abs(part), axis=0, keepdims=True)
-            power = jnp.ceil(jnp.log2(jnp.maximum(top, TINY)))
-            scales.append(power)
-            coded.append(jnp.round(part * (STEPS * jnp.exp2(-power))))
-        msg_ref[i * length : (i + 1) * length] = (
-            jnp.concatenate(coded, axis=0).astype(jnp.int32).astype(jnp.int16)
-        )
-    base = len(chunks) * length
-    rows = msg_ref.shape[0] - base
-    if rows > len(scales):
-        scales.append(jnp.zeros((rows - len(scales), length), jnp.float32))
-    msg_ref[base:] = jnp.concatenate(scales, axis=0).astype(jnp.int32).astype(jnp.int16)
+    for chunks, msg_ref in zip(parts, msgs):
+        scales = []
+        for i, c in enumerate(chunks):
+            rows = slice(c * GROUPS * length, (c + 1) * GROUPS * length)
+            mom = 0.999 * m_ref[rows] + g_ref[rows].astype(jnp.float32)
+            coef = transform(mom, weights)
+            coded = []
+            for g in range(GROUPS):
+                turned = coef[g * length : (g + 1) * length].T
+                values = []
+                for v in range(keep // SUB):
+                    at = c * length + g * keep + v * SUB
+                    pieces = {
+                        p: turned[p * SUB : (p + 1) * SUB] for p in range(v, v + spare + 1)
+                    }
+                    values.append(choose(pieces, picks_ref[at : at + SUB]))
+                part = jnp.concatenate(values, axis=0)
+                top = jnp.max(jnp.abs(part), axis=0, keepdims=True)
+                power = jnp.ceil(jnp.log2(jnp.maximum(top, TINY)))
+                scales.append(power)
+                coded.append(jnp.round(part * (STEPS * jnp.exp2(-power))))
+            msg_ref[i * length : (i + 1) * length] = (
+                jnp.concatenate(coded, axis=0).astype(jnp.int32).astype(jnp.int16)
+            )
+        base = len(chunks) * length
+        rows = msg_ref.shape[0] - base
+        if rows > len(scales):
+            scales.append(jnp.zeros((rows - len(scales), length), jnp.float32))
+        msg_ref[base:] = jnp.concatenate(scales, axis=0).astype(jnp.int32).astype(jnp.int16)
 
 
 def spread(msg_ref, ranks, i, base):
@@ -358,18 +361,14 @@
         order_kernel, prepared, short, *early,
         name="order", flops=10**4, onto={1: 0, 2: 1, 3: 2},
     )
-    msgs = []
-    other_msgs = []
-    for part in parts:
-        tail = -(-(len(part) * GROUPS) // 16) * 16
-        (msg,) = on_chip(
-            functools.partial(encode_kernel, part),
-            [array(len(part) * length + tail, jnp.int16)],
-            forward, picks, momentum[0], gradient[0],
-            name="encode",
-        )
-        msgs.append(msg)
-        other_msgs.append(to_others(msg))
+    tails = [-(-(len(part) * GROUPS) // 16) * 16 for part in parts]
+    msgs = on_chip(
+        functools.partial(encode_kernel, parts),
+        [array(len(part) * length + tail, jnp.int16) for part, tail in zip(parts, tails)],
+        forward, picks, momentum[0], gradient[0],
+        name="encode",
+    )
+    other_msgs = [to_others(msg) for msg in msgs]
     wide = array(count, jnp.float32)
     new, back = on_chip(
         functools.partial(own_kernel, parts), [wide, wide],

time: 12.8 us -> 12.6 us (0.984)
  Pallas kernels: 5.84 us -> 5.63 us
    pallas_call x8 -> x7, Pallas kernels: 5.84 us -> 5.63 us  [on_chip(): pl.pallas_call(kernel, in_specs=[vmem] * len(args), out_specs=out_specs,...]
  transfers between devices with their start and end apart: 3 -> 3, of which waited for: 1 -> 2; matrix products, arithmetic and copies ran while one was open for 0% -> 0% of each run, Pallas kernels for 31% -> 30%
where the time goes in v8:
time: 12.6 us; the launch traced here: 12.4 us
  Pallas kernels  5.63 us (45%)
  starting transfers between devices  4.51 us (36%)
  local copies, waits for them, and re-layouts  0.96 us (8%)
  between operations  0.69 us (5%)
  waiting for transfers between devices  0.63 us (5%)
    pallas_call x7, Pallas kernels, on_chip(): pl.pallas_call(kernel, in_specs=[vmem] * len(args), out_specs=out_specs,...  5.63 us
    ppermute x3, starting transfers between devices, to_others(): return [lax.ppermute(x, 'island', ring) for ring in rings]  4.51 us
    unnamed x8, local copies, waits for them, and re-layouts  0.96 us
    ppermute x3, waiting for transfers between devices, to_others(): return [lax.ppermute(x, 'island', ring) for ring in rings]  0.63 us
  transfers between devices with their start and end apart: 3, of which 2 were waited for; matrix products, arithmetic and copies ran while one was open for 0% of the time, Pallas kernels for 30%

profile of v8, /device:TPU:0, one launch (start us, length us, event | category | flops | bytes accessed | tf_op | source)
XLA Modules:
  0.0 12.4 jit_solution(7893064518034060322)
XLA Ops:
  0.6 0.0 copy-start.3
  0.6 0.9 %copy-done.3 = s32[1,2048,32]{1,2,0:T(8,128)S(1)} copy-done((s32[1,2048,32]{1,2,0:T(8,128)S(1)}, s32[1,2048,32]{1,2,0:T(8,128)}, u32[]{:S(2)}) %copy-start.3) | copy-done | bytes 262168
  1.6 0.0 copy-start.1
  1.6 0.6 %shorten.1 = (s16[32,2048]{1,0:T(8,128)(2,1)S(1)}, s32[512,128]{1,0:T(8,128)S(1)}, bf16[256,256]{1,0:T(8,128)(2,1)S(1)}, bf16[256,256]{1,0:T(8,128)(2,1)S(1)}) custom-call(s32[32,2048]{1,0:T(8,128)S(1)} %bitcast.10), custom_call_target="tpu_custom_call" | custom-call | flops 5000000000 | bytes 39062500 | tf_op jit(solution)/shard_map/shorten/pallas_call | solution.py:324
  2.2 0.0 copy-start.2
  2.2 2.4 %collective-permute-start = (s16[32,2048]{1,0:T(8,128)(2,1)S(1)}, s16[32,2048]{1,0:T(8,128)(2,1)S(1)}, u32[]{:S(2)}, u32[]{:S(2)}) collective-permute-start(s16[32,2048]{1,0:T(8,128)(2,1)S(1)} %get-tuple-element.15.short_ref), channel_id=1, source_target_pairs={{0,16},{16,0},{1,17},{17,1},{2,18},{18,2},{3,19},{19,3},{4,20},{20... | collective-permute-start | bytes 393224 | tf_op jit(solution)/shard_map/ppermute | solution.py:351
  4.6 0.0 copy-start
  4.6 0.0 copy-done.1
  4.7 0.0 copy-done.2
  4.7 0.8 %encode.1 = (s16[272,128]{1,0:T(8,128)(2,1)S(1)}, s16[272,128]{1,0:T(8,128)(2,1)S(1)}) custom-call(bf16[256,256]{1,0:T(8,128)(2,1)S(1)} %get-tuple-element.20.weights_ref, s32[512,128]{1,0:T(8,128)S(1)} %get-tuple-element.21.picks_ref, f32[2048,128]{1,0:T(8,128)S(1)} %bitcast.6, bf16[2048,128]{1,0:T(8,128)(2,1)S(1)} %bitcast.8), custom_call_target="tpu_custom_call" | custom-call | flops 500000000 | bytes 3906250 | tf_op jit(solution)/shard_map/encode/pallas_call | solution.py:324
  5.5 1.3 %collective-permute-start.2 = (s16[272,128]{1,0:T(8,128)(2,1)S(1)}, s16[272,128]{1,0:T(8,128)(2,1)S(1)}, u32[]{:S(2)}, u32[]{:S(2)}) collective-permute-start(s16[272,128]{1,0:T(8,128)(2,1)S(1)} %get-tuple-element.22.refs_0_), channel_id=1, source_target_pairs={{0,16},{16,0},{1,17},{17,1},{2,18},{18,2},{3,19},{19,3},{4,20},{20... | collective-permute-start | bytes 208904 | tf_op jit(solution)/shard_map/ppermute | solution.py:351
  6.8 0.8 %collective-permute-start.1 = (s16[272,128]{1,0:T(8,128)(2,1)S(1)}, s16[272,128]{1,0:T(8,128)(2,1)S(1)}, u32[]{:S(2)}, u32[]{:S(2)}) collective-permute-start(s16[272,128]{1,0:T(8,128)(2,1)S(1)} %get-tuple-element.23.refs_1_), channel_id=1, source_target_pairs={{0,16},{16,0},{1,17},{17,1},{2,18},{18,2},{3,19},{19,3},{4,20},{20... | collective-permute-start | bytes 208904 | tf_op jit(solution)/shard_map/ppermute | solution.py:351
  7.6 0.0 copy-done
  7.6 1.4 %own.1 = (f32[2048,128]{1,0:T(8,128)S(1)}, f32[2048,128]{1,0:T(8,128)S(1)}) custom-call(bf16[256,256]{1,0:T(8,128)(2,1)S(1)} %get-tuple-element.19.weights_ref, s16[32,2048]{1,0:T(8,128)(2,1)S(1)} %get-tuple-element.15.short_ref, f32[2048,128]{1,0:T(8,128)S(1)} %bitcast.7, bf16[2048,128]{1,0:T(8,128)(2,1)S(1)} %bitcast.9, f32[2048,128]{1,0:T(8,128)S(1)} %copy-done, ...), custom_call_target="tpu_custom_call" | custom-call | flops 500000000 | bytes 3906250 | tf_op jit(solution)/shard_map/own/pallas_call | solution.py:324
  9.0 0.0 collective-permute-done.refs_0_
  9.0 1.0 %positions.1 = (f32[2048,128]{1,0:T(8,128)}, s32[128,2048]{1,0:T(8,128)S(1)}) custom-call(f32[2048,128]{1,0:T(8,128)S(1)} %get-tuple-element.24.new_ref, s16[32,2048]{1,0:T(8,128)(2,1)S(1)} %collective-permute-done.refs_0_), custom_call_target="tpu_custom_call" | custom-call | flops 500000000 | bytes 3906250 | tf_op jit(solution)/shard_map/positions/pallas_call | solution.py:324
  10.0 0.4 %collective-permute-done.2.refs_0_ = s16[272,128]{1,0:T(8,128)(2,1)S(1)} collective-permute-done((s16[272,128]{1,0:T(8,128)(2,1)S(1)}, s16[272,128]{1,0:T(8,128)(2,1)S(1)}, u32[]{:S(2)}, u32[]{:S(2)}) %collective-permute-start.2) | collective-permute-done | bytes 69664 | tf_op jit(solution)/shard_map/ppermute | solution.py:351
  10.4 0.5 %finish.2.refs_2_ = bf16[1024,128]{1,0:T(8,128)(2,1)S(1)} custom-call(bf16[256,256]{1,0:T(8,128)(2,1)S(1)} %get-tuple-element.19.weights_ref, f32[2048,128]{1,0:T(8,128)S(1)} %get-tuple-element.26.back_ref, f32[2048,128]{1,0:T(8,128)S(1)} %copy-done, s16[272,128]{1,0:T(8,128)(2,1)S(1)} %collective-permute-done.2.refs_0_, ...), custom_call_target="tpu_custom_call" | custom-call | flops 500000000 | bytes 3906250 | tf_op jit(solution)/shard_map/finish/pallas_call | solution.py:324
  10.9 0.2 %collective-permute-done.1.refs_0_ = s16[272,128]{1,0:T(8,128)(2,1)S(1)} collective-permute-done((s16[272,128]{1,0:T(8,128)(2,1)S(1)}, s16[272,128]{1,0:T(8,128)(2,1)S(1)}, u32[]{:S(2)}, u32[]{:S(2)}) %collective-permute-start.1) | collective-permute-done | bytes 69664 | tf_op jit(solution)/shard_map/ppermute | solution.py:351
  11.2 1.2 %finish.3 = bf16[2048,128]{1,0:T(8,128)(2,1)} custom-call(bf16[256,256]{1,0:T(8,128)(2,1)S(1)} %get-tuple-element.19.weights_ref, f32[2048,128]{1,0:T(8,128)S(1)} %get-tuple-element.26.back_ref, f32[2048,128]{1,0:T(8,128)S(1)} %copy-done, s16[272,128]{1,0:T(8,128)(2,1)S(1)} %collective-permute-done.1.refs_0_, s32[128,2048]{1,0:T(8,128)S(1)} %get-tuple-element.27.refs_1_, ...), custom_call_target="tpu_custom_call" | custom-call | flops 500000000 | bytes 3906250 | tf_op jit(solution)/shard_map/finish/pallas_call | solution.py:324
  (1 shorter events, 0.0 us)
Async XLA Ops:
  0.6 1.0 %copy-start.3 = (s32[1,2048,32]{1,2,0:T(8,128)S(1)}, s32[1,2048,32]{1,2,0:T(8,128)}, u32[]{:S(2)}) copy-start(s32[1,2048,32]{1,2,0:T(8,128)} %param.7) | copy-start | bytes 786436
  1.6 3.1 %copy-start.1 = (f32[1,2048,128]{2,1,0:T(8,128)S(1)}, f32[1,2048,128]{2,1,0:T(8,128)}, u32[]{:S(2)}) copy-start(f32[1,2048,128]{2,1,0:T(8,128)} %param.4) | copy-start | bytes 3145732
  2.2 2.4 %copy-start.2 = (bf16[1,2048,128]{2,1,0:T(8,128)(2,1)S(1)}, bf16[1,2048,128]{2,1,0:T(8,128)(2,1)}, u32[]{:S(2)}) copy-start(bf16[1,2048,128]{2,1,0:T(8,128)(2,1)} %param.5) | copy-start | bytes 1572868
  2.2 6.8 %collective-permute-start = (s16[32,2048]{1,0:T(8,128)(2,1)S(1)}, s16[32,2048]{1,0:T(8,128)(2,1)S(1)}, u32[]{:S(2)}, u32[]{:S(2)}) collective-permute-start(s16[32,2048]{1,0:T(8,128)(2,1)S(1)} %get-tuple-element.15.short_ref), channel_id=1, source_target_pairs={{0,16},{16,0},{1,17},{17,1},{2,18},{18,2},{3,19},{19,3},{4,20},{20... | collective-permute-start | bytes 393224 | tf_op jit(solution)/shard_map/ppermute | solution.py:351
  4.6 2.9 %copy-start = (f32[2048,128]{1,0:T(8,128)S(1)}, f32[2048,128]{1,0:T(8,128)}, u32[]{:S(2)}) copy-start(f32[2048,128]{1,0:T(8,128)} %p_ref.5) | copy-start | bytes 3145732
  5.5 5.0 %collective-permute-start.2 = (s16[272,128]{1,0:T(8,128)(2,1)S(1)}, s16[272,128]{1,0:T(8,128)(2,1)S(1)}, u32[]{:S(2)}, u32[]{:S(2)}) collective-permute-start(s16[272,128]{1,0:T(8,128)(2,1)S(1)} %get-tuple-element.22.refs_0_), channel_id=1, source_target_pairs={{0,16},{16,0},{1,17},{17,1},{2,18},{18,2},{3,19},{19,3},{4,20},{20... | collective-permute-start | bytes 208904 | tf_op jit(solution)/shard_map/ppermute | solution.py:351
  6.8 4.4 %collective-permute-start.1 = (s16[272,128]{1,0:T(8,128)(2,1)S(1)}, s16[272,128]{1,0:T(8,128)(2,1)S(1)}, u32[]{:S(2)}, u32[]{:S(2)}) collective-permute-start(s16[272,128]{1,0:T(8,128)(2,1)S(1)} %get-tuple-element.23.refs_1_), channel_id=1, source_target_pairs={{0,16},{16,0},{1,17},{17,1},{2,18},{18,2},{3,19},{19,3},{4,20},{20... | collective-permute-start | bytes 208904 | tf_op jit(solution)/shard_map/ppermute | solution.py:351

commit v9 on v8

--- a/solution.py
+++ b/solution.py
@@ -170,8 +170,8 @@
     keep = length // GROUPS
     spare = (length - keep) // SUB
     weights = weights_ref[...]
+    scales = []
     for chunks, msg_ref in zip(parts, msgs):
-        scales = []
         for i, c in enumerate(chunks):
             rows = slice(c * GROUPS * length, (c + 1) * GROUPS * length)
             mom = 0.999 * m_ref[rows] + g_ref[rows].astype(jnp.float32)
@@ -194,20 +194,21 @@
             msg_ref[i * length : (i + 1) * length] = (
                 jnp.concatenate(coded, axis=0).astype(jnp.int32).astype(jnp.int16)
             )
-        base = len(chunks) * length
-        rows = msg_ref.shape[0] - base
-        if rows > len(scales):
-            scales.append(jnp.zeros((rows - len(scales), length), jnp.float32))
-        msg_ref[base:] = jnp.concatenate(scales, axis=0).astype(jnp.int32).astype(jnp.int16)
-
-
-def spread(msg_ref, ranks, i, base):
+    base = len(parts[0]) * length
+    rows = msgs[0].shape[0] - base
+    if rows > len(scales):
+        scales.append(jnp.zeros((rows - len(scales), length), jnp.float32))
+    msgs[0][base:] = jnp.concatenate(scales, axis=0).astype(jnp.int32).astype(jnp.int16)
+
+
+def spread(msg_ref, first_ref, ranks, i, scales):
     length = msg_ref.shape[1]
     keep = length // GROUPS
     spare = (length - keep) // SUB
     rows = msg_ref[i * length : (i + 1) * length].astype(jnp.int32).astype(jnp.float32)
-    tail = msg_ref[base:].astype(jnp.int32).astype(jnp.float32)
-    unit = jnp.exp2(tail[i * GROUPS : (i + 1) * GROUPS]) * (1.0 / STEPS)
+    base = scales // 16 * 16
+    tail = first_ref[base : base + 16].astype(jnp.int32).astype(jnp.float32)
+    unit = jnp.exp2(tail[scales - base : scales - base + GROUPS]) * (1.0 / STEPS)
     out = []
     for g, rank in enumerate(ranks):
         values = rows[g * keep : (g + 1) * keep] * unit[g : g + 1]
@@ -245,7 +246,8 @@
                 for b in range(c * GROUPS, (c + 1) * GROUPS)
             ]
             rows = slice(c * size, (c + 1) * size)
-            back = transform(spread(msg_ref, ranks, i, len(chunks) * length), weights)
+            scales = len(parts[0]) * length + c * GROUPS
+            back = transform(spread(msg_ref, msgs[0], ranks, i, scales), weights)
             back_ref[rows] = back
             new_ref[rows] = 0.999 * m_ref[rows] + g_ref[rows].astype(jnp.float32) - back
 
@@ -265,6 +267,7 @@
 
 def finish_kernel(parts, islands, weights_ref, back_ref, p_ref, *refs):
     msgs, refs = refs[: islands - 1], refs[islands - 1 :]
+    firsts, refs = refs[: islands - 1], refs[islands - 1 :]
     places, refs = refs[: islands - 1], refs[islands - 1 :]
     chunks = parts[-1]
     length = p_ref.shape[1]
@@ -284,12 +287,12 @@
     for i, c in enumerate(chunks):
         rows = slice(c * size, (c + 1) * size)
         terms = [back_ref[rows]]
-        for msg_ref, ranks_ref in zip(msgs, places):
+        for msg_ref, first_ref, ranks_ref in zip(msgs, firsts, places):
             ranks = [
                 ranks_ref[:, b * length : (b + 1) * length]
                 for b in range(c * GROUPS, (c + 1) * GROUPS)
             ]
-            kept = spread(msg_ref, ranks, i, len(chunks) * length)
+            kept = spread(msg_ref, first_ref, ranks, i, len(parts[0]) * length + c * GROUPS)
             terms.append(transform(kept, weights))
         if islands == 2:
             total = terms[0] + terms[1]
@@ -339,7 +342,7 @@
     _, count, length = momentum.shape
     numbers = indices[0].T
     chunks = count // (GROUPS * length)
-    parts = [part for part in (range(chunks - 2), range(chunks - 2, chunks)) if len(part)]
+    parts = [part for part in (range(chunks - 1), range(chunks - 1, chunks)) if len(part)]
     rings = [
         [(i, (i + away) % islands) for i in range(islands)] for away in range(1, islands)
     ]
@@ -361,7 +364,7 @@
         order_kernel, prepared, short, *early,
         name="order", flops=10**4, onto={1: 0, 2: 1, 3: 2},
     )
-    tails = [-(-(len(part) * GROUPS) // 16) * 16 for part in parts]
+    tails = [-(-(chunks * GROUPS) // 16) * 16] + [0] * (len(parts) - 1)
     msgs = on_chip(
         functools.partial(encode_kernel, parts),
         [array(len(part) * length + tail, jnp.int16) for part, tail in zip(parts, tails)],
@@ -387,7 +390,7 @@
         (done,) = on_chip(
             functools.partial(finish_kernel, parts[: i + 1], islands),
             [array(count, jnp.bfloat16) if last else mine],
-            inverse, back, params, *others, *places, *(fresh if last else []),
+            inverse, back, params, *others, *other_msgs[0], *places, *(fresh if last else []),
             name="finish", held=mine, copies=(i + len(part)) * last,
         )
         fresh.append(done)

time: 12.6 us -> 12.6 us (level)
  transfers between devices with their start and end apart: 3 -> 3, of which waited for: 2 -> 1; matrix products, arithmetic and copies ran while one was open for 0% -> 0% of each run, Pallas kernels for 30% -> 31%
where the time goes in v9:
time: 12.6 us; the launch traced here: 12.5 us
  Pallas kernels  5.6 us (44%)
  starting transfers between devices  4.51 us (36%)
  local copies, waits for them, and re-layouts  0.96 us (8%)
  waiting for transfers between devices  0.7 us (6%)
  between operations  0.7 us (6%)
    pallas_call x7, Pallas kernels, on_chip(): pl.pallas_call(kernel, in_specs=[vmem] * len(args), out_specs=out_specs,...  5.6 us
    ppermute x3, starting transfers between devices, to_others(): return [lax.ppermute(x, 'island', ring) for ring in rings]  4.51 us
    unnamed x8, local copies, waits for them, and re-layouts  0.96 us
    ppermute x3, waiting for transfers between devices, to_others(): return [lax.ppermute(x, 'island', ring) for ring in rings]  0.7 us
  transfers between devices with their start and end apart: 3, of which 1 were waited for; matrix products, arithmetic and copies ran while one was open for 0% of the time, Pallas kernels for 31%

profile of v9, /device:TPU:0, one launch (start us, length us, event | category | flops | bytes accessed | tf_op | source)
XLA Modules:
  0.0 12.5 jit_solution(17776988128932408694)
XLA Ops:
  0.6 0.0 copy-start.3
  0.6 0.9 %copy-done.3 = s32[1,2048,32]{1,2,0:T(8,128)S(1)} copy-done((s32[1,2048,32]{1,2,0:T(8,128)S(1)}, s32[1,2048,32]{1,2,0:T(8,128)}, u32[]{:S(2)}) %copy-start.3) | copy-done | bytes 262168
  1.6 0.0 copy-start.1
  1.6 0.6 %shorten.1 = (s16[32,2048]{1,0:T(8,128)(2,1)S(1)}, s32[512,128]{1,0:T(8,128)S(1)}, bf16[256,256]{1,0:T(8,128)(2,1)S(1)}, bf16[256,256]{1,0:T(8,128)(2,1)S(1)}) custom-call(s32[32,2048]{1,0:T(8,128)S(1)} %bitcast.10), custom_call_target="tpu_custom_call" | custom-call | flops 5000000000 | bytes 39062500 | tf_op jit(solution)/shard_map/shorten/pallas_call | solution.py:327
  2.2 0.0 copy-start.2
  2.2 2.4 %collective-permute-start = (s16[32,2048]{1,0:T(8,128)(2,1)S(1)}, s16[32,2048]{1,0:T(8,128)(2,1)S(1)}, u32[]{:S(2)}, u32[]{:S(2)}) collective-permute-start(s16[32,2048]{1,0:T(8,128)(2,1)S(1)} %get-tuple-element.15.short_ref), channel_id=1, source_target_pairs={{0,16},{16,0},{1,17},{17,1},{2,18},{18,2},{3,19},{19,3},{4,20},{20... | collective-permute-start | bytes 393224 | tf_op jit(solution)/shard_map/ppermute | solution.py:354
  4.6 0.0 copy-start
  4.6 0.0 copy-done.1
  4.7 0.0 copy-done.2
  4.7 0.8 %encode.1 = (s16[400,128]{1,0:T(8,128)(2,1)S(1)}, s16[128,128]{1,0:T(8,128)(2,1)S(1)}) custom-call(bf16[256,256]{1,0:T(8,128)(2,1)S(1)} %get-tuple-element.20.weights_ref, s32[512,128]{1,0:T(8,128)S(1)} %get-tuple-element.21.picks_ref, f32[2048,128]{1,0:T(8,128)S(1)} %bitcast.6, bf16[2048,128]{1,0:T(8,128)(2,1)S(1)} %bitcast.8), custom_call_target="tpu_custom_call" | custom-call | flops 500000000 | bytes 3906250 | tf_op jit(solution)/shard_map/encode/pallas_call | solution.py:327
  5.5 1.3 %collective-permute-start.2 = (s16[400,128]{1,0:T(8,128)(2,1)S(1)}, s16[400,128]{1,0:T(8,128)(2,1)S(1)}, u32[]{:S(2)}, u32[]{:S(2)}) collective-permute-start(s16[400,128]{1,0:T(8,128)(2,1)S(1)} %get-tuple-element.22.refs_0_), channel_id=1, source_target_pairs={{0,16},{16,0},{1,17},{17,1},{2,18},{18,2},{3,19},{19,3},{4,20},{20... | collective-permute-start | bytes 307208 | tf_op jit(solution)/shard_map/ppermute | solution.py:354
  6.8 0.8 %collective-permute-start.1 = (s16[128,128]{1,0:T(8,128)(2,1)S(1)}, s16[128,128]{1,0:T(8,128)(2,1)S(1)}, u32[]{:S(2)}, u32[]{:S(2)}) collective-permute-start(s16[128,128]{1,0:T(8,128)(2,1)S(1)} %get-tuple-element.23.refs_1_), channel_id=1, source_target_pairs={{0,16},{16,0},{1,17},{17,1},{2,18},{18,2},{3,19},{19,3},{4,20},{20... | collective-permute-start | bytes 98312 | tf_op jit(solution)/shard_map/ppermute | solution.py:354
  7.6 0.0 copy-done
  7.6 1.4 %own.1 = (f32[2048,128]{1,0:T(8,128)S(1)}, f32[2048,128]{1,0:T(8,128)S(1)}) custom-call(bf16[256,256]{1,0:T(8,128)(2,1)S(1)} %get-tuple-element.19.weights_ref, s16[32,2048]{1,0:T(8,128)(2,1)S(1)} %get-tuple-element.15.short_ref, f32[2048,128]{1,0:T(8,128)S(1)} %bitcast.7, bf16[2048,128]{1,0:T(8,128)(2,1)S(1)} %bitcast.9, f32[2048,128]{1,0:T(8,128)S(1)} %copy-done, ...), custom_call_target="tpu_custom_call" | custom-call | flops 500000000 | bytes 3906250 | tf_op jit(solution)/shard_map/own/pallas_call | solution.py:327
  9.0 0.0 collective-permute-done.refs_0_
  9.0 1.0 %positions.1 = (f32[2048,128]{1,0:T(8,128)}, s32[128,2048]{1,0:T(8,128)S(1)}) custom-call(f32[2048,128]{1,0:T(8,128)S(1)} %get-tuple-element.24.new_ref, s16[32,2048]{1,0:T(8,128)(2,1)S(1)} %collective-permute-done.refs_0_), custom_call_target="tpu_custom_call" | custom-call | flops 500000000 | bytes 3906250 | tf_op jit(solution)/shard_map/positions/pallas_call | solution.py:327
  10.0 0.7 %collective-permute-done.2.refs_0_.refs_1_ = s16[400,128]{1,0:T(8,128)(2,1)S(1)} collective-permute-done((s16[400,128]{1,0:T(8,128)(2,1)S(1)}, s16[400,128]{1,0:T(8,128)(2,1)S(1)}, u32[]{:S(2)}, u32[]{:S(2)}) %collective-permute-start.2) | collective-permute-done | bytes 102432 | tf_op jit(solution)/shard_map/ppermute | solution.py:354
  10.7 0.7 %finish.2.refs_3_ = bf16[1536,128]{1,0:T(8,128)(2,1)S(1)} custom-call(bf16[256,256]{1,0:T(8,128)(2,1)S(1)} %get-tuple-element.19.weights_ref, f32[2048,128]{1,0:T(8,128)S(1)} %get-tuple-element.26.back_ref, f32[2048,128]{1,0:T(8,128)S(1)} %copy-done, s16[400,128]{1,0:T(8,128)(2,1)S(1)} %collective-permute-done.2.refs_0_.refs_1_, ...), custom_call_target="tpu_custom_call" | custom-call | flops 500000000 | bytes 3906250 | tf_op jit(solution)/shard_map/finish/pallas_call | solution.py:327
  11.4 0.0 collective-permute-done.1.refs_0_
  11.4 1.0 %finish.3 = bf16[2048,128]{1,0:T(8,128)(2,1)} custom-call(bf16[256,256]{1,0:T(8,128)(2,1)S(1)} %get-tuple-element.19.weights_ref, f32[2048,128]{1,0:T(8,128)S(1)} %get-tuple-element.26.back_ref, f32[2048,128]{1,0:T(8,128)S(1)} %copy-done, s16[128,128]{1,0:T(8,128)(2,1)S(1)} %collective-permute-done.1.refs_0_, ...), custom_call_target="tpu_custom_call" | custom-call | flops 500000000 | bytes 3906250 | tf_op jit(solution)/shard_map/finish/pallas_call | solution.py:327
  (1 shorter events, 0.0 us)
Async XLA Ops:
  0.6 1.0 %copy-start.3 = (s32[1,2048,32]{1,2,0:T(8,128)S(1)}, s32[1,2048,32]{1,2,0:T(8,128)}, u32[]{:S(2)}) copy-start(s32[1,2048,32]{1,2,0:T(8,128)} %param.7) | copy-start | bytes 786436
  1.6 3.1 %copy-start.1 = (f32[1,2048,128]{2,1,0:T(8,128)S(1)}, f32[1,2048,128]{2,1,0:T(8,128)}, u32[]{:S(2)}) copy-start(f32[1,2048,128]{2,1,0:T(8,128)} %param.4) | copy-start | bytes 3145732
  2.2 2.4 %copy-start.2 = (bf16[1,2048,128]{2,1,0:T(8,128)(2,1)S(1)}, bf16[1,2048,128]{2,1,0:T(8,128)(2,1)}, u32[]{:S(2)}) copy-start(bf16[1,2048,128]{2,1,0:T(8,128)(2,1)} %param.5) | copy-start | bytes 1572868
  2.2 6.8 %collective-permute-start = (s16[32,2048]{1,0:T(8,128)(2,1)S(1)}, s16[32,2048]{1,0:T(8,128)(2,1)S(1)}, u32[]{:S(2)}, u32[]{:S(2)}) collective-permute-start(s16[32,2048]{1,0:T(8,128)(2,1)S(1)} %get-tuple-element.15.short_ref), channel_id=1, source_target_pairs={{0,16},{16,0},{1,17},{17,1},{2,18},{18,2},{3,19},{19,3},{4,20},{20... | collective-permute-start | bytes 393224 | tf_op jit(solution)/shard_map/ppermute | solution.py:354
  4.6 2.9 %copy-start = (f32[2048,128]{1,0:T(8,128)S(1)}, f32[2048,128]{1,0:T(8,128)}, u32[]{:S(2)}) copy-start(f32[2048,128]{1,0:T(8,128)} %p_ref.5) | copy-start | bytes 3145732
  5.5 5.2 %collective-permute-start.2 = (s16[400,128]{1,0:T(8,128)(2,1)S(1)}, s16[400,128]{1,0:T(8,128)(2,1)S(1)}, u32[]{:S(2)}, u32[]{:S(2)}) collective-permute-start(s16[400,128]{1,0:T(8,128)(2,1)S(1)} %get-tuple-element.22.refs_0_), channel_id=1, source_target_pairs={{0,16},{16,0},{1,17},{17,1},{2,18},{18,2},{3,19},{19,3},{4,20},{20... | collective-permute-start | bytes 307208 | tf_op jit(solution)/shard_map/ppermute | solution.py:354
  6.8 4.6 %collective-permute-start.1 = (s16[128,128]{1,0:T(8,128)(2,1)S(1)}, s16[128,128]{1,0:T(8,128)(2,1)S(1)}, u32[]{:S(2)}, u32[]{:S(2)}) collective-permute-start(s16[128,128]{1,0:T(8,128)(2,1)S(1)} %get-tuple-element.23.refs_1_), channel_id=1, source_target_pairs={{0,16},{16,0},{1,17},{17,1},{2,18},{18,2},{3,19},{19,3},{4,20},{20... | collective-permute-start | bytes 98312 | tf_op jit(solution)/shard_map/ppermute | solution.py:354

commit v10 on v8

--- a/solution.py
+++ b/solution.py
@@ -36,18 +36,14 @@
 
 def weights_of(table):
     hi, lo = two_parts(table)
-    return jnp.concatenate(
-        [jnp.concatenate([hi, lo], axis=1), jnp.concatenate([hi, jnp.zeros_like(hi)], axis=1)],
-        axis=0,
-    )
+    return jnp.concatenate([hi, hi, lo], axis=0)
 
 
 def transform(x, weights):
-    both = jnp.dot(
-        jnp.concatenate(two_parts(x), axis=1), weights, preferred_element_type=jnp.float32
-    )
-    length = x.shape[1]
-    return both[:, :length] + both[:, length:]
+    hi, lo = two_parts(x)
+    return jnp.dot(
+        jnp.concatenate([hi, lo, hi], axis=1), weights, preferred_element_type=jnp.float32
+    )
 
 
 def rows_of(x, index):
@@ -350,7 +346,7 @@
     def to_others(x):
         return [lax.ppermute(x, "island", ring) for ring in rings]
 
-    weights = array(2 * length, jnp.bfloat16, 2 * length)
+    weights = array(3 * length, jnp.bfloat16)
     prepared = [array(chunks * length, jnp.int32), weights, weights]
     short, *early = on_chip(
         shorten_kernel, [array(numbers.shape[0], jnp.int16, count)] + prepared, numbers,

time: 12.6 us -> 12.6 us (level)
  transfers between devices with their start and end apart: 3 -> 3, of which waited for: 2 -> 2; matrix products, arithmetic and copies ran while one was open for 0% -> 0% of each run, Pallas kernels for 30% -> 31%
where the time goes in v10:
time: 12.6 us; the launch traced here: 12.4 us
  Pallas kernels  5.67 us (45%)
  starting transfers between devices  4.51 us (36%)
  local copies, waits for them, and re-layouts  0.96 us (8%)
  between operations  0.69 us (5%)
  waiting for transfers between devices  0.57 us (5%)
    pallas_call x7, Pallas kernels, on_chip(): pl.pallas_call(kernel, in_specs=[vmem] * len(args), out_specs=out_specs,...  5.67 us
    ppermute x3, starting transfers between devices, to_others(): return [lax.ppermute(x, 'island', ring) for ring in rings]  4.51 us
    unnamed x8, local copies, waits for them, and re-layouts  0.96 us
    ppermute x3, waiting for transfers between devices, to_others(): return [lax.ppermute(x, 'island', ring) for ring in rings]  0.57 us
  transfers between devices with their start and end apart: 3, of which 2 were waited for; matrix products, arithmetic and copies ran while one was open for 0% of the time, Pallas kernels for 31%

profile of v10, /device:TPU:0, one launch (start us, length us, event | category | flops | bytes accessed | tf_op | source)
XLA Modules:
  0.0 12.4 jit_solution(13125641555384850255)
XLA Ops:
  0.6 0.0 copy-start.3
  0.6 0.9 %copy-done.3 = s32[1,2048,32]{1,2,0:T(8,128)S(1)} copy-done((s32[1,2048,32]{1,2,0:T(8,128)S(1)}, s32[1,2048,32]{1,2,0:T(8,128)}, u32[]{:S(2)}) %copy-start.3) | copy-done | bytes 262168
  1.6 0.0 copy-start.1
  1.6 0.6 %shorten.1 = (s16[32,2048]{1,0:T(8,128)(2,1)S(1)}, s32[512,128]{1,0:T(8,128)S(1)}, bf16[384,128]{1,0:T(8,128)(2,1)S(1)}, bf16[384,128]{1,0:T(8,128)(2,1)S(1)}) custom-call(s32[32,2048]{1,0:T(8,128)S(1)} %bitcast.10), custom_call_target="tpu_custom_call" | custom-call | flops 5000000000 | bytes 39062500 | tf_op jit(solution)/shard_map/shorten/pallas_call | solution.py:320
  2.2 0.0 copy-start.2
  2.2 2.4 %collective-permute-start = (s16[32,2048]{1,0:T(8,128)(2,1)S(1)}, s16[32,2048]{1,0:T(8,128)(2,1)S(1)}, u32[]{:S(2)}, u32[]{:S(2)}) collective-permute-start(s16[32,2048]{1,0:T(8,128)(2,1)S(1)} %get-tuple-element.15.short_ref), channel_id=1, source_target_pairs={{0,16},{16,0},{1,17},{17,1},{2,18},{18,2},{3,19},{19,3},{4,20},{20... | collective-permute-start | bytes 393224 | tf_op jit(solution)/shard_map/ppermute | solution.py:347
  4.6 0.0 copy-start
  4.6 0.0 copy-done.1
  4.7 0.0 copy-done.2
  4.7 0.8 %encode.1 = (s16[272,128]{1,0:T(8,128)(2,1)S(1)}, s16[272,128]{1,0:T(8,128)(2,1)S(1)}) custom-call(bf16[384,128]{1,0:T(8,128)(2,1)S(1)} %get-tuple-element.20.weights_ref, s32[512,128]{1,0:T(8,128)S(1)} %get-tuple-element.21.picks_ref, f32[2048,128]{1,0:T(8,128)S(1)} %bitcast.6, bf16[2048,128]{1,0:T(8,128)(2,1)S(1)} %bitcast.8), custom_call_target="tpu_custom_call" | custom-call | flops 500000000 | bytes 3906250 | tf_op jit(solution)/shard_map/encode/pallas_call | solution.py:320
  5.5 1.3 %collective-permute-start.2 = (s16[272,128]{1,0:T(8,128)(2,1)S(1)}, s16[272,128]{1,0:T(8,128)(2,1)S(1)}, u32[]{:S(2)}, u32[]{:S(2)}) collective-permute-start(s16[272,128]{1,0:T(8,128)(2,1)S(1)} %get-tuple-element.22.refs_0_), channel_id=1, source_target_pairs={{0,16},{16,0},{1,17},{17,1},{2,18},{18,2},{3,19},{19,3},{4,20},{20... | collective-permute-start | bytes 208904 | tf_op jit(solution)/shard_map/ppermute | solution.py:347
  6.8 0.8 %collective-permute-start.1 = (s16[272,128]{1,0:T(8,128)(2,1)S(1)}, s16[272,128]{1,0:T(8,128)(2,1)S(1)}, u32[]{:S(2)}, u32[]{:S(2)}) collective-permute-start(s16[272,128]{1,0:T(8,128)(2,1)S(1)} %get-tuple-element.23.refs_1_), channel_id=1, source_target_pairs={{0,16},{16,0},{1,17},{17,1},{2,18},{18,2},{3,19},{19,3},{4,20},{20... | collective-permute-start | bytes 208904 | tf_op jit(solution)/shard_map/ppermute | solution.py:347
  7.6 0.0 copy-done
  7.6 1.5 %own.1 = (f32[2048,128]{1,0:T(8,128)S(1)}, f32[2048,128]{1,0:T(8,128)S(1)}) custom-call(bf16[384,128]{1,0:T(8,128)(2,1)S(1)} %get-tuple-element.19.weights_ref, s16[32,2048]{1,0:T(8,128)(2,1)S(1)} %get-tuple-element.15.short_ref, f32[2048,128]{1,0:T(8,128)S(1)} %bitcast.7, bf16[2048,128]{1,0:T(8,128)(2,1)S(1)} %bitcast.9, f32[2048,128]{1,0:T(8,128)S(1)} %copy-done, ...), custom_call_target="tpu_custom_call" | custom-call | flops 500000000 | bytes 3906250 | tf_op jit(solution)/shard_map/own/pallas_call | solution.py:320
  9.0 0.0 collective-permute-done.refs_0_
  9.1 1.0 %positions.1 = (f32[2048,128]{1,0:T(8,128)}, s32[128,2048]{1,0:T(8,128)S(1)}) custom-call(f32[2048,128]{1,0:T(8,128)S(1)} %get-tuple-element.24.new_ref, s16[32,2048]{1,0:T(8,128)(2,1)S(1)} %collective-permute-done.refs_0_), custom_call_target="tpu_custom_call" | custom-call | flops 500000000 | bytes 3906250 | tf_op jit(solution)/shard_map/positions/pallas_call | solution.py:320
  10.0 0.4 %collective-permute-done.2.refs_0_ = s16[272,128]{1,0:T(8,128)(2,1)S(1)} collective-permute-done((s16[272,128]{1,0:T(8,128)(2,1)S(1)}, s16[272,128]{1,0:T(8,128)(2,1)S(1)}, u32[]{:S(2)}, u32[]{:S(2)}) %collective-permute-start.2) | collective-permute-done | bytes 69664 | tf_op jit(solution)/shard_map/ppermute | solution.py:347
  10.4 0.5 %finish.2.refs_2_ = bf16[1024,128]{1,0:T(8,128)(2,1)S(1)} custom-call(bf16[384,128]{1,0:T(8,128)(2,1)S(1)} %get-tuple-element.19.weights_ref, f32[2048,128]{1,0:T(8,128)S(1)} %get-tuple-element.26.back_ref, f32[2048,128]{1,0:T(8,128)S(1)} %copy-done, s16[272,128]{1,0:T(8,128)(2,1)S(1)} %collective-permute-done.2.refs_0_, ...), custom_call_target="tpu_custom_call" | custom-call | flops 500000000 | bytes 3906250 | tf_op jit(solution)/shard_map/finish/pallas_call | solution.py:320
  11.0 0.2 %collective-permute-done.1.refs_0_ = s16[272,128]{1,0:T(8,128)(2,1)S(1)} collective-permute-done((s16[272,128]{1,0:T(8,128)(2,1)S(1)}, s16[272,128]{1,0:T(8,128)(2,1)S(1)}, u32[]{:S(2)}, u32[]{:S(2)}) %collective-permute-start.1) | collective-permute-done | bytes 69664 | tf_op jit(solution)/shard_map/ppermute | solution.py:347
  11.2 1.2 %finish.3 = bf16[2048,128]{1,0:T(8,128)(2,1)} custom-call(bf16[384,128]{1,0:T(8,128)(2,1)S(1)} %get-tuple-element.19.weights_ref, f32[2048,128]{1,0:T(8,128)S(1)} %get-tuple-element.26.back_ref, f32[2048,128]{1,0:T(8,128)S(1)} %copy-done, s16[272,128]{1,0:T(8,128)(2,1)S(1)} %collective-permute-done.1.refs_0_, s32[128,2048]{1,0:T(8,128)S(1)} %get-tuple-element.27.refs_1_, ...), custom_call_target="tpu_custom_call" | custom-call | flops 500000000 | bytes 3906250 | tf_op jit(solution)/shard_map/finish/pallas_call | solution.py:320
  (1 shorter events, 0.0 us)
Async XLA Ops:
  0.6 1.0 %copy-start.3 = (s32[1,2048,32]{1,2,0:T(8,128)S(1)}, s32[1,2048,32]{1,2,0:T(8,128)}, u32[]{:S(2)}) copy-start(s32[1,2048,32]{1,2,0:T(8,128)} %param.7) | copy-start | bytes 786436
  1.6 3.1 %copy-start.1 = (f32[1,2048,128]{2,1,0:T(8,128)S(1)}, f32[1,2048,128]{2,1,0:T(8,128)}, u32[]{:S(2)}) copy-start(f32[1,2048,128]{2,1,0:T(8,128)} %param.4) | copy-start | bytes 3145732
  2.2 2.4 %copy-start.2 = (bf16[1,2048,128]{2,1,0:T(8,128)(2,1)S(1)}, bf16[1,2048,128]{2,1,0:T(8,128)(2,1)}, u32[]{:S(2)}) copy-start(bf16[1,2048,128]{2,1,0:T(8,128)(2,1)} %param.5) | copy-start | bytes 1572868
  2.2 6.8 %collective-permute-start = (s16[32,2048]{1,0:T(8,128)(2,1)S(1)}, s16[32,2048]{1,0:T(8,128)(2,1)S(1)}, u32[]{:S(2)}, u32[]{:S(2)}) collective-permute-start(s16[32,2048]{1,0:T(8,128)(2,1)S(1)} %get-tuple-element.15.short_ref), channel_id=1, source_target_pairs={{0,16},{16,0},{1,17},{17,1},{2,18},{18,2},{3,19},{19,3},{4,20},{20... | collective-permute-start | bytes 393224 | tf_op jit(solution)/shard_map/ppermute | solution.py:347
  4.6 2.9 %copy-start = (f32[2048,128]{1,0:T(8,128)S(1)}, f32[2048,128]{1,0:T(8,128)}, u32[]{:S(2)}) copy-start(f32[2048,128]{1,0:T(8,128)} %p_ref.5) | copy-start | bytes 3145732
  5.5 5.0 %collective-permute-start.2 = (s16[272,128]{1,0:T(8,128)(2,1)S(1)}, s16[272,128]{1,0:T(8,128)(2,1)S(1)}, u32[]{:S(2)}, u32[]{:S(2)}) collective-permute-start(s16[272,128]{1,0:T(8,128)(2,1)S(1)} %get-tuple-element.22.refs_0_), channel_id=1, source_target_pairs={{0,16},{16,0},{1,17},{17,1},{2,18},{18,2},{3,19},{19,3},{4,20},{20... | collective-permute-start | bytes 208904 | tf_op jit(solution)/shard_map/ppermute | solution.py:347
  6.8 4.4 %collective-permute-start.1 = (s16[272,128]{1,0:T(8,128)(2,1)S(1)}, s16[272,128]{1,0:T(8,128)(2,1)S(1)}, u32[]{:S(2)}, u32[]{:S(2)}) collective-permute-start(s16[272,128]{1,0:T(8,128)(2,1)S(1)} %get-tuple-element.23.refs_1_), channel_id=1, source_target_pairs={{0,16},{16,0},{1,17},{17,1},{2,18},{18,2},{3,19},{19,3},{4,20},{20... | collective-permute-start | bytes 208904 | tf_op jit(solution)/shard_map/ppermute | solution.py:347
